TPU v7x, 32 devices: a whole 2x2x4 slice. The times are simulated.
32 devices in a mesh: seq: 8 (over y, x, core), batch: 4 (over z).
Axes of the slice: x: 2, y: 2, z: 4, core: 2. Of those that a mesh axis runs over, the one named last changes fastest.
Arguments:
- frames_in: bfloat16 [4, 3072, 1024], P('batch', 'seq'), may hold values from -6 to 6
- skip_in: bfloat16 [4, 3072, 1024], P('batch', 'seq'), may hold values from -6 to 6
- time_table: bfloat16 [32, 1024], P(None, ('seq', 'batch')), may hold values from -6 to 6
- timestep: int32 [4, 3], P('batch'), may hold values from 0 to 31
- lengths: int32 [4, 3], P('batch'), may hold values from 1 to 2690, as said below
- span_start: int32 [4, 3], P('batch'), may hold values from 0 to 807, as said below
- span_len: int32 [4, 3], P('batch'), may hold values from 1 to 1883, as said below
- skip_proj: bfloat16 [2048, 1024], P(('seq', 'batch')), may hold values from -0.125 to 0.125
- mod_proj: bfloat16 [1024, 4096], P(('seq', 'batch')), may hold values from -0.1875 to 0.1875
- mod_bias: bfloat16 [4096], P(('seq', 'batch')), may hold values from -1.796875 to 1.796875
- qkv_proj: bfloat16 [1024, 3072], P(('seq', 'batch')), may hold values from -0.1875 to 0.1875
- out_proj: bfloat16 [1024, 1024], P(('seq', 'batch')), may hold values from -0.75 to 0.75
- up_proj: bfloat16 [1024, 4096], P(('seq', 'batch')), may hold values from -0.1875 to 0.1875
- up_bias: bfloat16 [4096], P(('seq', 'batch')), may hold values from -3 to 3
- down_proj: bfloat16 [4096, 1024], P(('seq', 'batch')), may hold values from -0.09375 to 0.09375
- cotangent: bfloat16 [4, 3072, 1024], P('batch', 'seq'), may hold values from -6 to 6
Outputs:
- block_out: bfloat16 [4, 3072, 1024], P('batch', 'seq')
- grad_frames: bfloat16 [4, 3072, 1024], P('batch', 'seq')
- grad_skip: bfloat16 [4, 3072, 1024], P('batch', 'seq')
- grad_time: float32 [32, 1024], P(None, ('seq', 'batch'))
- grad_skip_proj: float32 [2048, 1024], P(('seq', 'batch'))
- grad_mod_proj: float32 [1024, 4096], P(('seq', 'batch'))
- grad_mod_bias: float32 [4096], P(('seq', 'batch'))
- grad_qkv_proj: float32 [1024, 3072], P(('seq', 'batch'))
- grad_out_proj: float32 [1024, 1024], P(('seq', 'batch'))
- grad_up_proj: float32 [1024, 4096], P(('seq', 'batch'))
- grad_up_bias: float32 [4096], P(('seq', 'batch'))
- grad_down_proj: float32 [4096, 1024], P(('seq', 'batch'))
Inputs may be any that keep to these rules, and one draw needn't show every extreme that they name: In each group the 3 lengths sum to 3072; the longest utterance starts before frame 384 of its group and ends after frame 3072 - 384. span_start + span_len is at most the utterance's length. `span_len`: at least 70 percent of the utterance's length, rounded down, and at least 1.
All inputs are finite; a program needn't handle non-finite values.
Results may differ from a plain program's by a relative error of at most 0.018.
The roundings to bfloat16 on the way count: a program that leaves them out, or rounds other values in their place, can miss the bound.
Values may be sent and summed in bfloat16 or wider, within the bound.
No kernel may reach another device: no remote copies, remote signals or barrier semaphores. Data moves between devices by JAX's collectives and lax.ppermute only.
A program may use at most 320 MiB of HBM per device.

v0:
```python
import math

import jax
import jax.numpy as jnp
from jax import lax
from jax.sharding import PartitionSpec as P

HEADS = 16


highest = lax.Precision.HIGHEST
norm_eps = 1e-06


def frame_plan(utt_lengths, span_begins, span_sizes, frame_ids):
    utt_ends = jnp.cumsum(utt_lengths)
    starts = utt_ends - utt_lengths
    member = (frame_ids[:, None] >= starts[None, :]) & (frame_ids[:, None] < utt_ends[None, :])
    member_int = member.astype(jnp.int32)
    slot_ids = jnp.arange(utt_lengths.shape[0], dtype=jnp.int32)
    utterance = jnp.sum(member_int * slot_ids[None, :], axis=1)
    utt_begin = jnp.sum(member_int * starts[None, :], axis=1)
    position = frame_ids - utt_begin
    span_first = jnp.sum(member_int * span_begins[None, :], axis=1)
    span_after = span_first + jnp.sum(member_int * span_sizes[None, :], axis=1)
    in_span = (position >= span_first) & (position < span_after)
    return (member, utterance, position, in_span)


def layer_norm(hidden):
    centred = hidden - jnp.mean(hidden, axis=-1, keepdims=True)
    return centred * lax.rsqrt(jnp.mean(centred * centred, axis=-1, keepdims=True) + norm_eps)


def modulate(hidden, scale_part, shift_part):
    return layer_norm(hidden) * (1.0 + scale_part) + shift_part


def gelu_tanh(values):
    return jax.nn.gelu(values, approximate=True)


def rotary(values, position):
    half_size = values.shape[-1] // 2
    freq_rates = jnp.exp(
        jnp.arange(half_size, dtype=jnp.float32) * (-math.log(10000.0) / half_size)
    )
    angles = position.astype(jnp.float32)[:, None] * freq_rates[None, :]
    cosine = jnp.cos(angles)[:, None, :]
    sine_part = jnp.sin(angles)[:, None, :]
    first_half = values[..., :half_size]
    second_half = values[..., half_size:]
    return jnp.concatenate(
        [
            first_half * cosine - second_half * sine_part,
            second_half * cosine + first_half * sine_part,
        ],
        axis=-1,
    )


def contract_rows(first_op, second_op):
    return jnp.einsum("ti,tj->ij", first_op, second_op, preferred_element_type=jnp.float32)


def times_transpose(first_op, second_op):
    return jnp.einsum("tj,ij->ti", first_op, second_op, preferred_element_type=jnp.float32)


def blocking(rows_total, heads_here, keys_total):
    head_block = 1
    while (
        heads_here % (head_block * 2) == 0 and rows_total * keys_total * head_block * 2 <= 4194304
    ):
        head_block = head_block * 2
    return (rows_total, head_block)


def to_blocks(values, row_block, head_block):
    rows_total, heads_here, head_depth = values.shape
    shaped = values.reshape(
        rows_total // row_block, row_block, heads_here // head_block, head_block, head_depth
    )
    return shaped.transpose(0, 2, 1, 3, 4).reshape(-1, row_block, head_block, head_depth)


def from_blocks(blocks, rows_total, heads_here, row_block, head_block):
    head_depth = blocks.shape[-1]
    shaped = blocks.reshape(
        rows_total // row_block, heads_here // head_block, row_block, head_block, head_depth
    )
    return shaped.transpose(0, 2, 1, 3, 4).reshape(rows_total, heads_here, head_depth)


def key_groups(values, head_block):
    keys_total, heads_here, head_depth = values.shape
    return values.reshape(keys_total, heads_here // head_block, head_block, head_depth).transpose(
        1, 0, 2, 3
    )


def take_block(array_in, block_at):
    return lax.dynamic_index_in_dim(array_in, block_at, 0, keepdims=False)


def block_scores(query_block, key_block, query_utt, key_utt):
    scores = jnp.einsum("rhd,khd->hrk", query_block, key_block, preferred_element_type=jnp.float32)
    same_utt = (query_utt[:, None] == key_utt[None, :])[None]
    return jnp.where(same_utt, scores, -1e30)


def attend(query, key, value, query_utt, key_utt):
    rows_total, heads_here, head_depth = query.shape
    row_block, head_block = blocking(rows_total, heads_here, key.shape[0])
    head_groups = heads_here // head_block
    query_blocks = to_blocks(query, row_block, head_block)
    key_sets = key_groups(key, head_block)
    value_sets = key_groups(value, head_block)
    utt_blocks = query_utt.reshape(-1, row_block)

    def one_block(block_at):
        row_at = block_at // head_groups
        head_at = block_at % head_groups
        scores = block_scores(
            take_block(query_blocks, block_at),
            take_block(key_sets, head_at),
            take_block(utt_blocks, row_at),
            key_utt,
        )
        row_max = jnp.max(scores, axis=-1, keepdims=True)
        weights = jnp.exp(scores - row_max)
        row_sums = jnp.sum(weights, axis=-1, keepdims=True)
        row_probs = (weights / row_sums).astype(jnp.bfloat16)
        attended = jnp.einsum(
            "hrk,khd->rhd",
            row_probs,
            take_block(value_sets, head_at),
            preferred_element_type=jnp.float32,
        )
        return (attended.astype(jnp.bfloat16), (row_max + jnp.log(row_sums))[..., 0])

    outputs, log_sums = lax.map(one_block, jnp.arange(query_blocks.shape[0], dtype=jnp.int32))
    return (from_blocks(outputs, rows_total, heads_here, row_block, head_block), log_sums)


def attend_back(query, key, value, grad_attended, log_sums, query_utt, key_utt):
    rows_total, heads_here, head_depth = query.shape
    keys_total = key.shape[0]
    row_block, head_block = blocking(rows_total, heads_here, keys_total)
    head_groups = heads_here // head_block
    query_blocks = to_blocks(query, row_block, head_block)
    grad_blocks = to_blocks(grad_attended, row_block, head_block)
    key_sets = key_groups(key, head_block)
    value_sets = key_groups(value, head_block)
    utt_blocks = query_utt.reshape(-1, row_block)

    def one_block(running, block_at):
        key_acc, value_acc = running
        row_at = block_at // head_groups
        head_at = block_at % head_groups
        query_block = take_block(query_blocks, block_at)
        grad_block = take_block(grad_blocks, block_at)
        key_block = take_block(key_sets, head_at)
        value_block = take_block(value_sets, head_at)
        scores = block_scores(query_block, key_block, take_block(utt_blocks, row_at), key_utt)
        row_probs = jnp.exp(scores - take_block(log_sums, block_at)[..., None])
        grad_probs = jnp.einsum(
            "rhd,khd->hrk", grad_block, value_block, preferred_element_type=jnp.float32
        )
        grad_scores = (
            row_probs * (grad_probs - jnp.sum(grad_probs * row_probs, axis=-1, keepdims=True))
        ).astype(jnp.bfloat16)
        grad_query = jnp.einsum(
            "hrk,khd->rhd", grad_scores, key_block, preferred_element_type=jnp.float32
        )
        grad_key = jnp.einsum(
            "hrk,rhd->khd", grad_scores, query_block, preferred_element_type=jnp.float32
        )
        grad_value = jnp.einsum(
            "hrk,rhd->khd",
            row_probs.astype(jnp.bfloat16),
            grad_block,
            preferred_element_type=jnp.float32,
        )
        key_acc = key_acc.at[head_at].add(grad_key)
        value_acc = value_acc.at[head_at].add(grad_value)
        return ((key_acc, value_acc), grad_query)

    zero_acc = jnp.zeros((head_groups, keys_total, head_block, head_depth), jnp.float32)
    (key_acc, value_acc), grad_queries = lax.scan(
        one_block, (zero_acc, zero_acc), jnp.arange(query_blocks.shape[0], dtype=jnp.int32)
    )
    grad_query = from_blocks(grad_queries, rows_total, heads_here, row_block, head_block)
    grad_key = key_acc.transpose(1, 0, 2, 3).reshape(keys_total, heads_here, head_depth)
    grad_value = value_acc.transpose(1, 0, 2, 3).reshape(keys_total, heads_here, head_depth)
    return (grad_query, grad_key, grad_value)


def shards(
    frames_in,
    skip_in,
    time_table,
    timestep,
    lengths,
    span_start,
    span_len,
    skip_proj,
    mod_proj,
    mod_bias,
    qkv_proj,
    out_proj,
    up_proj,
    up_bias,
    down_proj,
    cotangent,
):
    gathered = (
        lax.all_gather(skip_proj, ("seq", "batch"), axis=0, tiled=True),
        lax.all_gather(mod_proj, ("seq", "batch"), axis=0, tiled=True),
        lax.all_gather(mod_bias, ("seq", "batch"), axis=0, tiled=True),
        lax.all_gather(qkv_proj, ("seq", "batch"), axis=0, tiled=True),
        lax.all_gather(out_proj, ("seq", "batch"), axis=0, tiled=True),
        lax.all_gather(up_proj, ("seq", "batch"), axis=0, tiled=True),
        lax.all_gather(up_bias, ("seq", "batch"), axis=0, tiled=True),
        lax.all_gather(down_proj, ("seq", "batch"), axis=0, tiled=True),
        lax.all_gather(time_table, ("seq", "batch"), axis=1, tiled=True),
    )
    full_skip, full_mod, full_bmod, full_qkv, full_out, full_up, full_bup, full_down, full_table = (
        gathered
    )
    inputs = frames_in[0]
    skip_rows = skip_in[0]
    cot_rows = cotangent[0]
    rows_here, model_width = inputs.shape
    head_depth = model_width // HEADS
    frames = rows_here * lax.axis_size("seq")
    utt_lengths = lengths[0]
    span_begins = span_start[0]
    span_sizes = span_len[0]
    step_group = timestep[0]
    frame_ids = lax.axis_index("seq") * rows_here + jnp.arange(rows_here, dtype=jnp.int32)
    member, utterance, position, in_span = frame_plan(
        utt_lengths, span_begins, span_sizes, frame_ids
    )
    all_utterance = frame_plan(
        utt_lengths, span_begins, span_sizes, jnp.arange(frames, dtype=jnp.int32)
    )[1]
    member_rows = member.astype(jnp.float32)
    step_pick = (
        step_group[:, None] == jnp.arange(full_table.shape[0], dtype=jnp.int32)[None, :]
    ).astype(jnp.float32)
    time_rows = jnp.dot(step_pick, full_table.astype(jnp.float32), precision=highest)
    silu_value, silu_pull = jax.vjp(jax.nn.silu, time_rows)
    time_vec = silu_value.astype(jnp.bfloat16)
    modulation = jnp.dot(time_vec, full_mod, preferred_element_type=jnp.float32) + full_bmod.astype(
        jnp.float32
    )
    per_frame = jnp.dot(member_rows, modulation, precision=highest)
    scale_one = per_frame[:, :model_width]
    shift_one = per_frame[:, model_width : 2 * model_width]
    scale_two = per_frame[:, 2 * model_width : 3 * model_width]
    shift_two = per_frame[:, 3 * model_width :]
    joined = jnp.concatenate([inputs, skip_rows], axis=1)
    stream_in = jnp.dot(joined, full_skip, preferred_element_type=jnp.float32)
    normed_value, adapt_one = jax.vjp(modulate, stream_in, scale_one, shift_one)
    normed_one = normed_value.astype(jnp.bfloat16)
    projected = jnp.dot(normed_one, full_qkv, preferred_element_type=jnp.float32).reshape(
        rows_here, 3, HEADS, head_depth
    )

    def turn(query_part, key_part):
        return (rotary(query_part, position) * head_depth ** (-0.5), rotary(key_part, position))

    (query_turned, key_turned), turn_pull = jax.vjp(turn, projected[:, 0], projected[:, 1])
    query = query_turned.astype(jnp.bfloat16)
    key = key_turned.astype(jnp.bfloat16)
    value = projected[:, 2].astype(jnp.bfloat16)
    all_keys, all_values = (
        lax.all_gather(key, "seq", axis=0, tiled=True),
        lax.all_gather(value, "seq", axis=0, tiled=True),
    )
    attended, log_sums = attend(query, all_keys, all_values, utterance, all_utterance)
    attended_flat = attended.reshape(rows_here, model_width)
    stream_mid = stream_in + jnp.dot(attended_flat, full_out, preferred_element_type=jnp.float32)
    normed_value_two, adapt_two = jax.vjp(modulate, stream_mid, scale_two, shift_two)
    normed_two = normed_value_two.astype(jnp.bfloat16)
    pre_act = jnp.dot(normed_two, full_up, preferred_element_type=jnp.float32) + full_bup.astype(
        jnp.float32
    )
    act_value, gelu_pull = jax.vjp(gelu_tanh, pre_act)
    activated = act_value.astype(jnp.bfloat16)
    result = (
        stream_mid + jnp.dot(activated, full_down, preferred_element_type=jnp.float32)
    ).astype(jnp.bfloat16)
    grad_result = cot_rows.astype(jnp.float32) * in_span[:, None].astype(jnp.float32)
    grad_branch = grad_result.astype(jnp.bfloat16)
    grad_down = contract_rows(activated, grad_branch)
    grad_pre = gelu_pull(times_transpose(grad_branch, full_down))[0].astype(jnp.bfloat16)
    grad_up = contract_rows(normed_two, grad_pre)
    grad_bup = jnp.sum(grad_pre.astype(jnp.float32), axis=0)
    grad_mid, grad_scale_two, grad_shift_two = adapt_two(times_transpose(grad_pre, full_up))
    grad_mid = grad_mid + grad_result
    grad_attn_out = grad_mid.astype(jnp.bfloat16)
    grad_out_w = contract_rows(attended_flat, grad_attn_out)
    grad_attended = (
        times_transpose(grad_attn_out, full_out)
        .astype(jnp.bfloat16)
        .reshape(rows_here, HEADS, head_depth)
    )
    grad_query, key_terms, value_terms = attend_back(
        query, all_keys, all_values, grad_attended, log_sums, utterance, all_utterance
    )
    grad_key, grad_value = (
        lax.psum_scatter(
            key_terms.astype(jnp.bfloat16), "seq", scatter_dimension=0, tiled=True
        ).astype(jnp.float32),
        lax.psum_scatter(
            value_terms.astype(jnp.bfloat16), "seq", scatter_dimension=0, tiled=True
        ).astype(jnp.float32),
    )
    grad_query_pre, grad_key_pre = turn_pull((grad_query, grad_key))
    grad_projected = (
        jnp.stack([grad_query_pre, grad_key_pre, grad_value], axis=1)
        .reshape(rows_here, 3 * model_width)
        .astype(jnp.bfloat16)
    )
    grad_qkv_w = contract_rows(normed_one, grad_projected)
    grad_in, grad_scale_one, grad_shift_one = adapt_one(times_transpose(grad_projected, full_qkv))
    grad_stream = (grad_in + grad_mid).astype(jnp.bfloat16)
    grad_skip_w = contract_rows(joined, grad_stream)
    grad_joined = times_transpose(grad_stream, full_skip)
    grad_inputs = grad_joined[:, :model_width].astype(jnp.bfloat16)
    grad_skip_rows = grad_joined[:, model_width:].astype(jnp.bfloat16)
    grad_frame_mod = jnp.concatenate(
        [grad_scale_one, grad_shift_one, grad_scale_two, grad_shift_two], axis=1
    )
    grad_modulation = jnp.dot(member_rows.T, grad_frame_mod, precision=highest)
    grad_bmod = jnp.sum(grad_modulation, axis=0)
    grad_mod_w = jnp.dot(time_vec.astype(jnp.float32).T, grad_modulation, precision=highest)
    grad_time_vec = jnp.dot(grad_modulation, full_mod.astype(jnp.float32).T, precision=highest)
    grad_rows = silu_pull(grad_time_vec)[0]
    grad_table = jnp.dot(step_pick.T, grad_rows, precision=highest)
    summed = (
        lax.psum_scatter(grad_skip_w, ("seq", "batch"), scatter_dimension=0, tiled=True),
        lax.psum_scatter(grad_mod_w, ("seq", "batch"), scatter_dimension=0, tiled=True),
        lax.psum_scatter(grad_bmod, ("seq", "batch"), scatter_dimension=0, tiled=True),
        lax.psum_scatter(grad_qkv_w, ("seq", "batch"), scatter_dimension=0, tiled=True),
        lax.psum_scatter(grad_out_w, ("seq", "batch"), scatter_dimension=0, tiled=True),
        lax.psum_scatter(grad_up, ("seq", "batch"), scatter_dimension=0, tiled=True),
        lax.psum_scatter(grad_bup, ("seq", "batch"), scatter_dimension=0, tiled=True),
        lax.psum_scatter(grad_down, ("seq", "batch"), scatter_dimension=0, tiled=True),
        lax.psum_scatter(grad_table, ("seq", "batch"), scatter_dimension=1, tiled=True),
    )
    return (
        result[None],
        grad_inputs[None],
        grad_skip_rows[None],
        summed[8],
        summed[0],
        summed[1],
        summed[2],
        summed[3],
        summed[4],
        summed[5],
        summed[6],
        summed[7],
    )


def solution(mesh):
    return jax.shard_map(
        shards,
        mesh=mesh,
        in_specs=(
            P("batch", "seq", None),
            P("batch", "seq", None),
            P(None, ("seq", "batch")),
            P("batch", None),
            P("batch", None),
            P("batch", None),
            P("batch", None),
            P(("seq", "batch"), None),
            P(("seq", "batch"), None),
            P(("seq", "batch")),
            P(("seq", "batch"), None),
            P(("seq", "batch"), None),
            P(("seq", "batch"), None),
            P(("seq", "batch")),
            P(("seq", "batch"), None),
            P("batch", "seq", None),
        ),
        out_specs=(
            P("batch", "seq", None),
            P("batch", "seq", None),
            P("batch", "seq", None),
            P(None, ("seq", "batch")),
            P(("seq", "batch"), None),
            P(("seq", "batch"), None),
            P(("seq", "batch")),
            P(("seq", "batch"), None),
            P(("seq", "batch"), None),
            P(("seq", "batch"), None),
            P(("seq", "batch")),
            P(("seq", "batch"), None),
        ),
        check_vma=False,
    )
```

profile of v0, /device:TPU:0, one launch (start us, length us, event | category | flops | bytes accessed | tf_op | source)
XLA Modules:
  0.0 2713.7 jit_solution(11447549889381173637)
XLA Ops:
  10.2 69.6 %all-gather.1 = bf16[32,1,128]{2,1,0:T(2,128)(2,1)S(1)} all-gather(bf16[1,1,128]{2,1,0:T(2,128)(2,1)} %bitcast.271), channel_id=1, replica_groups=mesh['seq'=8,'batch'=4] {'seq','batch'}, dimensions={0}, use_global_device_ids=true | all-gather | bytes 8448 | tf_op jit(solution)/shard_map/all_gather | solution.py:220
  80.7 67.6 %all_gather.34 = bf16[32,1024]{0,1:T(8,128)(2,1)S(1)} all-gather(bf16[32,32]{0,1:T(8,128)(2,1)S(1)} %copy.43), channel_id=1, replica_groups=mesh['seq'=8,'batch'=4] {'seq','batch'}, dimensions={1}, use_global_device_ids=true | all-gather | bytes 67584 | tf_op jit(solution)/shard_map/all_gather | solution.py:226
  151.0 4.8 fusion.116
  156.9 4.6 convolution_add_fusion.1
  167.2 59.7 %all-gather.16.cloned.1.call-done = bf16[1024,3072]{1,0:T(8,128)(2,1)} async-done(((bf16[32,3072]{1,0:T(8,128)(2,1)}), bf16[1024,3072]{1,0:T(8,128)(2,1)}) %all-gather.16.cloned.1.call-update) | async-done | bytes 6291472 | tf_op jit(solution)/shard_map/all_gather | solution.py:221
  226.9 5.7 fusion.120
  242.1 65.8 %all-gather.2 = bf16[32,1,128]{2,1,0:T(2,128)(2,1)S(1)} all-gather(bf16[1,1,128]{2,1,0:T(2,128)(2,1)S(1)} %bitcast.272), channel_id=1, replica_groups=mesh['seq'=8,'batch'=4] {'seq','batch'}, dimensions={0}, use_global_device_ids=true | all-gather | bytes 8448 | tf_op jit(solution)/shard_map/all_gather | solution.py:224
  309.4 22.2 all-gather.26.cloned.1.call-done
  331.7 113.3 %while.32 = (s32[]{:T(128)}, bf16[8,384,2,64]{1,3,2,0:T(8,128)(2,1)S(1)}, f32[8,2,384]{2,1,0:T(2,128)S(1)}, s32[8]{0:T(128)S(1)}, bf16[8,3072,2,64]{1,3,2,0:T(8,...) while((s32[]{:T(128)}, ...), condition=%wide.region_9.10_spmd, body=%wide.region_6.9_spmd.sunk | while | flops 626441472 | bytes 34841424 | solution.py:142
  451.8 18.2 all-gather.22.cloned.1.call-done
  470.1 8.8 convolution_add_fusion
  478.8 70.2 %all-gather.24.cloned.1.call-done = bf16[4096,1024]{1,0:T(8,128)(2,1)} async-done(((bf16[128,1024]{1,0:T(8,128)(2,1)}), bf16[4096,1024]{1,0:T(8,128)(2,1)}) %all-gather.24.cloned.1.call-update) | async-done | bytes 8388624 | tf_op jit(solution)/shard_map/all_gather | solution.py:225
  549.0 11.3 convert_reduce_fusion
  560.3 6.3 multiply_reduce_fusion.2
  574.2 6.1 broadcast_in_dim.125.clone
  580.3 6.1 broadcast_in_dim.125
  586.4 227.1 %while.33 = (s32[]{:T(128)}, f32[8,3072,2,64]{1,3,2,0:T(8,128)}, f32[8,3072,2,64]{1,3,2,0:T(8,128)}, f32[8,384,2,64]{1,3,2,0:T(8,128)S(1)}, s32[8]{0:T(128)S(1)}...) while((s32[]{:T(128)}, f32[8,3072,2,64]{1,3,2,0:T(8,128)}, ...), condition=%wide.region_19.20_spmd, body=%wide.region_16.19_spmd.sunk | while | flops 1541012736 | bytes 84780440 | solution.py:190
  605.2 5.6 fusion.187
  633.5 5.6 fusion.187
  661.8 5.7 fusion.187
  690.1 5.6 fusion.187
  708.0 4.5 multiply_reduce_fusion.6
  718.5 5.6 fusion.187
  746.8 5.7 fusion.187
  775.2 5.7 fusion.187
  803.5 5.7 fusion.187
  813.5 8.1 convert_element_type.155
  821.6 8.7 copy.53
  830.3 9.2 convert_element_type.159
  839.5 8.9 copy.55
  848.9 41.9 %reduce-scatter.28.cloned.1.call-done = bf16[384,1024]{1,0:T(8,128)(2,1)} async-done(((bf16[3072,1024]{1,0:T(8,128)(2,1)}), bf16[384,1024]{1,0:T(8,128)(2,1)}) %reduce-scatter.28.cloned.1.call-update) | async-done | bytes 786448
  893.2 63.0 %reduce-scatter.30.cloned.1.call-done = bf16[384,1024]{1,0:T(8,128)(2,1)} async-done(((bf16[3072,1024]{1,0:T(8,128)(2,1)}), bf16[384,1024]{1,0:T(8,128)(2,1)}) %reduce-scatter.30.cloned.1.call-update) | async-done | bytes 786448
  960.0 7.1 multiply_reduce_fusion.1
  972.2 6.6 fusion.121
  987.6 5.6 fusion.82
  995.2 6.3 fusion.122
  1002.6 11.6 fusion.88
  1015.3 10.0 fusion.124
  1025.7 10.2 fusion.113
  1037.3 10.1 fusion.81
  1047.4 39.7 %all-reduce.6 = (f32[4096]{0:T(1024)S(1)}, f32[4096]{0:T(1024)S(1)}) all-reduce(f32[4096]{0:T(1024)S(1)} %get-tuple-element.393, f32[4096]{0:T(1024)S(1)} %copy-done.47), channel_id=8, replica_groups=mesh['seq'=8,'batch'=4] {'seq','batch'}, use_global_device_ids=true, to_apply=%region_28.29.clone | all-reduce | flops 8192 | bytes 65536
  1093.6 21.4 reduce-scatter.32.cloned.1.call-done
  1116.4 145.4 %reduce-scatter.22.cloned.1.call-done = f32[32,1024]{1,0:T(8,128)} async-done(((f32[1024,1024]{1,0:T(8,128)}), f32[32,1024]{1,0:T(8,128)}) %reduce-scatter.22.cloned.1.call-update) | async-done | bytes 131088 | tf_op jit(solution)/shard_map/reduce_scatter | solution.py:348
  1261.8 188.1 %reduce-scatter.16.cloned.1.call-done = f32[64,1024]{1,0:T(8,128)} async-done(((f32[2048,1024]{1,0:T(8,128)}), f32[64,1024]{1,0:T(8,128)}) %reduce-scatter.16.cloned.1.call-update) | async-done | bytes 262160 | tf_op jit(solution)/shard_map/reduce_scatter | solution.py:344
  1449.9 160.9 %reduce-scatter.20.cloned.1.call-done = f32[32,3072]{1,0:T(8,128)} async-done(((f32[1024,3072]{1,0:T(8,128)}), f32[32,3072]{1,0:T(8,128)}) %reduce-scatter.20.cloned.1.call-update) | async-done | bytes 393232 | tf_op jit(solution)/shard_map/reduce_scatter | solution.py:347
  1610.8 366.0 %reduce-scatter.26.cloned.1.call-done = f32[128,1024]{1,0:T(8,128)} async-done(((f32[4096,1024]{1,0:T(8,128)}), f32[128,1024]{1,0:T(8,128)}) %reduce-scatter.26.cloned.1.call-update) | async-done | bytes 524304 | tf_op jit(solution)/shard_map/reduce_scatter | solution.py:351
  1976.9 364.9 %reduce-scatter.24.cloned.1.call-done = f32[32,4096]{1,0:T(8,128)} async-done(((f32[1024,4096]{1,0:T(8,128)}), f32[32,4096]{1,0:T(8,128)}) %reduce-scatter.24.cloned.1.call-update) | async-done | bytes 524304 | tf_op jit(solution)/shard_map/reduce_scatter | solution.py:349
  2341.8 364.9 %reduce-scatter.18.cloned.1.call-done = f32[32,4096]{1,0:T(8,128)} async-done(((f32[1024,4096]{1,0:T(8,128)}), f32[32,4096]{1,0:T(8,128)}) %reduce-scatter.18.cloned.1.call-update) | async-done | bytes 524304 | tf_op jit(solution)/shard_map/reduce_scatter | solution.py:345
  (345 shorter events, 310.1 us)
Async XLA Ops:
  7.2 143.8 %all-gather.12.cloned.1.call-start = ((), (), s32[]{:S(2)}) async-start(), calls=%async_computation.9 | async-start | bytes 4325376 | tf_op jit(solution)/shard_map/all_gather | solution.py:218
  7.9 148.3 %all-gather.14.cloned.1.call-start = ((), (), s32[]{:S(2)}) async-start(), calls=%async_computation.10 | async-start | bytes 8650752 | tf_op jit(solution)/shard_map/all_gather | solution.py:219
  8.7 218.2 %all-gather.16.cloned.1.call-start = ((), (), s32[]{:S(2)}) async-start(), calls=%async_computation.11 | async-start | bytes 6488064 | tf_op jit(solution)/shard_map/all_gather | solution.py:221
  9.4 300.0 %all-gather.18.cloned.1.call-start = ((), (), s32[]{:S(2)}) async-start(), calls=%async_computation.12 | async-start | bytes 7077888 | tf_op jit(solution)/shard_map/all_gather | solution.py:279
  149.8 11.7 copy-start.49
  150.1 84.7 %copy-start.31 = (f32[384,32]{0,1:T(8,128)}, f32[384,32]{0,1:T(8,128)S(1)}, u32[]{:S(2)}) copy-start(f32[384,32]{0,1:T(8,128)S(1)} %get-tuple-element.383) | copy-start | bytes 147460
  150.1 84.6 %copy-start.33 = (f32[384,32]{0,1:T(8,128)}, f32[384,32]{0,1:T(8,128)S(1)}, u32[]{:S(2)}) copy-start(f32[384,32]{0,1:T(8,128)S(1)} %get-tuple-element.384) | copy-start | bytes 147460
  151.0 5.9 copy-start.35
  155.8 290.3 %copy-start.1 = (f32[384,1024]{1,0:T(8,128)}, f32[384,1024]{1,0:T(8,128)S(1)}, u32[]{:S(2)}) copy-start(f32[384,1024]{1,0:T(8,128)S(1)} %get-tuple-element.386) | copy-start | bytes 4718596
  155.8 8.4 copy-start.37
  156.1 8.0 copy-start.43
  167.2 65.4 %copy-start.20 = (bf16[384,1024]{1,0:T(8,128)(2,1)}, bf16[384,1024]{1,0:T(8,128)(2,1)S(1)}, u32[]{:S(2)}) copy-start(bf16[384,1024]{1,0:T(8,128)(2,1)S(1)} %fusion.75) | copy-start | bytes 2359300
  236.3 5.8 copy-start.52
  237.3 94.4 %all-gather.26.cloned.1.call-start = ((), (), s32[]{:S(2)}) async-start(), calls=%async_computation.22 | async-start | bytes 7077888 | tf_op jit(solution)/shard_map/all_gather | solution.py:280
  239.8 205.2 %all-gather.20.cloned.1.call-start = ((), (), s32[]{:S(2)}) async-start(), calls=%async_computation.13 | async-start | bytes 2162688 | tf_op jit(solution)/shard_map/all_gather | solution.py:222
  240.4 229.7 %all-gather.22.cloned.1.call-start = ((), (), s32[]{:S(2)}) async-start(), calls=%async_computation.14 | async-start | bytes 8650752 | tf_op jit(solution)/shard_map/all_gather | solution.py:223
  241.1 307.9 %all-gather.24.cloned.1.call-start = ((), (), s32[]{:S(2)}) async-start(), calls=%async_computation.15 | async-start | bytes 8650752 | tf_op jit(solution)/shard_map/all_gather | solution.py:225
  241.9 648.9 %reduce-scatter.28.cloned.1.call-start = ((), (), s32[]{:S(2)}) async-start(), calls=%async_computation.23 | async-start | bytes 7077888
  307.9 262.6 %copy-start.39 = (f32[384]{0:T(512)}, f32[384]{0:T(512)S(1)}, u32[]{:S(2)}) copy-start(f32[384]{0:T(512)S(1)} %fusion.103) | copy-start | bytes 4612
  449.0 117.6 %copy-start.3 = (f32[384,1024]{1,0:T(8,128)}, f32[384,1024]{1,0:T(8,128)S(1)}, u32[]{:S(2)}) copy-start(f32[384,1024]{1,0:T(8,128)S(1)} %get-tuple-element.388) | copy-start | bytes 4718596
  451.8 27.0 copy-start.13
  470.1 78.9 %copy-start.18 = (bf16[1,384,1024]{2,1,0:T(8,128)(2,1)S(1)}, bf16[1,384,1024]{2,1,0:T(8,128)(2,1)}, u32[]{:S(2)}) copy-start(bf16[1,384,1024]{2,1,0:T(8,128)(2,1)} %param.39) | copy-start | bytes 2359300
  549.0 11.3 copy-start.53
  560.3 6.3 copy-start.15
  580.3 6.1 copy-start.25
  580.3 6.1 copy-start.48
  830.3 125.9 %reduce-scatter.30.cloned.1.call-start = ((), (), s32[]{:S(2)}) async-start(), calls=%async_computation.24 | async-start | bytes 7077888
  848.5 266.5 %reduce-scatter.32.cloned.1.call-start = ((), (), s32[]{:S(2)}) async-start(), calls=%async_computation.25 | async-start | bytes 540672
  848.7 43.7 %copy-start.32 = (f32[384,32]{0,1:T(8,128)S(1)}, f32[384,32]{0,1:T(8,128)}, u32[]{:S(2)}) copy-start(f32[384,32]{0,1:T(8,128)} %copy-done.31) | copy-start | bytes 147460
  848.7 43.7 %copy-start.34 = (f32[384,32]{0,1:T(8,128)S(1)}, f32[384,32]{0,1:T(8,128)}, u32[]{:S(2)}) copy-start(f32[384,32]{0,1:T(8,128)} %copy-done.33) | copy-start | bytes 147460
  893.1 66.8 %copy-start.2 = (f32[384,1024]{1,0:T(8,128)S(1)}, f32[384,1024]{1,0:T(8,128)}, u32[]{:S(2)}) copy-start(f32[384,1024]{1,0:T(8,128)} %copy-done.1) | copy-start | bytes 4718596
  893.2 66.8 %copy-start.38 = (f32[384]{0:T(512)S(1)}, f32[384]{0:T(512)}, u32[]{:S(2)}) copy-start(f32[384]{0:T(512)} %copy-done.37) | copy-start | bytes 4612
  959.9 7.1 copy-start.7
  959.9 7.1 copy-start.46
  960.0 7.1 copy-start.44
  967.1 4.5 slice-start
  972.1 6.6 copy-start.36
  972.1 6.6 copy-start.51
  972.1 8.4 copy-start.11
  972.2 8.4 copy-start.23
  980.5 281.3 %reduce-scatter.22.cloned.1.call-start = ((), (), s32[]{:S(2)}) async-start(), calls=%async_computation.19 | async-start | bytes 4325376 | tf_op jit(solution)/shard_map/reduce_scatter | solution.py:348
  983.8 466.1 %reduce-scatter.16.cloned.1.call-start = ((), (), s32[]{:S(2)}) async-start(), calls=%async_computation.16 | async-start | bytes 8650752 | tf_op jit(solution)/shard_map/reduce_scatter | solution.py:344
  993.3 617.5 %reduce-scatter.20.cloned.1.call-start = ((), (), s32[]{:S(2)}) async-start(), calls=%async_computation.18 | async-start | bytes 12976128 | tf_op jit(solution)/shard_map/reduce_scatter | solution.py:347
  1001.5 975.3 %reduce-scatter.26.cloned.1.call-start = ((), (), s32[]{:S(2)}) async-start(), calls=%async_computation.21 | async-start | bytes 17301504 | tf_op jit(solution)/shard_map/reduce_scatter | solution.py:351
  1014.2 1327.6 %reduce-scatter.24.cloned.1.call-start = ((), (), s32[]{:S(2)}) async-start(), calls=%async_computation.20 | async-start | bytes 17301504 | tf_op jit(solution)/shard_map/reduce_scatter | solution.py:349
  1025.4 1681.3 %reduce-scatter.18.cloned.1.call-start = ((), (), s32[]{:S(2)}) async-start(), calls=%async_computation.17 | async-start | bytes 17301504 | tf_op jit(solution)/shard_map/reduce_scatter | solution.py:345
  1037.3 10.1 copy-start.47
  1037.3 51.0 %copy-start.17 = (bf16[384,1024]{1,0:T(8,128)(2,1)S(1)}, bf16[384,1024]{1,0:T(8,128)(2,1)}, u32[]{:S(2)}) copy-start(bf16[384,1024]{1,0:T(8,128)(2,1)} %copy-done.16) | copy-start | bytes 2359300
  (25 other events, 48.6 us)
Sparse Core Ops, SparseCore 0:
  11.0 64.8 all-gather.11
  78.8 76.6 all-gather.13
  158.4 68.4 all-gather.15
  237.4 45.1 all-gather.17
  284.9 46.6 all-gather.25
  334.4 56.5 all-gather.19
  393.9 76.0 all-gather.21
  473.0 75.9 all-gather.23
  830.4 60.3 reduce-scatter.27
  894.4 61.7 reduce-scatter.29
  980.6 134.3 reduce-scatter.31
  1117.8 143.9 reduce-scatter.21
  1264.7 185.1 reduce-scatter.15
  1457.4 153.3 reduce-scatter.19
  1613.5 363.2 reduce-scatter.25
  1979.6 362.1 reduce-scatter.23
  2344.5 362.1 reduce-scatter.17
where the time goes:
time: 2720 us; the launch traced here: 2710 us
  waiting for transfers between devices  1890 us (69%)
  matrix products  342 us (13%)
  blocking collectives  243 us (9%)
  other arithmetic  102 us (4%)
  local copies, waits for them, and re-layouts  67 us (2%)
  loops' own time  53 us (2%)
    reduce_scatter x1, waiting for transfers between devices, shards(): lax.psum_scatter(grad_down, ('seq', 'batch'), scatter_dimension=0, tiled=...  366 us
    reduce_scatter x1, waiting for transfers between devices, shards(): lax.psum_scatter(grad_up, ('seq', 'batch'), scatter_dimension=0, tiled=True)  365 us
    reduce_scatter x1, waiting for transfers between devices, shards(): lax.psum_scatter(grad_mod_w, ('seq', 'batch'), scatter_dimension=0, tiled...  365 us
    reduce_scatter x1, waiting for transfers between devices, shards(): lax.psum_scatter(grad_skip_w, ('seq', 'batch'), scatter_dimension=0, tile...  188 us
    reduce_scatter x1, waiting for transfers between devices, shards(): lax.psum_scatter(grad_qkv_w, ('seq', 'batch'), scatter_dimension=0, tiled...  161 us
    reduce_scatter x1, waiting for transfers between devices, shards(): lax.psum_scatter(grad_out_w, ('seq', 'batch'), scatter_dimension=0, tiled...  145 us
    unnamed x20, waiting for transfers between devices  130 us
    all_gather x1, waiting for transfers between devices, shards(): lax.all_gather(down_proj, ('seq', 'batch'), axis=0, tiled=True)  70.2 us
  transfers between devices with their start and end apart: 17, of which 13 were waited for; matrix products, arithmetic and copies ran while one was open for 8% of the time, Pallas kernels for 0%

commit v1 on v0

v1 whole, which is shorter than its diff:
```python
import functools
import math

import jax
import jax.numpy as jnp
from jax import lax
from jax.experimental import pallas as pl
from jax.experimental.pallas import tpu as pltpu
from jax.sharding import PartitionSpec as P

HEADS = 16
HD = 64
LANES = 128
MASKED = -(2.0 ** 100)
NORM_EPS = 1e-06
BOTH = ("seq", "batch")
NT = (((1,), (1,)), ((), ()))
NN = (((1,), (0,)), ((), ()))
TN = (((0,), (0,)), ((), ()))
highest = lax.Precision.HIGHEST


def mm(a, b, dims):
    return lax.dot_general(a, b, dims, preferred_element_type=jnp.float32)


def utt_of(ends_ref, rows, utts):
    found = jnp.zeros_like(rows)
    for u in range(utts - 1):
        found = found + (rows >= ends_ref[u]).astype(jnp.int32)
    return found


def key_range(ends_ref, first, last, utts, frames):
    low = 0
    high = frames
    for u in range(utts - 1):
        low = jnp.where(first >= ends_ref[u], ends_ref[u], low)
    for u in reversed(range(utts - 1)):
        high = jnp.where(last < ends_ref[u], ends_ref[u], high)
    return low, high


def split3(x):
    a = x.astype(jnp.bfloat16).astype(jnp.float32)
    b = (x - a).astype(jnp.bfloat16).astype(jnp.float32)
    return a, b, x - a - b


def fwd_kernel(ends_ref, qkv_ref, out_ref, lse_ref, q_s, k_s, v_s, m_s, acc_s, *, heads, utts, bq, bk):
    sources, _, rows, _ = qkv_ref.shape
    frames = sources * rows

    def build(src, carry):
        at = pl.multiple_of(src * rows, rows)
        lane = lax.broadcasted_iota(jnp.int32, (rows, LANES), 1)
        row = lax.broadcasted_iota(jnp.int32, (rows, LANES), 0) + at
        utt = utt_of(ends_ref, row, utts)
        for h in range(heads):
            spare = (1 - h) * HD
            mine = (lane >= HD) if h else (lane < HD)
            slot = lane - spare
            is_slot = (slot >= 0) & (slot < utts)
            qf = jnp.where(is_slot & (slot != utt), MASKED, 0.0)
            kf = jnp.where(slot == utt, 1.0, 0.0)
            vf = jnp.where(slot == 0, 1.0, 0.0)
            for part, feat, dst in ((0, qf, q_s), (1, kf, k_s), (2, vf, v_s)):
                x = qkv_ref[src, part].astype(jnp.float32)
                dst[h, pl.ds(at, rows), :] = jnp.where(mine, x, feat).astype(jnp.bfloat16)
        return carry

    lax.fori_loop(0, sources, build, 0)

    def q_block(i, carry):
        at = pl.multiple_of(i * bq, bq)
        low, high = key_range(ends_ref, at, at + bq - 1, utts, frames)
        m_s[...] = jnp.full(m_s.shape, -3.0e38, jnp.float32)
        acc_s[...] = jnp.zeros(acc_s.shape, jnp.float32)

        def k_block(j, inner):
            kat = pl.multiple_of(j * bk, bk)
            for h in range(heads):
                s = mm(q_s[h, pl.ds(at, bq), :], k_s[h, pl.ds(kat, bk), :], NT)
                old = m_s[h]
                top = jnp.maximum(old, jnp.max(s, axis=1, keepdims=True))
                alpha = jnp.exp(old - top)
                p = jnp.exp(s - top[:, :1]).astype(jnp.bfloat16)
                acc_s[h] = acc_s[h] * alpha + mm(p, v_s[h, pl.ds(kat, bk), :], NN)
                m_s[h] = top
            return inner

        lax.fori_loop(low // bk, (high + bk - 1) // bk, k_block, 0)
        lane = lax.broadcasted_iota(jnp.int32, (bq, LANES), 1)
        out = None
        lse = None
        for h in range(heads):
            spare = (1 - h) * HD
            acc = acc_s[h]
            total = acc[:, spare : spare + 1]
            o = acc / total
            l = m_s[h] + jnp.log(total)
            out = o if out is None else jnp.where(lane < HD, out, o)
            lse = l if lse is None else jnp.where(lane < HD, lse, l)
        out_ref[pl.ds(at, bq), :] = out.astype(jnp.bfloat16)
        lse_ref[pl.ds(at, bq), :] = lse
        return carry

    lax.fori_loop(0, frames // bq, q_block, 0)


def attend(qkv, ends, heads, bq, bk):
    sources, _, rows, _ = qkv.shape
    frames = sources * rows
    utts = ends.shape[0]
    return pl.pallas_call(
        functools.partial(fwd_kernel, heads=heads, utts=utts, bq=bq, bk=bk),
        out_shape=(
            jax.ShapeDtypeStruct((frames, LANES), jnp.bfloat16),
            jax.ShapeDtypeStruct((frames, LANES), jnp.float32),
        ),
        in_specs=[pl.BlockSpec(memory_space=pltpu.SMEM), pl.BlockSpec(memory_space=pltpu.VMEM)],
        out_specs=(pl.BlockSpec(memory_space=pltpu.VMEM), pl.BlockSpec(memory_space=pltpu.VMEM)),
        scratch_shapes=[pltpu.VMEM((heads, frames, LANES), jnp.bfloat16)] * 3
        + [pltpu.VMEM((heads, bq, LANES), jnp.float32)] * 2,
        compiler_params=pltpu.CompilerParams(vmem_limit_bytes=56 * 1024 * 1024),
        cost_estimate=pl.CostEstimate(
            flops=40 * heads * frames * frames * HD, bytes_accessed=frames * LANES * 12,
            transcendentals=heads * frames * frames,
        ),
        name="attend",
    )(ends, qkv)


def bwd_kernel(ends_ref, qkv_ref, da_ref, out_ref, lse_ref, cos_ref, sin_ref, grad_ref,
               q_s, k_s, v_s, d_s, gq_s, gk_s, gv_s, *, heads, utts, bq, bk):
    sources, _, rows, _ = qkv_ref.shape
    frames = sources * rows

    def build(src, carry):
        at = pl.multiple_of(src * rows, rows)
        lane = lax.broadcasted_iota(jnp.int32, (rows, LANES), 1)
        row = lax.broadcasted_iota(jnp.int32, (rows, LANES), 0) + at
        utt = utt_of(ends_ref, row, utts)
        da = da_ref[pl.ds(at, rows), :].astype(jnp.float32)
        prod = da * out_ref[pl.ds(at, rows), :].astype(jnp.float32)
        lse = lse_ref[pl.ds(at, rows), :]
        for h in range(heads):
            spare = (1 - h) * HD
            mine = (lane >= HD) if h else (lane < HD)
            slot = lane - spare
            is_slot = (slot >= 0) & (slot < utts)
            delta = jnp.sum(jnp.where(mine, prod, 0.0), axis=1, keepdims=True)
            l3 = split3(-lse[:, h * HD : h * HD + 1])
            d3 = split3(-delta)
            qf = jnp.where(is_slot & (slot != utt), MASKED, 0.0)
            df = jnp.zeros_like(qf)
            for n in range(3):
                qf = jnp.where(slot == utts + n, l3[n], qf)
                df = jnp.where(slot == n, d3[n], df)
            kf = jnp.where((slot == utt) | ((slot >= utts) & (slot < utts + 3)), 1.0, 0.0)
            vf = jnp.where((slot >= 0) & (slot < 3), 1.0, 0.0)
            for x, feat, dst in (
                (qkv_ref[src, 0], qf, q_s), (qkv_ref[src, 1], kf, k_s), (qkv_ref[src, 2], vf, v_s),
            ):
                dst[h, pl.ds(at, rows), :] = jnp.where(mine, x.astype(jnp.float32), feat).astype(jnp.bfloat16)
            d_s[h, pl.ds(at, rows), :] = jnp.where(mine, da, df).astype(jnp.bfloat16)
        gq_s[:, pl.ds(at, rows), :] = jnp.zeros((heads, rows, LANES), jnp.float32)
        return carry

    lax.fori_loop(0, sources, build, 0)

    def k_block(j, carry):
        kat = pl.multiple_of(j * bk, bk)
        low, high = key_range(ends_ref, kat, kat + bk - 1, utts, frames)
        gk_s[:, pl.ds(kat, bk), :] = jnp.zeros((heads, bk, LANES), jnp.float32)
        gv_s[:, pl.ds(kat, bk), :] = jnp.zeros((heads, bk, LANES), jnp.float32)

        def q_block(i, inner):
            at = pl.multiple_of(i * bq, bq)
            for h in range(heads):
                q = q_s[h, pl.ds(at, bq), :]
                d = d_s[h, pl.ds(at, bq), :]
                k = k_s[h, pl.ds(kat, bk), :]
                p = jnp.exp(mm(k, q, NT))
                ds = (p * mm(v_s[h, pl.ds(kat, bk), :], d, NT)).astype(jnp.bfloat16)
                gv_s[h, pl.ds(kat, bk), :] += mm(p.astype(jnp.bfloat16), d, NN)
                gk_s[h, pl.ds(kat, bk), :] += mm(ds, q, NN)
                gq_s[h, pl.ds(at, bq), :] += mm(ds, k, TN)
            return inner

        lax.fori_loop(low // bq, (high + bq - 1) // bq, q_block, 0)
        return carry

    lax.fori_loop(0, frames // bk, k_block, 0)

    def finish(src, carry):
        at = pl.multiple_of(src * rows, rows)
        lane = lax.broadcasted_iota(jnp.int32, (rows, LANES), 1)
        first = (lane % HD) < HD // 2
        cos = cos_ref[pl.ds(at, rows), :]
        sin = sin_ref[pl.ds(at, rows), :]

        def both(ref):
            x = ref[0, pl.ds(at, rows), :]
            return jnp.where(lane < HD, x, ref[1, pl.ds(at, rows), :]) if heads == 2 else x

        def unturn(x):
            partner = jnp.where(first, pltpu.roll(x, LANES - HD // 2, 1), pltpu.roll(x, HD // 2, 1))
            return x * cos - partner * sin

        grad_ref[src, 0] = (unturn(both(gq_s)) * HD ** -0.5).astype(jnp.bfloat16)
        grad_ref[src, 1] = unturn(both(gk_s)).astype(jnp.bfloat16)
        grad_ref[src, 2] = both(gv_s).astype(jnp.bfloat16)
        return carry

    lax.fori_loop(0, sources, finish, 0)


def attend_back(qkv, grad_out, out, lse, cos, sin, ends, heads, bq, bk):
    sources, _, rows, _ = qkv.shape
    frames = sources * rows
    utts = ends.shape[0]
    vmem = pl.BlockSpec(memory_space=pltpu.VMEM)
    return pl.pallas_call(
        functools.partial(bwd_kernel, heads=heads, utts=utts, bq=bq, bk=bk),
        out_shape=jax.ShapeDtypeStruct(qkv.shape, jnp.bfloat16),
        in_specs=[pl.BlockSpec(memory_space=pltpu.SMEM)] + [vmem] * 6,
        out_specs=vmem,
        scratch_shapes=[pltpu.VMEM((heads, frames, LANES), jnp.bfloat16)] * 4
        + [pltpu.VMEM((heads, frames, LANES), jnp.float32)] * 3,
        compiler_params=pltpu.CompilerParams(vmem_limit_bytes=60 * 1024 * 1024),
        cost_estimate=pl.CostEstimate(
            flops=64 * heads * frames * frames * HD, bytes_accessed=frames * LANES * 24,
            transcendentals=heads * frames * frames,
        ),
        name="attend_back",
    )(ends, qkv, grad_out, out, lse, cos, sin)


def project_kernel(normed_ref, weight_ref, cos_ref, sin_ref, out_ref):
    part = pl.program_id(0)
    weight = weight_ref[...].reshape(-1, weight_ref.shape[-1])
    turned = mm(normed_ref[...], weight, NN)
    lane = lax.broadcasted_iota(jnp.int32, (turned.shape[0], LANES), 1)
    first = (lane % HD) < HD // 2
    scale = jnp.where(part == 0, HD ** -0.5, 1.0)
    for at in range(out_ref.shape[0]):
        x = turned[:, at * LANES : (at + 1) * LANES]
        partner = jnp.where(first, pltpu.roll(x, LANES - HD // 2, 1), pltpu.roll(x, HD // 2, 1))
        rotated = (x * cos_ref[...] + partner * sin_ref[...]) * scale
        out_ref[at, 0] = jnp.where(part == 2, x, rotated).astype(jnp.bfloat16)


def project(normed, gathered, first_row, rows_each, cos, sin):
    rows, width = normed.shape
    devices = gathered.shape[0]
    targets = width // LANES
    each = 2
    at = first_row // rows_each
    return pl.pallas_call(
        project_kernel,
        grid=(3, targets // each),
        out_shape=jax.ShapeDtypeStruct((targets, 3, rows, LANES), jnp.bfloat16),
        in_specs=[
            pl.BlockSpec((rows, width), lambda p, t: (0, 0)),
            pl.BlockSpec((devices, rows_each, each * LANES), lambda p, t: (0, at + p, t)),
            pl.BlockSpec((rows, LANES), lambda p, t: (0, 0)),
            pl.BlockSpec((rows, LANES), lambda p, t: (0, 0)),
        ],
        out_specs=pl.BlockSpec((each, 1, rows, LANES), lambda p, t: (t, p, 0, 0)),
        compiler_params=pltpu.CompilerParams(vmem_limit_bytes=40 * 1024 * 1024),
        cost_estimate=pl.CostEstimate(
            flops=6 * rows * width * width, bytes_accessed=8 * width * width, transcendentals=0
        ),
        name="project",
    )(normed, gathered, cos, sin)


def rows_of(first_op, second_op):
    return lax.dot_general(first_op, second_op, TN, preferred_element_type=jnp.float32)


def times(first_op, second_op):
    return lax.dot_general(first_op, second_op, NN, preferred_element_type=jnp.float32)


def times_transpose(first_op, second_op):
    return lax.dot_general(first_op, second_op, NT, preferred_element_type=jnp.float32)


def swap(value, bit):
    size = lax.axis_size("seq")
    return lax.ppermute(value, "seq", [(i, i ^ bit) for i in range(size)])


def ahead(value, step):
    size = lax.axis_size("batch")
    return lax.ppermute(value, "batch", [(i, (i + step) % size) for i in range(size)])


def column_blocks(value, starts, width):
    return jnp.concatenate(
        [lax.dynamic_slice_in_dim(value, s, width, axis=1) for s in starts], axis=1
    )


def scatter_sum(first_op, second_op, bits):
    seq = lax.axis_size("seq")
    batch = lax.axis_size("batch")
    me = lax.axis_index("seq")
    rows_total = first_op.shape[1]
    block = rows_total // seq
    core = me & 1

    def starts(keep_of):
        return [(2 * i + keep_of(i)) * block for i in range(seq // 2)]

    other = swap(column_blocks(first_op, starts(lambda i: 1 - core), block), 1)
    second_other = swap(second_op, 1)
    mine = column_blocks(first_op, starts(lambda i: core), block)
    left = jnp.concatenate([mine, other], axis=0)
    right = jnp.concatenate([second_op, second_other], axis=0)
    high_bits = [seq >> (i + 1) for i in range(seq.bit_length() - 2)]
    bit = bits[0]
    shift = bit.bit_length() - 1
    value = (me >> shift) & 1
    chosen = [i for i in range(seq // 2) if not (2 * i) & bit]
    keep_at = [(i + value * (bit // 2)) * block for i in chosen]
    send_at = [(i + (1 - value) * (bit // 2)) * block for i in chosen]
    sent = rows_of(column_blocks(left, send_at, block), right).astype(jnp.bfloat16)
    came = swap(sent, bit)
    total = rows_of(column_blocks(left, keep_at, block), right) + came.astype(jnp.float32)
    left_bits = [b for b in high_bits if b != bit]
    total = total.astype(jnp.bfloat16).reshape(
        (2,) * len(left_bits) + (batch, block // batch, second_op.shape[1])
    )
    for bit in bits[1:]:
        axis = left_bits.index(bit)
        value = (me >> (bit.bit_length() - 1)) & 1
        came = swap(lax.dynamic_index_in_dim(total, 1 - value, axis, keepdims=False), bit)
        kept = lax.dynamic_index_in_dim(total, value, axis, keepdims=False)
        total = (kept.astype(jnp.float32) + came.astype(jnp.float32)).astype(jnp.bfloat16)
        left_bits.remove(bit)
    place = lax.axis_index("batch")
    result = lax.dynamic_index_in_dim(total, place, 0, keepdims=False).astype(jnp.float32)
    for step in range(1, batch):
        piece = lax.dynamic_index_in_dim(total, (place + step) % batch, 0, keepdims=False)
        result = result + ahead(piece, step).astype(jnp.float32)
    return result


def normalise(hidden):
    centred = hidden - jnp.mean(hidden, axis=-1, keepdims=True)
    inverse = lax.rsqrt(jnp.mean(centred * centred, axis=-1, keepdims=True) + NORM_EPS)
    return centred * inverse, inverse


def normalise_back(grad, normed, inverse):
    return inverse * (
        grad
        - jnp.mean(grad, axis=-1, keepdims=True)
        - normed * jnp.mean(grad * normed, axis=-1, keepdims=True)
    )


def per_row(member, table):
    total = member[:, 0:1] * table[0:1]
    for u in range(1, table.shape[0]):
        total = total + member[:, u : u + 1] * table[u : u + 1]
    return total


def gelu_parts(x):
    rate = math.sqrt(2.0 / math.pi)
    inner = jnp.tanh(rate * (x + 0.044715 * x * x * x))
    value = 0.5 * x * (1.0 + inner)
    slope = 0.5 * (1.0 + inner) + 0.5 * x * (1.0 - inner * inner) * rate * (
        1.0 + 3 * 0.044715 * x * x
    )
    return value, slope


def turn_tables(position):
    half = HD // 2
    lane = jnp.arange(LANES, dtype=jnp.int32)
    rates = jnp.exp((lane % half).astype(jnp.float32) * (-math.log(10000.0) / half))
    angles = position.astype(jnp.float32)[:, None] * rates[None, :]
    side = jnp.where((lane % HD) < half, -1.0, 1.0).astype(jnp.float32)
    return jnp.cos(angles), jnp.sin(angles) * side[None, :]


def all_pieces(value):
    batch = lax.axis_size("batch")
    place = lax.axis_index("batch")
    out = jnp.zeros((batch,) + value.shape, value.dtype)
    out = lax.dynamic_update_index_in_dim(out, value, place, 0)
    for step in range(1, batch):
        out = lax.dynamic_update_index_in_dim(
            out, ahead(value, step), (place - step) % batch, 0
        )
    return out


def seq_total(value):
    bit = 1
    while bit < lax.axis_size("seq"):
        value = value + swap(value, bit)
        bit *= 2
    return value


def shards(
    frames_in,
    skip_in,
    time_table,
    timestep,
    lengths,
    span_start,
    span_len,
    skip_proj,
    mod_proj,
    mod_bias,
    qkv_proj,
    out_proj,
    up_proj,
    up_bias,
    down_proj,
    cotangent,
):
    seq = lax.axis_size("seq")
    batch = lax.axis_size("batch")
    seq_at = lax.axis_index("seq")
    batch_at = lax.axis_index("batch")
    device = seq_at * batch + batch_at
    devices = seq * batch
    inputs = frames_in[0]
    skip_rows = skip_in[0]
    rows, width = inputs.shape
    hidden = up_proj.shape[1]
    frames = rows * seq
    heads = HEADS // seq
    utts = lengths.shape[1]

    early = jnp.concatenate(
        [skip_proj] + [qkv_proj[:, p * width : (p + 1) * width] for p in range(3)], axis=0
    )
    late = jnp.concatenate(
        [down_proj, out_proj]
        + [up_proj[:, p * width : (p + 1) * width] for p in range(hidden // width)],
        axis=0,
    )
    early = lax.all_gather(early, BOTH, axis=0, tiled=False)
    late = lax.all_gather(late, BOTH, axis=0, tiled=False)
    skip_each, qkv_each, out_each, up_each, down_each = (
        skip_proj.shape[0],
        qkv_proj.shape[0],
        out_proj.shape[0],
        up_proj.shape[0],
        down_proj.shape[0],
    )
    full_skip = early[:, :skip_each].reshape(2 * width, width)
    full_qkv = [
        early[:, skip_each + p * qkv_each : skip_each + (p + 1) * qkv_each].reshape(width, width)
        for p in range(3)
    ]
    full_down = late[:, :down_each].reshape(hidden, width)
    full_out = late[:, down_each : down_each + out_each].reshape(width, width)
    full_up = (
        late[:, down_each + out_each :]
        .reshape(devices, hidden // width, up_each, width)
        .transpose(0, 2, 1, 3)
        .reshape(width, hidden)
    )

    utt_lengths = lengths[0]
    ends = jnp.cumsum(utt_lengths).astype(jnp.int32)
    starts = ends - utt_lengths
    frame_ids = seq_at * rows + jnp.arange(rows, dtype=jnp.int32)
    group_ids = jnp.arange(frames, dtype=jnp.int32)

    def members(ids):
        return (ids[:, None] >= starts[None, :]) & (ids[:, None] < ends[None, :])

    member = members(frame_ids)
    member_int = member.astype(jnp.int32)
    position = frame_ids - jnp.sum(member_int * starts[None, :], axis=1)
    span_first = jnp.sum(member_int * span_start[0][None, :], axis=1)
    span_after = span_first + jnp.sum(member_int * span_len[0][None, :], axis=1)
    in_span = ((position >= span_first) & (position < span_after)).astype(jnp.float32)
    member_rows = member.astype(jnp.float32)
    group_position = group_ids - jnp.sum(members(group_ids).astype(jnp.int32) * starts[None, :], axis=1)
    cos, sin = turn_tables(position)
    group_cos, group_sin = turn_tables(group_position)

    steps = all_pieces(timestep[0]).reshape(-1)
    step_pick = (
        steps[:, None] == jnp.arange(time_table.shape[0], dtype=jnp.int32)[None, :]
    ).astype(jnp.float32)
    time_rows = jnp.dot(step_pick, time_table.astype(jnp.float32), precision=highest)
    silu_value, silu_pull = jax.vjp(jax.nn.silu, time_rows)
    time_vec = silu_value.astype(jnp.bfloat16)
    terms = times(time_vec, mod_proj)
    bias_terms = lax.dynamic_update_slice(
        jnp.zeros((4 * width,), jnp.float32),
        mod_bias.astype(jnp.float32),
        (device * mod_bias.shape[0],),
    )
    terms = (terms + bias_terms[None, :]).reshape(batch, utts, 4 * width)
    modulation = lax.dynamic_index_in_dim(terms, batch_at, 0, keepdims=False)
    for step in range(1, batch):
        modulation = modulation + ahead(
            lax.dynamic_index_in_dim(terms, (batch_at + step) % batch, 0, keepdims=False), step
        )
    modulation = seq_total(modulation)
    scale_one = per_row(member_rows, 1.0 + modulation[:, :width])
    shift_one = per_row(member_rows, modulation[:, width : 2 * width])
    scale_two = per_row(member_rows, 1.0 + modulation[:, 2 * width : 3 * width])
    shift_two = per_row(member_rows, modulation[:, 3 * width :])
    full_bup = all_gather_bias(up_bias)

    joined = jnp.concatenate([inputs, skip_rows], axis=1)
    stream_in = times(joined, full_skip)
    unit_one, inverse_one = normalise(stream_in)
    normed_one = (unit_one * scale_one + shift_one).astype(jnp.bfloat16)
    sent = project(normed_one, early, skip_each, qkv_each, cos, sin)
    per_device = width // seq
    if per_device < LANES:
        sent = sent.reshape(-1, 3, rows, 2, per_device).transpose(0, 3, 1, 2, 4)
        sent = sent.reshape(seq, 3, rows, per_device)
        sent = jnp.pad(sent, ((0, 0), (0, 0), (0, 0), (0, LANES - per_device)))
    held = lax.all_to_all(sent, "seq", 0, 0, tiled=True)
    head_out, log_sums = attend(held, ends, heads, 1024, 512)
    attended = lax.all_to_all(
        head_out.reshape(seq, rows, LANES)[:, :, :per_device], "seq", 0, 0, tiled=True
    )
    attended = attended.transpose(1, 0, 2).reshape(rows, width)
    stream_mid = stream_in + times(attended, full_out)
    unit_two, inverse_two = normalise(stream_mid)
    normed_two = (unit_two * scale_two + shift_two).astype(jnp.bfloat16)
    pre_act = times(normed_two, full_up) + full_bup[None, :]
    act_value, act_slope = gelu_parts(pre_act)
    activated = act_value.astype(jnp.bfloat16)
    result = (stream_mid + times(activated, full_down)).astype(jnp.bfloat16)

    grad_result = cotangent[0].astype(jnp.float32) * in_span[:, None]
    grad_branch = grad_result.astype(jnp.bfloat16)
    grad_pre = (times_transpose(grad_branch, full_down) * act_slope).astype(jnp.bfloat16)
    grad_normed = times_transpose(grad_pre, full_up)
    grad_mid = grad_result + normalise_back(grad_normed * scale_two, unit_two, inverse_two)
    grad_attn_out = grad_mid.astype(jnp.bfloat16)
    grad_attended = times_transpose(grad_attn_out, full_out).astype(jnp.bfloat16)
    high = [seq >> (i + 1) for i in range(seq.bit_length() - 2)]
    low = high[::-1]
    grad_down = scatter_sum(activated, grad_branch, low)
    grad_up = scatter_sum(normed_two, grad_pre, high)
    grad_out_w = scatter_sum(attended, grad_attn_out, high)
    mod_two = jnp.concatenate(
        [
            jnp.dot(member_rows.T, grad_normed * unit_two, precision=highest),
            jnp.dot(member_rows.T, grad_normed, precision=highest),
        ],
        axis=1,
    )

    back = grad_attended.reshape(rows, seq, per_device).transpose(1, 0, 2)
    if per_device < LANES:
        back = jnp.pad(back, ((0, 0), (0, 0), (0, LANES - per_device)))
    back = lax.all_to_all(back, "seq", 0, 0, tiled=True).reshape(frames, LANES)
    grad_held = attend_back(
        held, back, head_out, log_sums, group_cos, group_sin, ends, heads, 1024, 512
    )
    grad_projected = lax.all_to_all(grad_held[..., :per_device], "seq", 0, 0, tiled=True)
    grad_projected = grad_projected.transpose(2, 1, 0, 3).reshape(rows, 3 * width)
    grad_qkv_w = scatter_sum(normed_one, grad_projected, low)
    grad_normed_one = sum(
        times_transpose(grad_projected[:, p * width : (p + 1) * width], full_qkv[p])
        for p in range(3)
    )
    grad_stream = (
        grad_mid + normalise_back(grad_normed_one * scale_one, unit_one, inverse_one)
    ).astype(jnp.bfloat16)
    grad_skip_w = scatter_sum(joined, grad_stream, high)
    grad_joined = times_transpose(grad_stream, full_skip)
    grad_inputs = grad_joined[:, :width].astype(jnp.bfloat16)
    grad_skip_rows = grad_joined[:, width:].astype(jnp.bfloat16)

    mod_one = jnp.concatenate(
        [
            jnp.dot(member_rows.T, grad_normed_one * unit_one, precision=highest),
            jnp.dot(member_rows.T, grad_normed_one, precision=highest),
        ],
        axis=1,
    )
    grad_modulation = all_pieces(seq_total(jnp.concatenate([mod_one, mod_two], axis=1)))
    grad_modulation = grad_modulation.reshape(batch * utts, 4 * width)
    grad_bmod = lax.dynamic_slice_in_dim(
        jnp.sum(grad_modulation, axis=0), device * mod_bias.shape[0], mod_bias.shape[0]
    )
    grad_mod_w = jnp.dot(time_vec.astype(jnp.float32).T, grad_modulation, precision=highest)
    grad_time_vec = jnp.dot(grad_modulation, mod_proj.astype(jnp.float32).T, precision=highest)
    grad_table = jnp.dot(step_pick.T, silu_pull(grad_time_vec)[0], precision=highest)
    grad_bup = bias_total(jnp.sum(grad_pre.astype(jnp.float32), axis=0))
    return (
        result[None],
        grad_inputs[None],
        grad_skip_rows[None],
        grad_table,
        grad_skip_w,
        grad_mod_w,
        grad_bmod,
        grad_qkv_w,
        grad_out_w,
        grad_up,
        grad_bup,
        grad_down,
    )


def all_gather_bias(bias):
    seq = lax.axis_size("seq")
    pieces = all_pieces(bias.astype(jnp.float32)).reshape(1, -1)
    bit = 1
    out = jnp.zeros((seq, pieces.shape[1]), jnp.float32)
    out = lax.dynamic_update_slice(out, pieces, (lax.axis_index("seq"), 0))
    return seq_total(out).reshape(-1)


def bias_total(terms):
    batch = lax.axis_size("batch")
    place = lax.axis_index("batch")
    size = terms.shape[0] // (lax.axis_size("seq") * batch)
    terms = seq_total(terms.reshape(-1, size))
    total = lax.dynamic_slice_in_dim(terms, lax.axis_index("seq") * batch, batch, axis=0)
    result = lax.dynamic_index_in_dim(total, place, 0, keepdims=False)
    for step in range(1, batch):
        result = result + ahead(
            lax.dynamic_index_in_dim(total, (place + step) % batch, 0, keepdims=False), step
        )
    return result


def solution(mesh):
    return jax.shard_map(
        shards,
        mesh=mesh,
        in_specs=(
            P("batch", "seq", None),
            P("batch", "seq", None),
            P(None, BOTH),
            P("batch", None),
            P("batch", None),
            P("batch", None),
            P("batch", None),
            P(BOTH, None),
            P(BOTH, None),
            P(BOTH),
            P(BOTH, None),
            P(BOTH, None),
            P(BOTH, None),
            P(BOTH),
            P(BOTH, None),
            P("batch", "seq", None),
        ),
        out_specs=(
            P("batch", "seq", None),
            P("batch", "seq", None),
            P("batch", "seq", None),
            P(None, BOTH),
            P(BOTH, None),
            P(BOTH, None),
            P(BOTH),
            P(BOTH, None),
            P(BOTH, None),
            P(BOTH, None),
            P(BOTH),
            P(BOTH, None),
        ),
        check_vma=False,
    )
```

time: 2720 us -> 726 us (0.27)
  waiting for transfers between devices: 1890 us -> 273 us
  matrix products: 342 us -> 93.8 us
  blocking collectives: 243 us -> 0 us
  Pallas kernels: 0 us -> 118 us
  starting transfers between devices: 1.11 us -> 96.9 us
  loops' own time: 53 us -> 0 us
  other arithmetic: 102 us -> 49.2 us
    reduce_scatter x6 -> x0, waiting for transfers between devices: 1590 us -> none  [the longest x1 366 us: shards(): lax.psum_scatter(grad_down, ('seq', 'batch'), scatter_dimension=0, tiled=...]
    dot_general x76 -> x29, matrix products: 330 us -> 92.6 us  [the longest x10 35.6 us: rows_of(): lax.dot_general(first_op, second_op, TN, preferred_element_type=jnp.float32)]
    ppermute x0 -> x62, waiting for transfers between devices: none -> 212 us  [the longest x32 158 us: swap(): return lax.ppermute(value, 'seq', [(i, i ^ bit) for i in range(size)])]
    all_gather x3 -> x0, blocking collectives: 203 us -> none  [the longest x1 69.6 us: shards(): lax.all_gather(mod_bias, ('seq', 'batch'), axis=0, tiled=True)]
    unnamed x20 -> x2, waiting for transfers between devices: 130 us -> 0.03 us
    pallas_call x0 -> x3, Pallas kernels: none -> 118 us  [the longest x1 65.3 us: attend_back(): pl.pallas_call(functools.partial(bwd_kernel, heads=heads, utts=utts, bq=b...]
    all_gather x8 -> x2, waiting for transfers between devices: 170 us -> 53.4 us  [the longest x1 53.4 us: shards(): early = lax.all_gather(early, BOTH, axis=0, tiled=False)]
    ppermute x0 -> x62, starting transfers between devices: none -> 80.2 us  [the longest x30 55.4 us: ahead(): lax.ppermute(value, 'batch', [(i, (i + step) % size) for i in range(size)])]
  transfers between devices with their start and end apart: 17 -> 68, of which waited for: 13 -> 28; matrix products, arithmetic and copies ran while one was open for 8% -> 19% of each run, Pallas kernels for 0% -> 16%
where the time goes in v1:
time: 726 us; the launch traced here: 716 us
  waiting for transfers between devices  273 us (38%)
  Pallas kernels  118 us (16%)
  starting transfers between devices  96.9 us (13%)
  matrix products  93.8 us (13%)
  local copies, waits for them, and re-layouts  69.1 us (10%)
  other arithmetic  49.2 us (7%)
  between operations  16 us (2%)
    ppermute x32, waiting for transfers between devices, swap(): return lax.ppermute(value, 'seq', [(i, i ^ bit) for i in range(size)])  158 us
    pallas_call x1, Pallas kernels, attend_back(): pl.pallas_call(functools.partial(bwd_kernel, heads=heads, utts=utts, bq=b...  65.3 us
    ppermute x30, starting transfers between devices, ahead(): lax.ppermute(value, 'batch', [(i, (i + step) % size) for i in range(size)])  55.4 us
    ppermute x30, waiting for transfers between devices, ahead(): lax.ppermute(value, 'batch', [(i, (i + step) % size) for i in range(size)])  53.9 us
    all_gather x1, waiting for transfers between devices, shards(): early = lax.all_gather(early, BOTH, axis=0, tiled=False)  53.4 us
    pallas_call x1, Pallas kernels, attend(): pl.pallas_call(functools.partial(fwd_kernel, heads=heads, utts=utts, bq=b...  44 us
    dot_general x10, matrix products, rows_of(): lax.dot_general(first_op, second_op, TN, preferred_element_type=jnp.float32)  35.6 us
    dot_general x7, matrix products, times_transpose(): lax.dot_general(first_op, second_op, NT, preferred_element_type=jnp.float32)  34.3 us
  transfers between devices with their start and end apart: 68, of which 28 were waited for; matrix products, arithmetic and copies ran while one was open for 19% of the time, Pallas kernels for 16%

profile of v1, /device:TPU:0, one launch (start us, length us, event | category | flops | bytes accessed | tf_op | source)
XLA Modules:
  0.0 715.8 jit_solution(5357680943049535149)
XLA Ops:
  12.0 5.1 collective-permute-start.2
  18.6 3.8 collective-permute-done
  23.9 3.8 collective-permute-start.5
  27.7 4.1 collective-permute-done.3
  31.8 6.3 collective-permute-done.4
  45.5 4.1 collective-permute-done.8
  49.7 53.4 %all-gather.5.cloned.1.call-done = bf16[5120,1024]{1,0:T(8,128)(2,1)} async-done(((bf16[160,1024]{1,0:T(8,128)(2,1)}), bf16[5120,1024]{1,0:T(8,128)(2,1)}) %all-gather.5.cloned.1.call-update) | async-done | bytes 10485776 | tf_op jit(solution)/shard_map/all_gather | solution.py:452
  105.9 5.3 fusion.142
  111.6 4.5 add_convert_fusion.5.normed_ref
  116.2 8.5 %project.1 = bf16[8,3,384,128]{3,2,1,0:T(8,128)(2,1)} custom-call(bf16[384,1024]{1,0:T(8,128)(2,1)S(1)} %add_convert_fusion.5.normed_ref, bf16[32,160,1024]{2,1,0:T(8,128)(2,1)S(1)} %bitcast.231, f32[384,128]{1,0:T(8,128)S(1)} %get-tuple-element.140.cos_ref, f32[384,128]{1,0:T(8,128)S(1)} %get-tuple-element.139.sin_ref), custom_call_target="tpu_custom_call" | custom-call | flops 2415919104 | bytes 8388608 | tf_op jit(solution)/shard_map/project/pallas_call | solution.py:260
  124.7 4.5 all-to-all-start
  139.6 7.1 fusion.15
  149.5 25.3 %collective-permute-done.13 = f32[8,512]{1,0:T(8,128)S(1)} collective-permute-done((f32[8,512]{1,0:T(8,128)S(1)}, f32[8,512]{1,0:T(8,128)S(1)}, u32[]{:S(2)}, u32[]{:S(2)}) %collective-permute-start.13) | collective-permute-done | bytes 16416 | tf_op jit(solution)/shard_map/ppermute | solution.py:293
  176.3 44.0 %attend.1 = (bf16[3072,128]{1,0:T(8,128)(2,1)}, f32[3072,128]{1,0:T(8,128)}) custom-call(s32[3]{0:T(128)} %bitcast.300, bf16[8,3,384,128]{3,2,1,0:T(8,128)(2,1)} %all-to-all-done.qkv_ref), custom_call_target="tpu_custom_call" | custom-call | flops 48318382080 | bytes 4718592 | tf_op jit(solution)/shard_map/attend/pallas_call | solution.py:115
  230.9 7.8 %all-to-all-done.1 = bf16[8,384,128]{1,2,0:T(8,128)(2,1)S(1)} async-done(((bf16[8,384,128]{1,2,0:T(8,128)(2,1)}), bf16[8,384,128]{1,2,0:T(8,128)(2,1)S(1)}, u32[]{:S(2)}, u32[]{:S(2)}) %all-to-all-start.1) | async-done | bytes 786464 | tf_op jit(solution)/shard_map/all_to_all | solution.py:533
  238.9 6.1 fusion.136
  249.9 9.6 %fusion.135 = (bf16[32,128,1024]{2,1,0:T(8,128)(2,1)}, bf16[32,128,1024]{2,1,0:T(8,128)(2,1)S(1)}) fusion(bf16[32,288,1024]{2,1,0:T(8,128)(2,1)} %bitcast.235), kind=kLoop, calls=%fused_computation.343 | loop fusion | bytes 33554432 | tf_op jit(solution)/shard_map/slice | solution.py:466
  259.4 7.9 %copy.37 = bf16[32,32,4,1024]{3,2,1,0:T(4,128)(2,1)} copy(bf16[32,32,4,1024]{3,1,2,0:T(8,128)(2,1)S(1)} %bitcast.233) | data formatting | bytes 16777216 | tf_op jit(solution)/shard_map/transpose | solution.py:471
  267.3 12.3 %copy.41 = bf16[128,8,4,1024]{3,1,2,0:T(8,128)(2,1)} copy(bf16[128,8,4,1024]{3,2,1,0:T(4,128)(2,1)} %bitcast.232) | data formatting | bytes 16777216
  284.3 6.6 multiply_convert_fusion
  290.9 15.2 %convert_reduce_fusion = (f32[4096]{0:T(1024)S(1)}, bf16[384,4096]{1,0:T(8,128)(2,1)}) fusion(f32[384,4096]{1,0:T(8,128)} %get-tuple-element.148, f32[4096]{0:T(1024)S(1)} %bitcast.297, bf16[4096,1024]{1,0:T(8,128)(2,1)} %bitcast.240, bf16[1,384,1024]{2,1,0:T(8,128)(2,1)S(1)} %copy-done.18, f32[384]{0:T(512)S(1)} %copy-done.75), kind=kOutput, calls=%fused_computation.10 | convolution fusion | flops 3257004032 | bytes 18646528 | tf_op jit(solution)/shard_map/dot_general | solution.py:288
  306.1 5.8 fusion.131
  319.1 4.4 fusion.31
  324.5 4.2 all-to-all-start.2
  336.2 4.4 collective-permute-done.50
  353.1 65.3 %attend_back.1 = bf16[8,3,384,128]{3,2,1,0:T(8,128)(2,1)} custom-call(s32[3]{0:T(128)} %bitcast.301, bf16[8,3,384,128]{3,2,1,0:T(8,128)(2,1)} %all-to-all-done.qkv_ref, bf16[3072,128]{1,0:T(8,128)(2,1)} %bitcast.47.da_ref, bf16[3072,128]{1,0:T(8,128)(2,1)} %get-tuple-element.14.out_ref, f32[3072,128]{1,0:T(8,128)} %get-tuple-element.15.lse_ref, ...), custom_call_target="tpu_custom_call" | custom-call | flops 77309411328 | bytes 9437184 | tf_op jit(solution)/shard_map/attend_back/pallas_call | solution.py:224
  418.4 4.4 all-to-all-start.3
  430.5 26.3 %collective-permute-done.38 = bf16[4,32,1024]{2,1,0:T(8,128)(2,1)S(1)} collective-permute-done((bf16[4,32,1024]{2,1,0:T(8,128)(2,1)S(1)}, bf16[4,32,1024]{2,1,0:T(8,128)(2,1)S(1)}, u32[]{:S(2)}, u32[]{:S(2)}) %collective-permute-start.38) | collective-permute-done | bytes 262176 | tf_op jit(solution)/shard_map/ppermute | solution.py:293
  461.9 10.7 %pad_maximum_fusion.5 = bf16[768,2048]{1,0:T(8,128)(2,1)S(1)} fusion(bf16[384,2048]{1,0:T(8,128)(2,1)} %collective-permute-done.55, bf16[384,512]{1,0:T(8,128)(2,1)S(1)} %copy-done.14, bf16[384,512]{1,0:T(8,128)(2,1)S(1)} %copy-done.15, bf16[384,512]{1,0:T(8,128)(2,1)S(1)} %copy-done.16, bf16[384,512]{1,0:T(8,128)(2,1)S(1)} %copy-done.13), kind=kLoop, calls=%fused_computation.38 | loop fusion | flops 15728640 | bytes 6291456 | tf_op jit(solution)/shard_map/concatenate | solution.py:321
  478.5 4.7 copy.39
  498.0 27.3 %collective-permute-done.16 = f32[3,4096]{1,0:T(4,128)S(1)} collective-permute-done((f32[3,4096]{1,0:T(4,128)S(1)}, f32[3,4096]{1,0:T(4,128)S(1)}, u32[]{:S(2)}, u32[]{:S(2)}) %collective-permute-start.16) | collective-permute-done | bytes 49184 | tf_op jit(solution)/shard_map/ppermute | solution.py:293
  532.2 4.4 collective-permute-done.18
  536.7 5.8 collective-permute-done.19
  542.7 4.2 collective-permute-done.20
  556.9 5.1 convolution_convert_fusion
  565.9 11.1 %collective-permute-done.58 = bf16[4,128,1024]{2,1,0:T(8,128)(2,1)S(1)} collective-permute-done((bf16[4,128,1024]{2,1,0:T(8,128)(2,1)S(1)}, bf16[4,128,1024]{2,1,0:T(8,128)(2,1)S(1)}, u32[]{:S(2)}, u32[]{:S(2)}) %collective-permute-start.58) | collective-permute-done | bytes 1048608 | tf_op jit(solution)/shard_map/ppermute | solution.py:293
  578.8 3.8 collective-permute-start.61
  582.6 17.0 %collective-permute-done.23 = bf16[512,1024]{1,0:T(8,128)(2,1)} collective-permute-done((bf16[512,1024]{1,0:T(8,128)(2,1)}, bf16[512,1024]{1,0:T(8,128)(2,1)}, u32[]{:S(2)}, u32[]{:S(2)}) %collective-permute-start.23) | collective-permute-done | bytes 1048608 | tf_op jit(solution)/shard_map/ppermute | solution.py:293
  603.1 6.3 collective-permute-done.60
  610.4 4.0 convolution_convert_fusion.1
  616.2 3.8 collective-permute-start.25
  622.8 17.4 %collective-permute-done.44 = bf16[256,4096]{1,0:T(8,128)(2,1)} collective-permute-done((bf16[256,4096]{1,0:T(8,128)(2,1)}, bf16[256,4096]{1,0:T(8,128)(2,1)}, u32[]{:S(2)}, u32[]{:S(2)}) %collective-permute-start.44) | collective-permute-done | bytes 2097184 | tf_op jit(solution)/shard_map/ppermute | solution.py:293
  640.2 4.4 fusion.7
  647.5 3.9 fusion.8
  652.3 15.5 %collective-permute-done.45 = bf16[4,32,4096]{2,1,0:T(8,128)(2,1)S(1)} collective-permute-done((bf16[4,32,4096]{2,1,0:T(8,128)(2,1)S(1)}, bf16[4,32,4096]{2,1,0:T(8,128)(2,1)S(1)}, u32[]{:S(2)}, u32[]{:S(2)}) %collective-permute-start.45) | collective-permute-done | bytes 1048608 | tf_op jit(solution)/shard_map/ppermute | solution.py:293
  679.3 12.0 %collective-permute-start.33 = (bf16[32,3072]{1,0:T(8,128)(2,1)S(1)}, bf16[32,3072]{1,0:T(8,128)(2,1)S(1)}, u32[]{:S(2)}, u32[]{:S(2)}) collective-permute-start(bf16[32,3072]{1,0:T(8,128)(2,1)S(1)} %get-tuple-element.95), channel_id=1, source_target_pairs={{0,2},{1,3},{2,0},{3,1},{4,6},{5,7},{6,4},{7,5},{8,10},{9,11},{10,... | collective-permute-start | bytes 589832 | tf_op jit(solution)/shard_map/ppermute | solution.py:298
  691.4 9.6 %collective-permute-done.47 = bf16[32,4096]{1,0:T(8,128)(2,1)S(1)} collective-permute-done((bf16[32,4096]{1,0:T(8,128)(2,1)S(1)}, bf16[32,4096]{1,0:T(8,128)(2,1)S(1)}, u32[]{:S(2)}, u32[]{:S(2)}) %collective-permute-start.47) | collective-permute-done | bytes 262176 | tf_op jit(solution)/shard_map/ppermute | solution.py:298
  701.9 6.0 collective-permute-done.33
  (445 shorter events, 162.8 us)
Async XLA Ops:
  7.2 95.9 %all-gather.5.cloned.1.call-start = ((), (), s32[]{:S(2)}) async-start(), calls=%async_computation.4 | async-start | bytes 10813440 | tf_op jit(solution)/shard_map/all_gather | solution.py:452
  10.0 238.1 %all-gather.7.cloned.1.call-start = ((), (), s32[]{:S(2)}) async-start(), calls=%async_computation.5 | async-start | bytes 19464192 | tf_op jit(solution)/shard_map/all_gather | solution.py:453
  12.0 10.5 %collective-permute-start.2 = (s32[3]{0:T(128)S(1)}, s32[3]{0:T(128)S(1)}, u32[]{:S(2)}, u32[]{:S(2)}) collective-permute-start(s32[3]{0:T(128)S(1)} %bitcast.304), channel_id=1, source_target_pairs={{0,3},{1,0},{2,1},{3,2},{4,7},{5,4},{6,5},{7,6},{8,11},{9,8},{10,9... | collective-permute-start | bytes 44 | tf_op jit(solution)/shard_map/ppermute | solution.py:298
  27.7 10.5 %collective-permute-start.4 = (f32[3,4096]{1,0:T(4,128)S(1)}, f32[3,4096]{1,0:T(4,128)S(1)}, u32[]{:S(2)}, u32[]{:S(2)}) collective-permute-start(f32[3,4096]{1,0:T(4,128)S(1)} %get-tuple-element.116), channel_id=1, source_target_pairs={{0,2},{1,3},{2,0},{3,1},{4,6},{5,7},{6,4},{7,5},{8,10},{9,11},{10,... | collective-permute-start | bytes 147464 | tf_op jit(solution)/shard_map/ppermute | solution.py:298
  124.7 51.6 %all-to-all-start = ((bf16[8,3,384,128]{3,2,1,0:T(8,128)(2,1)}), bf16[8,3,384,128]{3,2,1,0:T(8,128)(2,1)}, u32[]{:S(2)}, u32[]{:S(2)}) async-start(bf16[8,3,384,128]{3,2,1,0:T(8,128)(2,1)} %project.1), calls=%async_computation | async-start | bytes 4718592 | tf_op jit(solution)/shard_map/all_to_all | solution.py:531
  129.2 9.7 %collective-permute-start.10 = (f32[128]{0:T(128)S(1)}, f32[128]{0:T(128)S(1)}, u32[]{:S(2)}, u32[]{:S(2)}) collective-permute-start(f32[128]{0:T(128)S(1)} %get-tuple-element.141), channel_id=1, source_target_pairs={{0,2},{1,3},{2,0},{3,1},{4,6},{5,7},{6,4},{7,5},{8,10},{9,11},{10,... | collective-permute-start | bytes 1544 | tf_op jit(solution)/shard_map/ppermute | solution.py:298
  138.6 88.2 %collective-permute-start.21 = (bf16[384,1024]{1,0:T(8,128)(2,1)}, bf16[384,1024]{1,0:T(8,128)(2,1)}, u32[]{:S(2)}, u32[]{:S(2)}) collective-permute-start(bf16[384,1024]{1,0:T(8,128)(2,1)} %pad_maximum_fusion.20), channel_id=1, source_target_pairs={{0,4},{4,0},{8,12},{12,8},{16,20},{20,16},{24,28},{28,24},{1,5},{5... | collective-permute-start | bytes 2359304 | tf_op jit(solution)/shard_map/ppermute | solution.py:293
  147.0 27.8 %collective-permute-start.13 = (f32[8,512]{1,0:T(8,128)S(1)}, f32[8,512]{1,0:T(8,128)S(1)}, u32[]{:S(2)}, u32[]{:S(2)}) collective-permute-start(f32[8,512]{1,0:T(8,128)S(1)} %add.716), channel_id=1, source_target_pairs={{0,8},{4,12},{8,0},{12,4},{16,24},{20,28},{24,16},{28,20},{1,9},{5... | collective-permute-start | bytes 49160 | tf_op jit(solution)/shard_map/ppermute | solution.py:293
  174.8 51.4 %collective-permute-start.14 = (f32[8,512]{1,0:T(8,128)S(1)}, f32[8,512]{1,0:T(8,128)S(1)}, u32[]{:S(2)}, u32[]{:S(2)}) collective-permute-start(f32[8,512]{1,0:T(8,128)S(1)} %add.717), channel_id=1, source_target_pairs={{0,16},{4,20},{8,24},{12,28},{16,0},{20,4},{24,8},{28,12},{1,17},{... | collective-permute-start | bytes 49160 | tf_op jit(solution)/shard_map/ppermute | solution.py:293
  222.6 16.1 %all-to-all-start.1 = ((bf16[8,384,128]{1,2,0:T(8,128)(2,1)}), bf16[8,384,128]{1,2,0:T(8,128)(2,1)S(1)}, u32[]{:S(2)}, u32[]{:S(2)}) async-start(bf16[8,384,128]{1,2,0:T(8,128)(2,1)} %copy.36), calls=%async_computation.1 | async-start | bytes 1572864 | tf_op jit(solution)/shard_map/all_to_all | solution.py:533
  230.4 14.7 %collective-permute-start.28 = (bf16[384,512]{1,0:T(8,128)(2,1)S(1)}, bf16[384,512]{1,0:T(8,128)(2,1)}, u32[]{:S(2)}, u32[]{:S(2)}) collective-permute-start(bf16[384,512]{1,0:T(8,128)(2,1)S(1)} %pad_maximum_fusion.24), channel_id=1, source_target_pairs={{0,4},{4,0},{8,12},{12,8},{16,20},{20,16},{24,28},{28,24},{1,5},{5... | collective-permute-start | bytes 1179656 | tf_op jit(solution)/shard_map/ppermute | solution.py:293
  318.7 30.1 %collective-permute-start.36 = (bf16[384,1024]{1,0:T(8,128)(2,1)}, bf16[384,1024]{1,0:T(8,128)(2,1)}, u32[]{:S(2)}, u32[]{:S(2)}) collective-permute-start(bf16[384,1024]{1,0:T(8,128)(2,1)} %get-tuple-element.28), channel_id=1, source_target_pairs={{0,4},{4,0},{8,12},{12,8},{16,20},{20,16},{24,28},{28,24},{1,5},{5... | collective-permute-start | bytes 2359304 | tf_op jit(solution)/shard_map/ppermute | solution.py:293
  324.5 28.6 %all-to-all-start.2 = ((bf16[8,384,128]{2,1,0:T(8,128)(2,1)}), bf16[8,384,128]{2,1,0:T(8,128)(2,1)}, u32[]{:S(2)}, u32[]{:S(2)}) async-start(bf16[8,384,128]{2,1,0:T(8,128)(2,1)} %bitcast.254), calls=%async_computation.2 | async-start | bytes 1572864 | tf_op jit(solution)/shard_map/all_to_all | solution.py:568
  336.2 124.6 %collective-permute-start.55 = (bf16[384,2048]{1,0:T(8,128)(2,1)}, bf16[384,2048]{1,0:T(8,128)(2,1)}, u32[]{:S(2)}, u32[]{:S(2)}) collective-permute-start(bf16[384,2048]{1,0:T(8,128)(2,1)} %pad_maximum_fusion.12), channel_id=1, source_target_pairs={{0,4},{4,0},{8,12},{12,8},{16,20},{20,16},{24,28},{28,24},{1,5},{5... | collective-permute-start | bytes 4718600 | tf_op jit(solution)/shard_map/ppermute | solution.py:293
  345.0 77.8 %collective-permute-start.52 = (f32[128]{0:T(128)}, f32[128]{0:T(128)}, u32[]{:S(2)}, u32[]{:S(2)}) collective-permute-start(f32[128]{0:T(128)} %get-tuple-element.128), channel_id=1, source_target_pairs={{0,1},{1,2},{2,3},{3,0},{4,5},{5,6},{6,7},{7,4},{8,9},{9,10},{10,1... | collective-permute-start | bytes 1544 | tf_op jit(solution)/shard_map/ppermute | solution.py:298
  346.3 76.9 %collective-permute-start.54 = (f32[128]{0:T(128)}, f32[128]{0:T(128)}, u32[]{:S(2)}, u32[]{:S(2)}) collective-permute-start(f32[128]{0:T(128)} %get-tuple-element.129), channel_id=1, source_target_pairs={{0,3},{1,0},{2,1},{3,2},{4,7},{5,4},{6,5},{7,6},{8,11},{9,8},{10,9... | collective-permute-start | bytes 1544 | tf_op jit(solution)/shard_map/ppermute | solution.py:298
  348.8 74.5 %collective-permute-start.53 = (f32[128]{0:T(128)}, f32[128]{0:T(128)}, u32[]{:S(2)}, u32[]{:S(2)}) collective-permute-start(f32[128]{0:T(128)} %get-tuple-element.130), channel_id=1, source_target_pairs={{0,2},{1,3},{2,0},{3,1},{4,6},{5,7},{6,4},{7,5},{8,10},{9,11},{10,... | collective-permute-start | bytes 1544 | tf_op jit(solution)/shard_map/ppermute | solution.py:298
  351.6 73.2 %collective-permute-start.37 = (bf16[256,1024]{1,0:T(8,128)(2,1)}, bf16[256,1024]{1,0:T(8,128)(2,1)}, u32[]{:S(2)}, u32[]{:S(2)}) collective-permute-start(bf16[256,1024]{1,0:T(8,128)(2,1)} %convolution_convert_fusion.6), channel_id=1, source_target_pairs={{0,16},{4,20},{8,24},{12,28},{16,0},{20,4},{24,8},{28,12},{1,17},{... | collective-permute-start | bytes 1572872 | tf_op jit(solution)/shard_map/ppermute | solution.py:293
  418.4 60.1 %all-to-all-start.3 = ((bf16[8,3,384,128]{3,2,1,0:T(8,128)(2,1)}), bf16[8,3,384,128]{3,2,1,0:T(8,128)(2,1)}, u32[]{:S(2)}, u32[]{:S(2)}) async-start(bf16[8,3,384,128]{3,2,1,0:T(8,128)(2,1)} %attend_back.1), calls=%async_computation.3 | async-start | bytes 4718592 | tf_op jit(solution)/shard_map/all_to_all | solution.py:572
  422.8 134.1 %collective-permute-start.43 = (bf16[384,4096]{1,0:T(8,128)(2,1)}, bf16[384,4096]{1,0:T(8,128)(2,1)}, u32[]{:S(2)}, u32[]{:S(2)}) collective-permute-start(bf16[384,4096]{1,0:T(8,128)(2,1)} %get-tuple-element.152), channel_id=1, source_target_pairs={{0,4},{4,0},{8,12},{12,8},{16,20},{20,16},{24,28},{28,24},{1,5},{5... | collective-permute-start | bytes 9437192 | tf_op jit(solution)/shard_map/ppermute | solution.py:293
  423.3 50.8 %collective-permute-start.56 = (bf16[384,1024]{1,0:T(8,128)(2,1)}, bf16[384,1024]{1,0:T(8,128)(2,1)S(1)}, u32[]{:S(2)}, u32[]{:S(2)}) collective-permute-start(bf16[384,1024]{1,0:T(8,128)(2,1)} %get-tuple-element.68), channel_id=1, source_target_pairs={{0,4},{4,0},{8,12},{12,8},{16,20},{20,16},{24,28},{28,24},{1,5},{5... | collective-permute-start | bytes 2359304 | tf_op jit(solution)/shard_map/ppermute | solution.py:293
  427.2 29.6 %collective-permute-start.38 = (bf16[4,32,1024]{2,1,0:T(8,128)(2,1)S(1)}, bf16[4,32,1024]{2,1,0:T(8,128)(2,1)S(1)}, u32[]{:S(2)}, u32[]{:S(2)}) collective-permute-start(bf16[4,32,1024]{2,1,0:T(8,128)(2,1)S(1)} %dynamic-slice_bitcast_fusion.10), channel_id=1, source_target_pairs={{0,8},{4,12},{8,0},{12,4},{16,24},{20,28},{24,16},{28,20},{1,9},{5... | collective-permute-start | bytes 786440 | tf_op jit(solution)/shard_map/ppermute | solution.py:293
  456.9 20.8 %collective-permute-start.39 = (bf16[32,1024]{1,0:T(8,128)(2,1)S(1)}, bf16[32,1024]{1,0:T(8,128)(2,1)S(1)}, u32[]{:S(2)}, u32[]{:S(2)}) collective-permute-start(bf16[32,1024]{1,0:T(8,128)(2,1)S(1)} %get-tuple-element.111), channel_id=1, source_target_pairs={{0,1},{1,2},{2,3},{3,0},{4,5},{5,6},{6,7},{7,4},{8,9},{9,10},{10,1... | collective-permute-start | bytes 196616 | tf_op jit(solution)/shard_map/ppermute | solution.py:298
  457.8 20.0 %collective-permute-start.41 = (bf16[32,1024]{1,0:T(8,128)(2,1)S(1)}, bf16[32,1024]{1,0:T(8,128)(2,1)S(1)}, u32[]{:S(2)}, u32[]{:S(2)}) collective-permute-start(bf16[32,1024]{1,0:T(8,128)(2,1)S(1)} %get-tuple-element.112), channel_id=1, source_target_pairs={{0,3},{1,0},{2,1},{3,2},{4,7},{5,4},{6,5},{7,6},{8,11},{9,8},{10,9... | collective-permute-start | bytes 196616 | tf_op jit(solution)/shard_map/ppermute | solution.py:298
  460.8 17.0 %collective-permute-start.40 = (bf16[32,1024]{1,0:T(8,128)(2,1)S(1)}, bf16[32,1024]{1,0:T(8,128)(2,1)S(1)}, u32[]{:S(2)}, u32[]{:S(2)}) collective-permute-start(bf16[32,1024]{1,0:T(8,128)(2,1)S(1)} %get-tuple-element.113), channel_id=1, source_target_pairs={{0,2},{1,3},{2,0},{3,1},{4,6},{5,7},{6,4},{7,5},{8,10},{9,11},{10,... | collective-permute-start | bytes 196616 | tf_op jit(solution)/shard_map/ppermute | solution.py:298
  477.3 69.7 %collective-permute-start.57 = (bf16[1024,1024]{1,0:T(8,128)(2,1)}, bf16[1024,1024]{1,0:T(8,128)(2,1)}, u32[]{:S(2)}, u32[]{:S(2)}) collective-permute-start(bf16[1024,1024]{1,0:T(8,128)(2,1)} %convolution_convert_fusion.3), channel_id=1, source_target_pairs={{0,8},{4,12},{8,0},{12,4},{16,24},{20,28},{24,16},{28,20},{1,9},{5... | collective-permute-start | bytes 6291464 | tf_op jit(solution)/shard_map/ppermute | solution.py:293
  494.6 30.7 %collective-permute-start.16 = (f32[3,4096]{1,0:T(4,128)S(1)}, f32[3,4096]{1,0:T(4,128)S(1)}, u32[]{:S(2)}, u32[]{:S(2)}) collective-permute-start(f32[3,4096]{1,0:T(4,128)S(1)} %fusion.130), channel_id=1, source_target_pairs={{0,8},{4,12},{8,0},{12,4},{16,24},{20,28},{24,16},{28,20},{1,9},{5... | collective-permute-start | bytes 147464 | tf_op jit(solution)/shard_map/ppermute | solution.py:293
  529.8 22.0 %collective-permute-start.22 = (bf16[384,1024]{1,0:T(8,128)(2,1)}, bf16[384,1024]{1,0:T(8,128)(2,1)}, u32[]{:S(2)}, u32[]{:S(2)}) collective-permute-start(bf16[384,1024]{1,0:T(8,128)(2,1)} %add_convert_fusion.2), channel_id=1, source_target_pairs={{0,4},{4,0},{8,12},{12,8},{16,20},{20,16},{24,28},{28,24},{1,5},{5... | collective-permute-start | bytes 2359304 | tf_op jit(solution)/shard_map/ppermute | solution.py:293
  529.9 80.4 %collective-permute-start.29 = (bf16[384,3072]{0,1:T(8,128)(2,1)}, bf16[384,3072]{0,1:T(8,128)(2,1)}, u32[]{:S(2)}, u32[]{:S(2)}) collective-permute-start(bf16[384,3072]{0,1:T(8,128)(2,1)} %bitcast.49), channel_id=1, source_target_pairs={{0,4},{4,0},{8,12},{12,8},{16,20},{20,16},{24,28},{28,24},{1,5},{5... | collective-permute-start | bytes 7077896 | tf_op jit(solution)/shard_map/ppermute | solution.py:293
  550.9 26.2 %collective-permute-start.58 = (bf16[4,128,1024]{2,1,0:T(8,128)(2,1)S(1)}, bf16[4,128,1024]{2,1,0:T(8,128)(2,1)S(1)}, u32[]{:S(2)}, u32[]{:S(2)}) collective-permute-start(bf16[4,128,1024]{2,1,0:T(8,128)(2,1)S(1)} %dynamic-slice_bitcast_fusion), channel_id=1, source_target_pairs={{0,16},{4,20},{8,24},{12,28},{16,0},{20,4},{24,8},{28,12},{1,17},{... | collective-permute-start | bytes 3145736 | tf_op jit(solution)/shard_map/ppermute | solution.py:293
  556.0 43.6 %collective-permute-start.23 = (bf16[512,1024]{1,0:T(8,128)(2,1)}, bf16[512,1024]{1,0:T(8,128)(2,1)}, u32[]{:S(2)}, u32[]{:S(2)}) collective-permute-start(bf16[512,1024]{1,0:T(8,128)(2,1)} %convolution_convert_fusion.4), channel_id=1, source_target_pairs={{0,16},{4,20},{8,24},{12,28},{16,0},{20,4},{24,8},{28,12},{1,17},{... | collective-permute-start | bytes 3145736 | tf_op jit(solution)/shard_map/ppermute | solution.py:293
  562.0 78.2 %collective-permute-start.44 = (bf16[256,4096]{1,0:T(8,128)(2,1)}, bf16[256,4096]{1,0:T(8,128)(2,1)}, u32[]{:S(2)}, u32[]{:S(2)}) collective-permute-start(bf16[256,4096]{1,0:T(8,128)(2,1)} %convolution_convert_fusion), channel_id=1, source_target_pairs={{0,16},{4,20},{8,24},{12,28},{16,0},{20,4},{24,8},{28,12},{1,17},{... | collective-permute-start | bytes 6291464 | tf_op jit(solution)/shard_map/ppermute | solution.py:293
  578.7 23.7 %collective-permute-start.59 = (bf16[128,1024]{1,0:T(8,128)(2,1)S(1)}, bf16[128,1024]{1,0:T(8,128)(2,1)S(1)}, u32[]{:S(2)}, u32[]{:S(2)}) collective-permute-start(bf16[128,1024]{1,0:T(8,128)(2,1)S(1)} %get-tuple-element.62), channel_id=1, source_target_pairs={{0,1},{1,2},{2,3},{3,0},{4,5},{5,6},{6,7},{7,4},{8,9},{9,10},{10,1... | collective-permute-start | bytes 786440 | tf_op jit(solution)/shard_map/ppermute | solution.py:298
  578.8 24.3 %collective-permute-start.61 = (bf16[128,1024]{1,0:T(8,128)(2,1)S(1)}, bf16[128,1024]{1,0:T(8,128)(2,1)S(1)}, u32[]{:S(2)}, u32[]{:S(2)}) collective-permute-start(bf16[128,1024]{1,0:T(8,128)(2,1)S(1)} %get-tuple-element.63), channel_id=1, source_target_pairs={{0,3},{1,0},{2,1},{3,2},{4,7},{5,4},{6,5},{7,6},{8,11},{9,8},{10,9... | collective-permute-start | bytes 786440 | tf_op jit(solution)/shard_map/ppermute | solution.py:298
  599.6 9.8 %collective-permute-start.60 = (bf16[128,1024]{1,0:T(8,128)(2,1)S(1)}, bf16[128,1024]{1,0:T(8,128)(2,1)S(1)}, u32[]{:S(2)}, u32[]{:S(2)}) collective-permute-start(bf16[128,1024]{1,0:T(8,128)(2,1)S(1)} %get-tuple-element.64), channel_id=1, source_target_pairs={{0,2},{1,3},{2,0},{3,1},{4,6},{5,7},{6,4},{7,5},{8,10},{9,11},{10,... | collective-permute-start | bytes 786440 | tf_op jit(solution)/shard_map/ppermute | solution.py:298
  602.4 13.6 %collective-permute-start.24 = (bf16[4,64,1024]{2,1,0:T(8,128)(2,1)S(1)}, bf16[4,64,1024]{2,1,0:T(8,128)(2,1)S(1)}, u32[]{:S(2)}, u32[]{:S(2)}) collective-permute-start(bf16[4,64,1024]{2,1,0:T(8,128)(2,1)S(1)} %dynamic-slice_bitcast_fusion.3), channel_id=1, source_target_pairs={{0,8},{4,12},{8,0},{12,4},{16,24},{20,28},{24,16},{28,20},{1,9},{5... | collective-permute-start | bytes 1572872 | tf_op jit(solution)/shard_map/ppermute | solution.py:293
  614.4 33.1 %collective-permute-start.30 = (bf16[256,3072]{1,0:T(8,128)(2,1)S(1)}, bf16[256,3072]{1,0:T(8,128)(2,1)S(1)}, u32[]{:S(2)}, u32[]{:S(2)}) collective-permute-start(bf16[256,3072]{1,0:T(8,128)(2,1)S(1)} %convolution_convert_fusion.1), channel_id=1, source_target_pairs={{0,8},{4,12},{8,0},{12,4},{16,24},{20,28},{24,16},{28,20},{1,9},{5... | collective-permute-start | bytes 4718600 | tf_op jit(solution)/shard_map/ppermute | solution.py:293
  616.2 29.1 %collective-permute-start.25 = (bf16[64,1024]{1,0:T(8,128)(2,1)S(1)}, bf16[64,1024]{1,0:T(8,128)(2,1)S(1)}, u32[]{:S(2)}, u32[]{:S(2)}) collective-permute-start(bf16[64,1024]{1,0:T(8,128)(2,1)S(1)} %get-tuple-element.108), channel_id=1, source_target_pairs={{0,1},{1,2},{2,3},{3,0},{4,5},{5,6},{6,7},{7,4},{8,9},{9,10},{10,1... | collective-permute-start | bytes 393224 | tf_op jit(solution)/shard_map/ppermute | solution.py:298
  620.0 25.4 %collective-permute-start.27 = (bf16[64,1024]{1,0:T(8,128)(2,1)S(1)}, bf16[64,1024]{1,0:T(8,128)(2,1)S(1)}, u32[]{:S(2)}, u32[]{:S(2)}) collective-permute-start(bf16[64,1024]{1,0:T(8,128)(2,1)S(1)} %get-tuple-element.109), channel_id=1, source_target_pairs={{0,3},{1,0},{2,1},{3,2},{4,7},{5,4},{6,5},{7,6},{8,11},{9,8},{10,9... | collective-permute-start | bytes 393224 | tf_op jit(solution)/shard_map/ppermute | solution.py:298
  620.3 25.1 %collective-permute-start.26 = (bf16[64,1024]{1,0:T(8,128)(2,1)S(1)}, bf16[64,1024]{1,0:T(8,128)(2,1)S(1)}, u32[]{:S(2)}, u32[]{:S(2)}) collective-permute-start(bf16[64,1024]{1,0:T(8,128)(2,1)S(1)} %get-tuple-element.110), channel_id=1, source_target_pairs={{0,2},{1,3},{2,0},{3,1},{4,6},{5,7},{6,4},{7,5},{8,10},{9,11},{10,... | collective-permute-start | bytes 393224 | tf_op jit(solution)/shard_map/ppermute | solution.py:298
  644.7 23.1 %collective-permute-start.45 = (bf16[4,32,4096]{2,1,0:T(8,128)(2,1)S(1)}, bf16[4,32,4096]{2,1,0:T(8,128)(2,1)S(1)}, u32[]{:S(2)}, u32[]{:S(2)}) collective-permute-start(bf16[4,32,4096]{2,1,0:T(8,128)(2,1)S(1)} %dynamic-slice_bitcast_fusion.1), channel_id=1, source_target_pairs={{0,8},{4,12},{8,0},{12,4},{16,24},{20,28},{24,16},{28,20},{1,9},{5... | collective-permute-start | bytes 3145736 | tf_op jit(solution)/shard_map/ppermute | solution.py:293
  651.5 20.6 %collective-permute-start.31 = (bf16[4,32,3072]{2,1,0:T(8,128)(2,1)S(1)}, bf16[4,32,3072]{2,1,0:T(8,128)(2,1)S(1)}, u32[]{:S(2)}, u32[]{:S(2)}) collective-permute-start(bf16[4,32,3072]{2,1,0:T(8,128)(2,1)S(1)} %dynamic-slice_bitcast_fusion.2), channel_id=1, source_target_pairs={{0,16},{4,20},{8,24},{12,28},{16,0},{20,4},{24,8},{28,12},{1,17},{... | collective-permute-start | bytes 2359304 | tf_op jit(solution)/shard_map/ppermute | solution.py:293
  668.1 11.2 %collective-permute-start.46 = (bf16[32,4096]{1,0:T(8,128)(2,1)S(1)}, bf16[32,4096]{1,0:T(8,128)(2,1)S(1)}, u32[]{:S(2)}, u32[]{:S(2)}) collective-permute-start(bf16[32,4096]{1,0:T(8,128)(2,1)S(1)} %get-tuple-element.65), channel_id=1, source_target_pairs={{0,1},{1,2},{2,3},{3,0},{4,5},{5,6},{6,7},{7,4},{8,9},{9,10},{10,1... | collective-permute-start | bytes 786440 | tf_op jit(solution)/shard_map/ppermute | solution.py:298
  668.4 23.0 %collective-permute-start.48 = (bf16[32,4096]{1,0:T(8,128)(2,1)S(1)}, bf16[32,4096]{1,0:T(8,128)(2,1)S(1)}, u32[]{:S(2)}, u32[]{:S(2)}) collective-permute-start(bf16[32,4096]{1,0:T(8,128)(2,1)S(1)} %get-tuple-element.66), channel_id=1, source_target_pairs={{0,3},{1,0},{2,1},{3,2},{4,7},{5,4},{6,5},{7,6},{8,11},{9,8},{10,9... | collective-permute-start | bytes 786440 | tf_op jit(solution)/shard_map/ppermute | solution.py:298
  672.0 29.0 %collective-permute-start.47 = (bf16[32,4096]{1,0:T(8,128)(2,1)S(1)}, bf16[32,4096]{1,0:T(8,128)(2,1)S(1)}, u32[]{:S(2)}, u32[]{:S(2)}) collective-permute-start(bf16[32,4096]{1,0:T(8,128)(2,1)S(1)} %get-tuple-element.67), channel_id=1, source_target_pairs={{0,2},{1,3},{2,0},{3,1},{4,6},{5,7},{6,4},{7,5},{8,10},{9,11},{10,... | collective-permute-start | bytes 786440 | tf_op jit(solution)/shard_map/ppermute | solution.py:298
  672.3 29.6 %collective-permute-start.32 = (bf16[32,3072]{1,0:T(8,128)(2,1)S(1)}, bf16[32,3072]{1,0:T(8,128)(2,1)S(1)}, u32[]{:S(2)}, u32[]{:S(2)}) collective-permute-start(bf16[32,3072]{1,0:T(8,128)(2,1)S(1)} %get-tuple-element.93), channel_id=1, source_target_pairs={{0,1},{1,2},{2,3},{3,0},{4,5},{5,6},{6,7},{7,4},{8,9},{9,10},{10,1... | collective-permute-start | bytes 589832 | tf_op jit(solution)/shard_map/ppermute | solution.py:298
  673.1 28.8 %collective-permute-start.34 = (bf16[32,3072]{1,0:T(8,128)(2,1)S(1)}, bf16[32,3072]{1,0:T(8,128)(2,1)S(1)}, u32[]{:S(2)}, u32[]{:S(2)}) collective-permute-start(bf16[32,3072]{1,0:T(8,128)(2,1)S(1)} %get-tuple-element.94), channel_id=1, source_target_pairs={{0,3},{1,0},{2,1},{3,2},{4,7},{5,4},{6,5},{7,6},{8,11},{9,8},{10,9... | collective-permute-start | bytes 589832 | tf_op jit(solution)/shard_map/ppermute | solution.py:298
  679.3 28.6 %collective-permute-start.33 = (bf16[32,3072]{1,0:T(8,128)(2,1)S(1)}, bf16[32,3072]{1,0:T(8,128)(2,1)S(1)}, u32[]{:S(2)}, u32[]{:S(2)}) collective-permute-start(bf16[32,3072]{1,0:T(8,128)(2,1)S(1)} %get-tuple-element.95), channel_id=1, source_target_pairs={{0,2},{1,3},{2,0},{3,1},{4,6},{5,7},{6,4},{7,5},{8,10},{9,11},{10,... | collective-permute-start | bytes 589832 | tf_op jit(solution)/shard_map/ppermute | solution.py:298
  (114 other events, 3065.8 us)
Sparse Core Ops, SparseCore 0:
  11.5 91.5 all-gather.4
  105.9 140.3 all-gather.6

commit v2 on v1

--- a/solution.py
+++ b/solution.py
@@ -13,6 +13,7 @@
 LANES = 128
 MASKED = -(2.0 ** 100)
 NORM_EPS = 1e-06
+VMEM = 60 * 1024 * 1024
 BOTH = ("seq", "batch")
 NT = (((1,), (1,)), ((), ()))
 NN = (((1,), (0,)), ((), ()))
@@ -122,7 +123,7 @@
         out_specs=(pl.BlockSpec(memory_space=pltpu.VMEM), pl.BlockSpec(memory_space=pltpu.VMEM)),
         scratch_shapes=[pltpu.VMEM((heads, frames, LANES), jnp.bfloat16)] * 3
         + [pltpu.VMEM((heads, bq, LANES), jnp.float32)] * 2,
-        compiler_params=pltpu.CompilerParams(vmem_limit_bytes=56 * 1024 * 1024),
+        compiler_params=pltpu.CompilerParams(vmem_limit_bytes=VMEM),
         cost_estimate=pl.CostEstimate(
             flops=40 * heads * frames * frames * HD, bytes_accessed=frames * LANES * 12,
             transcendentals=heads * frames * frames,
@@ -131,8 +132,10 @@
     )(ends, qkv)
 
 
-def bwd_kernel(ends_ref, qkv_ref, da_ref, out_ref, lse_ref, cos_ref, sin_ref, grad_ref,
-               q_s, k_s, v_s, d_s, gq_s, gk_s, gv_s, *, heads, utts, bq, bk):
+def bwd_kernel(
+    ends_ref, qkv_ref, da_ref, out_ref, lse_ref, cos_ref, sin_ref, *rest, heads, utts, bq, bk
+):
+    grad_ref, q_s, k_s, v_s, d_s, gq_s, gk_s, gv_s = rest[-8:]
     sources, _, rows, _ = qkv_ref.shape
     frames = sources * rows
 
@@ -216,7 +219,7 @@
     lax.fori_loop(0, sources, finish, 0)
 
 
-def attend_back(qkv, grad_out, out, lse, cos, sin, ends, heads, bq, bk):
+def attend_back(qkv, grad_out, out, lse, cos, sin, ends, heads, after, bq, bk):
     sources, _, rows, _ = qkv.shape
     frames = sources * rows
     utts = ends.shape[0]
@@ -224,129 +227,58 @@
     return pl.pallas_call(
         functools.partial(bwd_kernel, heads=heads, utts=utts, bq=bq, bk=bk),
         out_shape=jax.ShapeDtypeStruct(qkv.shape, jnp.bfloat16),
-        in_specs=[pl.BlockSpec(memory_space=pltpu.SMEM)] + [vmem] * 6,
+        in_specs=[pl.BlockSpec(memory_space=pltpu.SMEM)]
+        + [vmem] * 6
+        + [pl.BlockSpec(memory_space=pl.ANY)] * len(after),
         out_specs=vmem,
         scratch_shapes=[pltpu.VMEM((heads, frames, LANES), jnp.bfloat16)] * 4
         + [pltpu.VMEM((heads, frames, LANES), jnp.float32)] * 3,
-        compiler_params=pltpu.CompilerParams(vmem_limit_bytes=60 * 1024 * 1024),
+        compiler_params=pltpu.CompilerParams(vmem_limit_bytes=VMEM),
         cost_estimate=pl.CostEstimate(
             flops=64 * heads * frames * frames * HD, bytes_accessed=frames * LANES * 24,
             transcendentals=heads * frames * frames,
         ),
         name="attend_back",
-    )(ends, qkv, grad_out, out, lse, cos, sin)
-
-
-def project_kernel(normed_ref, weight_ref, cos_ref, sin_ref, out_ref):
-    part = pl.program_id(0)
-    weight = weight_ref[...].reshape(-1, weight_ref.shape[-1])
-    turned = mm(normed_ref[...], weight, NN)
-    lane = lax.broadcasted_iota(jnp.int32, (turned.shape[0], LANES), 1)
-    first = (lane % HD) < HD // 2
-    scale = jnp.where(part == 0, HD ** -0.5, 1.0)
-    for at in range(out_ref.shape[0]):
-        x = turned[:, at * LANES : (at + 1) * LANES]
-        partner = jnp.where(first, pltpu.roll(x, LANES - HD // 2, 1), pltpu.roll(x, HD // 2, 1))
-        rotated = (x * cos_ref[...] + partner * sin_ref[...]) * scale
-        out_ref[at, 0] = jnp.where(part == 2, x, rotated).astype(jnp.bfloat16)
-
-
-def project(normed, gathered, first_row, rows_each, cos, sin):
-    rows, width = normed.shape
-    devices = gathered.shape[0]
-    targets = width // LANES
-    each = 2
-    at = first_row // rows_each
+    )(ends, qkv, grad_out, out, lse, cos, sin, *after)
+
+
+def unjoin_kernel(grad_ref, weight_ref, *rest):
+    width = grad_ref.shape[1]
+    i = pl.program_id(0)
+    made = mm(grad_ref[...], weight_ref[...].reshape(-1, width), NT).astype(jnp.bfloat16)
+
+    @pl.when(i < 2)
+    def _():
+        rest[-2][...] = made
+
+    @pl.when(i >= 2)
+    def _():
+        rest[-1][...] = made
+
+
+def unjoin(grad, early, skip_each, after):
+    rows, width = grad.shape
+    devices = early.shape[0]
+    half = width // 2
     return pl.pallas_call(
-        project_kernel,
-        grid=(3, targets // each),
-        out_shape=jax.ShapeDtypeStruct((targets, 3, rows, LANES), jnp.bfloat16),
+        unjoin_kernel,
+        grid=(4,),
+        out_shape=[jax.ShapeDtypeStruct((rows, width), jnp.bfloat16)] * 2,
         in_specs=[
-            pl.BlockSpec((rows, width), lambda p, t: (0, 0)),
-            pl.BlockSpec((devices, rows_each, each * LANES), lambda p, t: (0, at + p, t)),
-            pl.BlockSpec((rows, LANES), lambda p, t: (0, 0)),
-            pl.BlockSpec((rows, LANES), lambda p, t: (0, 0)),
+            pl.BlockSpec((rows, width), lambda i: (0, 0)),
+            pl.BlockSpec((devices // 4, skip_each, width), lambda i: (i, 0, 0)),
+        ]
+        + [pl.BlockSpec(memory_space=pl.ANY)] * len(after),
+        out_specs=[
+            pl.BlockSpec((rows, half), lambda i: (0, jnp.minimum(i, 1))),
+            pl.BlockSpec((rows, half), lambda i: (0, jnp.maximum(i - 2, 0))),
         ],
-        out_specs=pl.BlockSpec((each, 1, rows, LANES), lambda p, t: (t, p, 0, 0)),
-        compiler_params=pltpu.CompilerParams(vmem_limit_bytes=40 * 1024 * 1024),
         cost_estimate=pl.CostEstimate(
-            flops=6 * rows * width * width, bytes_accessed=8 * width * width, transcendentals=0
-        ),
-        name="project",
-    )(normed, gathered, cos, sin)
-
-
-def rows_of(first_op, second_op):
-    return lax.dot_general(first_op, second_op, TN, preferred_element_type=jnp.float32)
-
-
-def times(first_op, second_op):
-    return lax.dot_general(first_op, second_op, NN, preferred_element_type=jnp.float32)
-
-
-def times_transpose(first_op, second_op):
-    return lax.dot_general(first_op, second_op, NT, preferred_element_type=jnp.float32)
-
-
-def swap(value, bit):
-    size = lax.axis_size("seq")
-    return lax.ppermute(value, "seq", [(i, i ^ bit) for i in range(size)])
-
-
-def ahead(value, step):
-    size = lax.axis_size("batch")
-    return lax.ppermute(value, "batch", [(i, (i + step) % size) for i in range(size)])
-
-
-def column_blocks(value, starts, width):
-    return jnp.concatenate(
-        [lax.dynamic_slice_in_dim(value, s, width, axis=1) for s in starts], axis=1
-    )
-
-
-def scatter_sum(first_op, second_op, bits):
-    seq = lax.axis_size("seq")
-    batch = lax.axis_size("batch")
-    me = lax.axis_index("seq")
-    rows_total = first_op.shape[1]
-    block = rows_total // seq
-    core = me & 1
-
-    def starts(keep_of):
-        return [(2 * i + keep_of(i)) * block for i in range(seq // 2)]
-
-    other = swap(column_blocks(first_op, starts(lambda i: 1 - core), block), 1)
-    second_other = swap(second_op, 1)
-    mine = column_blocks(first_op, starts(lambda i: core), block)
-    left = jnp.concatenate([mine, other], axis=0)
-    right = jnp.concatenate([second_op, second_other], axis=0)
-    high_bits = [seq >> (i + 1) for i in range(seq.bit_length() - 2)]
-    bit = bits[0]
-    shift = bit.bit_length() - 1
-    value = (me >> shift) & 1
-    chosen = [i for i in range(seq // 2) if not (2 * i) & bit]
-    keep_at = [(i + value * (bit // 2)) * block for i in chosen]
-    send_at = [(i + (1 - value) * (bit // 2)) * block for i in chosen]
-    sent = rows_of(column_blocks(left, send_at, block), right).astype(jnp.bfloat16)
-    came = swap(sent, bit)
-    total = rows_of(column_blocks(left, keep_at, block), right) + came.astype(jnp.float32)
-    left_bits = [b for b in high_bits if b != bit]
-    total = total.astype(jnp.bfloat16).reshape(
-        (2,) * len(left_bits) + (batch, block // batch, second_op.shape[1])
-    )
-    for bit in bits[1:]:
-        axis = left_bits.index(bit)
-        value = (me >> (bit.bit_length() - 1)) & 1
-        came = swap(lax.dynamic_index_in_dim(total, 1 - value, axis, keepdims=False), bit)
-        kept = lax.dynamic_index_in_dim(total, value, axis, keepdims=False)
-        total = (kept.astype(jnp.float32) + came.astype(jnp.float32)).astype(jnp.bfloat16)
-        left_bits.remove(bit)
-    place = lax.axis_index("batch")
-    result = lax.dynamic_index_in_dim(total, place, 0, keepdims=False).astype(jnp.float32)
-    for step in range(1, batch):
-        piece = lax.dynamic_index_in_dim(total, (place + step) % batch, 0, keepdims=False)
-        result = result + ahead(piece, step).astype(jnp.float32)
-    return result
+            flops=4 * rows * width * width, bytes_accessed=6 * width * width, transcendentals=0
+        ),
+        compiler_params=pltpu.CompilerParams(vmem_limit_bytes=VMEM),
+        name="unjoin",
+    )(grad, early, *after)
 
 
 def normalise(hidden):
@@ -363,21 +295,600 @@
     )
 
 
-def per_row(member, table):
-    total = member[:, 0:1] * table[0:1]
-    for u in range(1, table.shape[0]):
-        total = total + member[:, u : u + 1] * table[u : u + 1]
+def per_row(info, table, utts):
+    total = info[:, 0:1] * table[0:1]
+    for u in range(1, utts):
+        total = total + info[:, u : u + 1] * table[u : u + 1]
     return total
+
+
+def sums_by_utt(ref, at, info, value, utts):
+    width = value.shape[1]
+    for u in range(utts):
+        ref[u : u + 1, at : at + width] = jnp.sum(info[:, u : u + 1] * value, axis=0, keepdims=True)
 
 
 def gelu_parts(x):
     rate = math.sqrt(2.0 / math.pi)
-    inner = jnp.tanh(rate * (x + 0.044715 * x * x * x))
-    value = 0.5 * x * (1.0 + inner)
-    slope = 0.5 * (1.0 + inner) + 0.5 * x * (1.0 - inner * inner) * rate * (
-        1.0 + 3 * 0.044715 * x * x
-    )
+    square = x * x
+    inner = jnp.tanh(x * (rate + rate * 0.044715 * square))
+    half = 0.5 + 0.5 * inner
+    value = x * half
+    slope = half + 0.5 * x * (1.0 - inner * inner) * (rate + 3 * rate * 0.044715 * square)
     return value, slope
+
+
+def front_kernel(frames_ref, skip_ref, info_ref, mod_ref, wskip_ref, wqkv_ref, cos_ref, sin_ref,
+                 *rest, utts, steps, parts):
+    stream_ref, out_ref, flipped_ref, normed_ref = rest[-4:]
+    i = pl.program_id(0)
+    width = stream_ref.shape[1]
+    weight = wskip_ref[...].reshape(-1, width)
+    depth = weight.shape[0]
+
+    for n in range(steps):
+        @pl.when(i == n)
+        def _(n=n):
+            at = n * depth
+            source = frames_ref if at < width else skip_ref
+            at = at % width
+            term = mm(source[:, at : at + depth], weight, NN)
+            stream_ref[...] = term if n == 0 else stream_ref[...] + term
+
+    @pl.when(i == steps - 1)
+    def _():
+        info = info_ref[...]
+        unit, _unused = normalise(stream_ref[...])
+        scale = per_row(info, 1.0 + mod_ref[:, :width], utts)
+        shift = per_row(info, mod_ref[:, width : 2 * width], utts)
+        normed = (unit * scale + shift).astype(jnp.bfloat16)
+        normed_ref[...] = normed
+        flipped_ref[...] = normed.T
+
+    @pl.when(i >= steps)
+    def _():
+        part = (i - steps) // parts
+        w = wqkv_ref[...].reshape(width, -1)
+        turned = mm(normed_ref[...], w, NN)
+        lane = lax.broadcasted_iota(jnp.int32, (turned.shape[0], LANES), 1)
+        first = (lane % HD) < HD // 2
+        scale = jnp.where(part == 0, HD ** -0.5, 1.0)
+        for at in range(out_ref.shape[0]):
+            x = turned[:, at * LANES : (at + 1) * LANES]
+            partner = jnp.where(first, pltpu.roll(x, LANES - HD // 2, 1), pltpu.roll(x, HD // 2, 1))
+            rotated = (x * cos_ref[...] + partner * sin_ref[...]) * scale
+            out_ref[at, 0] = jnp.where(part == 2, x, rotated).astype(jnp.bfloat16)
+
+
+def front(frames, skip, info, modulation, early, skip_each, qkv_each, cos, sin, utts, after):
+    rows, width = frames.shape
+    devices = early.shape[0]
+    steps, parts = 4, 4
+    targets = width // LANES
+    each = targets // parts
+    first = skip_each // qkv_each
+
+    def fixed(*shape):
+        return pl.BlockSpec(shape, lambda i: (0,) * len(shape))
+
+    def later(i):
+        return jnp.maximum(i - steps, 0)
+
+    return pl.pallas_call(
+        functools.partial(front_kernel, utts=utts, steps=steps, parts=parts),
+        grid=(steps + 3 * parts,),
+        out_shape=(
+            jax.ShapeDtypeStruct((rows, width), jnp.float32),
+            jax.ShapeDtypeStruct((targets, 3, rows, LANES), jnp.bfloat16),
+            jax.ShapeDtypeStruct((width, rows), jnp.bfloat16),
+        ),
+        in_specs=[
+            fixed(rows, width),
+            fixed(rows, width),
+            fixed(rows, LANES),
+            fixed(utts, 4 * width),
+            pl.BlockSpec((devices // steps, skip_each, width), lambda i: (jnp.minimum(i, steps - 1), 0, 0)),
+            pl.BlockSpec(
+                (devices, qkv_each, each * LANES),
+                lambda i: (0, first + later(i) // parts, later(i) % parts),
+            ),
+            fixed(rows, LANES),
+            fixed(rows, LANES),
+        ]
+        + [pl.BlockSpec(memory_space=pl.ANY)] * len(after),
+        out_specs=(
+            fixed(rows, width),
+            pl.BlockSpec((each, 1, rows, LANES), lambda i: (later(i) % parts, later(i) // parts, 0, 0)),
+            fixed(width, rows),
+        ),
+        scratch_shapes=[pltpu.VMEM((rows, width), jnp.bfloat16)],
+        compiler_params=pltpu.CompilerParams(vmem_limit_bytes=VMEM),
+        cost_estimate=pl.CostEstimate(
+            flops=16 * rows * width * width, bytes_accessed=20 * width * width, transcendentals=0
+        ),
+        name="front",
+    )(frames, skip, info, modulation, early, early, cos, sin, *after)
+
+
+def middle_kernel(att_ref, stream_ref, info_ref, mod_ref, branch_ref, wout_ref, wup_ref, wdown_ref, bias_ref,
+                  result_ref, attended_ref, normed_ref, act_ref, pre_ref, grad_ref, grad_low_ref,
+                  back_ref, sums_ref, bup_ref,
+                  mid_s, unit_s, inv_s, total_s, gn_s, att_s, normed_s, *, utts, blocks):
+    b = pl.program_id(0)
+    rows, width = stream_ref.shape
+    groups = att_ref.shape[0]
+
+    @pl.when(b == 0)
+    def _():
+        for s in range(groups):
+            att_s[:, s * LANES : (s + 1) * LANES] = att_ref[s]
+            attended_ref[s * LANES : (s + 1) * LANES, :] = att_ref[s].T
+        mid = stream_ref[...] + mm(att_s[...], wout_ref[...].reshape(width, width), NN)
+        mid_s[...] = mid
+        unit, inverse = normalise(mid)
+        unit_s[...] = unit
+        inv_s[...] = jnp.broadcast_to(inverse, inv_s.shape)
+        info = info_ref[...]
+        scale = per_row(info, 1.0 + mod_ref[:, 2 * width : 3 * width], utts)
+        shift = per_row(info, mod_ref[:, 3 * width :], utts)
+        normed = (unit * scale + shift).astype(jnp.bfloat16)
+        normed_s[...] = normed
+        normed_ref[...] = normed.T
+
+    up = wup_ref[...].reshape(width, -1)
+    down = wdown_ref[...].reshape(-1, width)
+    value, slope = gelu_parts(mm(normed_s[...], up, NN) + bias_ref[...])
+    act = value.astype(jnp.bfloat16)
+    act_ref[...] = act.T
+    term = mm(act, down, NN)
+    pre = (mm(branch_ref[...], down, NT) * slope).astype(jnp.bfloat16)
+    pre_ref[...] = pre
+    bup_ref[...] = jnp.sum(pre.astype(jnp.float32), axis=0, keepdims=True)
+    grad_term = mm(pre, up, NT)
+
+    @pl.when(b == 0)
+    def _():
+        total_s[...] = mid_s[...] + term
+        gn_s[...] = grad_term
+
+    @pl.when(b > 0)
+    def _():
+        total_s[...] += term
+        gn_s[...] += grad_term
+
+    @pl.when(b == blocks - 1)
+    def _():
+        result_ref[...] = total_s[...].astype(jnp.bfloat16)
+        info = info_ref[...]
+        scale = per_row(info, 1.0 + mod_ref[:, 2 * width : 3 * width], utts)
+        gn = gn_s[...]
+        unit = unit_s[...]
+        grad = branch_ref[...].astype(jnp.float32) + normalise_back(gn * scale, unit, inv_s[:, :1])
+        grad_ref[...] = grad
+        low = grad.astype(jnp.bfloat16)
+        grad_low_ref[...] = low
+        back = mm(low, wout_ref[...].reshape(width, width), NT).astype(jnp.bfloat16)
+        for s in range(groups):
+            back_ref[s] = back[:, s * LANES : (s + 1) * LANES]
+        sums_by_utt(sums_ref, 0, info, gn * unit, utts)
+        sums_by_utt(sums_ref, width, info, gn, utts)
+
+
+def middle(att, stream, info, modulation, cot, late, down_each, out_each, up_each, bias, utts):
+    rows, width = stream.shape
+    devices = late.shape[0]
+    hidden = down_each * devices
+    block = 512
+    blocks = hidden // block
+    halves = width // block
+    groups = width // LANES
+    out_at = down_each // out_each
+    up_at = (down_each + out_each) // up_each
+
+    def fixed(*shape):
+        return pl.BlockSpec(shape, lambda b: (0,) * len(shape))
+
+    def whole(*shape, dtype=jnp.bfloat16):
+        return jax.ShapeDtypeStruct(shape, dtype)
+
+    f32 = jnp.float32
+    return pl.pallas_call(
+        functools.partial(middle_kernel, utts=utts, blocks=blocks),
+        grid=(blocks,),
+        out_shape=(
+            whole(rows, width),
+            whole(width, rows),
+            whole(width, rows),
+            whole(hidden, rows),
+            whole(rows, hidden),
+            whole(rows, width, dtype=f32),
+            whole(rows, width),
+            whole(groups, rows, LANES),
+            whole(utts, 2 * width, dtype=f32),
+            whole(1, hidden, dtype=f32),
+        ),
+        in_specs=[
+            fixed(groups, rows, LANES),
+            fixed(rows, width),
+            fixed(rows, LANES),
+            fixed(utts, 4 * width),
+            fixed(rows, width),
+            pl.BlockSpec((devices, out_each, width), lambda b: (0, out_at, 0)),
+            pl.BlockSpec((devices, up_each, block), lambda b: (0, up_at + b // halves, b % halves)),
+            pl.BlockSpec((devices // blocks, down_each, width), lambda b: (b, 0, 0)),
+            pl.BlockSpec((1, block), lambda b: (0, b)),
+        ],
+        out_specs=(
+            fixed(rows, width),
+            fixed(width, rows),
+            fixed(width, rows),
+            pl.BlockSpec((block, rows), lambda b: (b, 0)),
+            pl.BlockSpec((rows, block), lambda b: (0, b)),
+            fixed(rows, width),
+            fixed(rows, width),
+            fixed(groups, rows, LANES),
+            fixed(utts, 2 * width),
+            pl.BlockSpec((1, block), lambda b: (0, b)),
+        ),
+        scratch_shapes=[
+            pltpu.VMEM((rows, width), f32),
+            pltpu.VMEM((rows, width), f32),
+            pltpu.VMEM((rows, LANES), f32),
+            pltpu.VMEM((rows, width), f32),
+            pltpu.VMEM((rows, width), f32),
+            pltpu.VMEM((rows, width), jnp.bfloat16),
+            pltpu.VMEM((rows, width), jnp.bfloat16),
+        ],
+        compiler_params=pltpu.CompilerParams(vmem_limit_bytes=VMEM),
+        cost_estimate=pl.CostEstimate(
+            flops=12 * rows * hidden * width, bytes_accessed=20 * width * width,
+            transcendentals=rows * hidden,
+        ),
+        name="middle",
+    )(att, stream, info, modulation, cot, late, late, late, bias)
+
+
+def tail_kernel(held_ref, stream_ref, info_ref, mod_ref, mid_ref, w_ref, two_ref, bup_ref,
+                *rest, utts):
+    proj_ref, out_ref, sums_ref, gn_s = rest[-4:]
+    p = pl.program_id(0)
+    rows, width = stream_ref.shape
+    groups = held_ref.shape[0]
+    for s in range(groups):
+        proj_ref[:, s * LANES : (s + 1) * LANES] = held_ref[s, 0]
+    term = mm(proj_ref[...], w_ref[...].reshape(width, width), NT)
+
+    @pl.when(p == 0)
+    def _():
+        gn_s[...] = term
+
+    @pl.when(p > 0)
+    def _():
+        gn_s[...] += term
+
+    @pl.when(p == 2)
+    def _():
+        info = info_ref[...]
+        unit, inverse = normalise(stream_ref[...])
+        scale = per_row(info, 1.0 + mod_ref[:, :width], utts)
+        gn = gn_s[...]
+        out_ref[...] = (mid_ref[...] + normalise_back(gn * scale, unit, inverse)).astype(jnp.bfloat16)
+        sums_ref[0:utts, 2 * width :] = two_ref[...]
+        sums_ref[utts : utts + 1, :] = bup_ref[...]
+        sums_by_utt(sums_ref, 0, info, gn * unit, utts)
+        sums_by_utt(sums_ref, width, info, gn, utts)
+
+
+def tail(held, stream, info, modulation, mid, early, skip_each, qkv_each, two, bup, utts, after):
+    rows, width = stream.shape
+    devices = early.shape[0]
+    groups = held.shape[0]
+    first = skip_each // qkv_each
+
+    def fixed(*shape):
+        return pl.BlockSpec(shape, lambda p: (0,) * len(shape))
+
+    return pl.pallas_call(
+        functools.partial(tail_kernel, utts=utts),
+        grid=(3,),
+        out_shape=(
+            jax.ShapeDtypeStruct((rows, 3 * width), jnp.bfloat16),
+            jax.ShapeDtypeStruct((rows, width), jnp.bfloat16),
+            jax.ShapeDtypeStruct((utts + 1, 4 * width), jnp.float32),
+        ),
+        in_specs=[
+            pl.BlockSpec((groups, 1, rows, LANES), lambda p: (0, p, 0, 0)),
+            fixed(rows, width),
+            fixed(rows, LANES),
+            fixed(utts, 4 * width),
+            fixed(rows, width),
+            pl.BlockSpec((devices, qkv_each, width), lambda p: (0, first + p, 0)),
+            fixed(utts, 2 * width),
+            fixed(1, 4 * width),
+        ]
+        + [pl.BlockSpec(memory_space=pl.ANY)] * len(after),
+        out_specs=(
+            pl.BlockSpec((rows, width), lambda p: (0, p)),
+            fixed(rows, width),
+            fixed(utts + 1, 4 * width),
+        ),
+        scratch_shapes=[pltpu.VMEM((rows, width), jnp.float32)],
+        compiler_params=pltpu.CompilerParams(vmem_limit_bytes=VMEM),
+        cost_estimate=pl.CostEstimate(
+            flops=6 * rows * width * width, bytes_accessed=14 * width * width, transcendentals=0
+        ),
+        name="tail",
+    )(held, stream, info, modulation, mid, early, two, bup, *after)
+
+
+def outer_kernel(pick_ref, *refs, sizes, counts, batch, chosen, adds, extra):
+    u = pl.program_id(0)
+    out_refs = refs[len(refs) - chosen :] if adds else [refs[-1].at[n] for n in range(chosen)]
+    came = refs[len(refs) - chosen - extra - 1] if adds else None
+    at = 0
+    start = 0
+    row = 0
+    for each, count in zip(sizes, counts):
+        own = refs[at : at + chosen]
+        other = refs[at + chosen : at + 2 * chosen]
+        second, second_other = refs[at + 2 * chosen : at + 2 * chosen + 2]
+        for j in range(count):
+            @pl.when(u == start + j)
+            def _(own=own, other=other, second=second, second_other=second_other, each=each, row=row):
+                left = jnp.concatenate(
+                    [
+                        jnp.concatenate([one[...] for one in own], axis=0),
+                        jnp.concatenate([one[...] for one in other], axis=0),
+                    ],
+                    axis=1,
+                )
+                right = jnp.concatenate([second[...], second_other[...]], axis=0)
+                total = mm(left, right, NN)
+                for n in range(chosen):
+                    for z in range(batch):
+                        low = (n * batch + z) * each
+                        part = total[low : low + each]
+                        if adds:
+                            part = part + came[n, z, row : row + each, :].astype(jnp.float32)
+                        out_refs[n][z, row : row + each, :] = part.astype(jnp.bfloat16)
+            row += each
+        start += count
+        at += 2 * chosen + 2
+
+
+def outer_plain(weights, picks, half, batch, wide, add):
+    made = []
+    for first, first_other, second, second_other in weights:
+        block = first.shape[0] // lax.axis_size("seq")
+        columns = second.shape[1] // 2
+        total = 0.0
+        for one, two in ((first, second), (first_other, second_other)):
+            chosen = [
+                lax.dynamic_slice_in_dim(one, picks[n] * block, block, axis=0)
+                for n in range(picks.shape[0])
+            ]
+            total = total + mm(
+                jnp.concatenate(chosen, axis=0), two[:, half * columns : (half + 1) * columns], NN
+            )
+        total = total.reshape(picks.shape[0], batch, block // batch, columns // wide, wide)
+        total = total.transpose(0, 1, 3, 2, 4)
+        made.append(total.reshape(picks.shape[0], batch, -1, wide))
+    made = jnp.concatenate(made, axis=2)
+    if add is None:
+        return made.astype(jnp.bfloat16)
+    return list((made + add.astype(jnp.float32)).astype(jnp.bfloat16))
+
+
+def outer(weights, picks, half, batch, wide, add=None, after=()):
+    chosen = picks.shape[0]
+    seq = lax.axis_size("seq")
+    blocks = [first.shape[0] // seq for first, _, _, _ in weights]
+    sizes = [block // batch for block in blocks]
+    counts = [second.shape[1] // 2 // wide for _, _, second, _ in weights]
+    if any(block % LANES for block in blocks):
+        return outer_plain(weights, picks, half, batch, wide, add)
+    tokens = weights[0][0].shape[1]
+    height = sum(e * c for e, c in zip(sizes, counts))
+    shape = (batch, height, wide)
+    specs = []
+    operands = []
+    start = 0
+    flops = 0
+    for (first, first_other, second, second_other), block, count in zip(weights, blocks, counts):
+        def rows_at(n, block=block):
+            return pl.BlockSpec((block, tokens), lambda u, pick: (pick[n], 0))
+
+        def column_at(u, pick, start=start, count=count):
+            return (0, half * count + jnp.clip(u - start, 0, count - 1))
+
+        specs += [rows_at(n) for n in range(chosen)] * 2
+        specs += [pl.BlockSpec((tokens, wide), column_at)] * 2
+        operands += [first] * chosen + [first_other] * chosen + [second, second_other]
+        start += count
+        flops += 4 * tokens * chosen * block * count * wide
+    whole = pl.BlockSpec(shape, lambda u, pick: (0, 0, 0))
+    stacked = pl.BlockSpec((chosen,) + shape, lambda u, pick: (0, 0, 0, 0))
+    made = jax.ShapeDtypeStruct((chosen,) + shape, jnp.bfloat16)
+    return pl.pallas_call(
+        functools.partial(
+            outer_kernel, sizes=sizes, counts=counts, batch=batch, chosen=chosen,
+            adds=add is not None, extra=len(after),
+        ),
+        grid_spec=pltpu.PrefetchScalarGridSpec(
+            num_scalar_prefetch=1,
+            grid=(sum(counts),),
+            in_specs=specs
+            + ([] if add is None else [stacked])
+            + [pl.BlockSpec(memory_space=pl.ANY)] * len(after),
+            out_specs=stacked if add is None else [whole] * chosen,
+        ),
+        out_shape=made if add is None else [jax.ShapeDtypeStruct(shape, jnp.bfloat16)] * chosen,
+        compiler_params=pltpu.CompilerParams(vmem_limit_bytes=VMEM),
+        cost_estimate=pl.CostEstimate(flops=2 * flops, bytes_accessed=flops // 300, transcendentals=0),
+        name="outer",
+    )(picks, *operands, *(() if add is None else (add,)), *after)
+
+
+def merge_kernel(at_ref, *refs, sums, count):
+    outs = refs[len(refs) - count :]
+    for n in range(count):
+        z = lax.rem(at_ref[0] + n, count)
+        for h in range(sums):
+            total = refs[2 * h][z].astype(jnp.float32) + refs[2 * h + 1][z].astype(jnp.float32)
+            outs[n][h] = total.astype(jnp.bfloat16)
+
+
+def merge(pairs, after):
+    batch, height, wide = pairs[0][0].shape
+    at = lax.axis_index("batch").reshape(1).astype(jnp.int32)
+    vmem = pl.BlockSpec(memory_space=pltpu.VMEM)
+    sums = len(pairs)
+    size = sums * batch * height * wide
+    return list(pl.pallas_call(
+        functools.partial(merge_kernel, sums=sums, count=batch),
+        out_shape=[jax.ShapeDtypeStruct((sums, height, wide), jnp.bfloat16)] * batch,
+        in_specs=[pl.BlockSpec(memory_space=pltpu.SMEM)]
+        + [vmem] * (2 * sums)
+        + [pl.BlockSpec(memory_space=pl.ANY)] * len(after),
+        out_specs=[vmem] * batch,
+        cost_estimate=pl.CostEstimate(flops=size, bytes_accessed=6 * size, transcendentals=0),
+        compiler_params=pltpu.CompilerParams(vmem_limit_bytes=VMEM // 2),
+        name="merge",
+    )(at, *[one for pair in pairs for one in pair], *after))
+
+
+def finish_kernel(own_ref, *rest, count):
+    total = own_ref[...].astype(jnp.float32)
+    for n in range(count):
+        total = total + rest[n][...].astype(jnp.float32)
+    rest[-1][...] = total
+
+
+def finish(own, came, after):
+    vmem = pl.BlockSpec(memory_space=pltpu.VMEM)
+    return pl.pallas_call(
+        functools.partial(finish_kernel, count=len(came)),
+        out_shape=jax.ShapeDtypeStruct(own.shape, jnp.float32),
+        in_specs=[vmem] * (1 + len(came)) + [pl.BlockSpec(memory_space=pl.ANY)] * len(after),
+        out_specs=vmem,
+        cost_estimate=pl.CostEstimate(
+            flops=4 * own.size, bytes_accessed=12 * own.size, transcendentals=0
+        ),
+        name="finish",
+    )(own, *came, *after)
+
+
+def tie_kernel(*refs):
+    pass
+
+
+def tie(value, after):
+    anywhere = pl.BlockSpec(memory_space=pl.ANY)
+    return pl.pallas_call(
+        tie_kernel,
+        out_shape=jax.ShapeDtypeStruct(value.shape, value.dtype),
+        in_specs=[anywhere] * (1 + len(after)),
+        out_specs=anywhere,
+        input_output_aliases={0: 0},
+        name="tie",
+    )(value, *after)
+
+
+def times(first_op, second_op):
+    return lax.dot_general(first_op, second_op, NN, preferred_element_type=jnp.float32)
+
+
+def swap(value, bit):
+    size = lax.axis_size("seq")
+    return lax.ppermute(value, "seq", [(i, i ^ bit) for i in range(size)])
+
+
+def ahead(value, step):
+    size = lax.axis_size("batch")
+    return lax.ppermute(value, "batch", [(i, (i + step) % size) for i in range(size)])
+
+
+class Sum:
+    wide = 512
+
+    def __init__(self, weights, half, bits):
+        self.weights, self.half, self.bits = weights, half, bits
+        self.seq = lax.axis_size("seq")
+        self.batch = lax.axis_size("batch")
+        self.next = 1
+
+    def picks(self, sent):
+        me = lax.axis_index("seq")
+        first = me ^ self.bits[0] if sent else me
+        found = [0]
+        for bit in self.bits[:0:-1]:
+            found = found + [f | bit for f in found]
+        return (jnp.array(found, jnp.int32) ^ first).astype(jnp.int32)
+
+    def send(self, after=()):
+        sent = outer(self.weights, self.picks(True), self.half, self.batch, self.wide, None, after)
+        self.came = swap(sent, self.bits[0])
+        return [sent]
+
+    def keep(self, after=()):
+        self.total = list(
+            outer(self.weights, self.picks(False), self.half, self.batch, self.wide, self.came, after)
+        )
+
+    def pass_on(self):
+        count = len(self.total) // 2
+        sent = self.total[count:]
+        self.total = self.total[:count]
+        self.came = [swap(one, self.bits[self.next]) for one in sent]
+        self.next += 1
+        return sent
+
+    def take(self):
+        self.total = [
+            (a.astype(jnp.float32) + b.astype(jnp.float32)).astype(jnp.bfloat16)
+            for a, b in zip(self.total, self.came)
+        ]
+
+
+class Sums:
+    def __init__(self, weights, orders):
+        self.weights = weights
+        self.halves = [Sum(weights, half, bits) for half, bits in enumerate(orders)]
+
+    def send(self, after=()):
+        return sum([one.send(after) for one in self.halves], [])
+
+    def came(self):
+        return [one.came for one in self.halves]
+
+    def keep(self, after=()):
+        for one in self.halves:
+            one.keep(after)
+        return sum([one.pass_on() for one in self.halves], [])
+
+    def spread(self, after=()):
+        for one in self.halves:
+            while one.next < len(one.bits):
+                one.take()
+                one.pass_on()
+        pieces = merge([(one.total[0], one.came[0]) for one in self.halves], tuple(after))
+        self.own = pieces[0]
+        self.pieces = [ahead(piece, step) for step, piece in enumerate(pieces) if step]
+        return pieces[1:]
+
+    def result(self, after=()):
+        total = finish(self.own, self.pieces, tuple(after))
+        devices = lax.axis_size("seq") * lax.axis_size("batch")
+        made = []
+        at = 0
+        for first, _, second, _ in self.weights:
+            each = first.shape[0] // devices
+            columns = second.shape[1] // 2
+            count = columns // Sum.wide
+            piece = total[:, at : at + each * count].reshape(2, count, each, Sum.wide)
+            made.append(piece.transpose(2, 0, 1, 3).reshape(each, 2 * columns))
+            at += each * count
+        return made
 
 
 def turn_tables(position):
@@ -458,20 +969,6 @@
         up_proj.shape[0],
         down_proj.shape[0],
     )
-    full_skip = early[:, :skip_each].reshape(2 * width, width)
-    full_qkv = [
-        early[:, skip_each + p * qkv_each : skip_each + (p + 1) * qkv_each].reshape(width, width)
-        for p in range(3)
-    ]
-    full_down = late[:, :down_each].reshape(hidden, width)
-    full_out = late[:, down_each : down_each + out_each].reshape(width, width)
-    full_up = (
-        late[:, down_each + out_each :]
-        .reshape(devices, hidden // width, up_each, width)
-        .transpose(0, 2, 1, 3)
-        .reshape(width, hidden)
-    )
-
     utt_lengths = lengths[0]
     ends = jnp.cumsum(utt_lengths).astype(jnp.int32)
     starts = ends - utt_lengths
@@ -500,106 +997,111 @@
     silu_value, silu_pull = jax.vjp(jax.nn.silu, time_rows)
     time_vec = silu_value.astype(jnp.bfloat16)
     terms = times(time_vec, mod_proj)
-    bias_terms = lax.dynamic_update_slice(
-        jnp.zeros((4 * width,), jnp.float32),
-        mod_bias.astype(jnp.float32),
-        (device * mod_bias.shape[0],),
-    )
-    terms = (terms + bias_terms[None, :]).reshape(batch, utts, 4 * width)
+    def placed(bias):
+        return lax.dynamic_update_slice(
+            jnp.zeros((4 * width,), jnp.float32), bias.astype(jnp.float32), (device * bias.shape[0],)
+        )
+
+    terms = (terms + placed(mod_bias)[None, :]).reshape(batch, utts, 4 * width)
+    up_terms = jnp.broadcast_to(placed(up_bias), (batch, 1, 4 * width))
+    terms = jnp.concatenate([terms, up_terms], axis=1)
     modulation = lax.dynamic_index_in_dim(terms, batch_at, 0, keepdims=False)
     for step in range(1, batch):
         modulation = modulation + ahead(
             lax.dynamic_index_in_dim(terms, (batch_at + step) % batch, 0, keepdims=False), step
         )
     modulation = seq_total(modulation)
-    scale_one = per_row(member_rows, 1.0 + modulation[:, :width])
-    shift_one = per_row(member_rows, modulation[:, width : 2 * width])
-    scale_two = per_row(member_rows, 1.0 + modulation[:, 2 * width : 3 * width])
-    shift_two = per_row(member_rows, modulation[:, 3 * width :])
-    full_bup = all_gather_bias(up_bias)
-
-    joined = jnp.concatenate([inputs, skip_rows], axis=1)
-    stream_in = times(joined, full_skip)
-    unit_one, inverse_one = normalise(stream_in)
-    normed_one = (unit_one * scale_one + shift_one).astype(jnp.bfloat16)
-    sent = project(normed_one, early, skip_each, qkv_each, cos, sin)
+    full_bup = modulation[utts:]
+    modulation = modulation[:utts]
+    info = jnp.pad(member_rows, ((0, 0), (0, LANES - utts)))
+    branch = (cotangent[0].astype(jnp.float32) * in_span[:, None]).astype(jnp.bfloat16)
+    joined = jnp.concatenate([inputs.T, skip_rows.T], axis=0)
+    branch_pair = (branch, swap(branch, 1))
+    joined_pair = (joined, swap(joined, 1))
+
+    stream_in, sent, normed_one = front(
+        inputs, skip_rows, info, modulation, early, skip_each, qkv_each, cos, sin, utts,
+        (group_cos, group_sin, branch_pair[1], joined_pair[1]),
+    )
     per_device = width // seq
+    groups = width // LANES
     if per_device < LANES:
-        sent = sent.reshape(-1, 3, rows, 2, per_device).transpose(0, 3, 1, 2, 4)
+        sent = sent.reshape(groups, 3, rows, 2, per_device).transpose(0, 3, 1, 2, 4)
         sent = sent.reshape(seq, 3, rows, per_device)
         sent = jnp.pad(sent, ((0, 0), (0, 0), (0, 0), (0, LANES - per_device)))
     held = lax.all_to_all(sent, "seq", 0, 0, tiled=True)
+    normed_one_pair = (normed_one, swap(normed_one, 1))
     head_out, log_sums = attend(held, ends, heads, 1024, 512)
-    attended = lax.all_to_all(
+    att = lax.all_to_all(
         head_out.reshape(seq, rows, LANES)[:, :, :per_device], "seq", 0, 0, tiled=True
     )
-    attended = attended.transpose(1, 0, 2).reshape(rows, width)
-    stream_mid = stream_in + times(attended, full_out)
-    unit_two, inverse_two = normalise(stream_mid)
-    normed_two = (unit_two * scale_two + shift_two).astype(jnp.bfloat16)
-    pre_act = times(normed_two, full_up) + full_bup[None, :]
-    act_value, act_slope = gelu_parts(pre_act)
-    activated = act_value.astype(jnp.bfloat16)
-    result = (stream_mid + times(activated, full_down)).astype(jnp.bfloat16)
-
-    grad_result = cotangent[0].astype(jnp.float32) * in_span[:, None]
-    grad_branch = grad_result.astype(jnp.bfloat16)
-    grad_pre = (times_transpose(grad_branch, full_down) * act_slope).astype(jnp.bfloat16)
-    grad_normed = times_transpose(grad_pre, full_up)
-    grad_mid = grad_result + normalise_back(grad_normed * scale_two, unit_two, inverse_two)
-    grad_attn_out = grad_mid.astype(jnp.bfloat16)
-    grad_attended = times_transpose(grad_attn_out, full_out).astype(jnp.bfloat16)
+    if per_device < LANES:
+        att = att.reshape(groups, 2, rows, per_device).transpose(0, 2, 1, 3).reshape(groups, rows, LANES)
+
+    result, attended, normed_two, activated, grad_pre, grad_mid, grad_low, back, mod_two, bup_terms = middle(
+        att, stream_in, info, modulation, branch, late, down_each, out_each, up_each, full_bup, utts
+    )
+    if per_device < LANES:
+        back = back.reshape(groups, rows, 2, per_device).transpose(0, 2, 1, 3).reshape(seq, rows, per_device)
+        back = jnp.pad(back, ((0, 0), (0, 0), (0, LANES - per_device)))
+    back = lax.all_to_all(back, "seq", 0, 0, tiled=True).reshape(frames, LANES)
     high = [seq >> (i + 1) for i in range(seq.bit_length() - 2)]
     low = high[::-1]
-    grad_down = scatter_sum(activated, grad_branch, low)
-    grad_up = scatter_sum(normed_two, grad_pre, high)
-    grad_out_w = scatter_sum(attended, grad_attn_out, high)
-    mod_two = jnp.concatenate(
-        [
-            jnp.dot(member_rows.T, grad_normed * unit_two, precision=highest),
-            jnp.dot(member_rows.T, grad_normed, precision=highest),
-        ],
-        axis=1,
-    )
-
-    back = grad_attended.reshape(rows, seq, per_device).transpose(1, 0, 2)
+
+    def pairs(first, second):
+        return (first[0], first[1], second[0], second[1])
+
+    def pair(value):
+        return (value, swap(value, 1))
+
+    first_weights = [
+        pairs(pair(activated), branch_pair),
+        pairs(pair(normed_two), pair(grad_pre)),
+        pairs(pair(attended), pair(grad_low)),
+    ]
+    sums = Sums(first_weights, (low, high))
+    waits = sums.send()
+
+    grad_held = attend_back(
+        held, back, head_out, log_sums, group_cos, group_sin, ends, heads, waits, 1024, 512
+    )
+    mark = (grad_held,)
+    grad_held = tie(grad_held, sums.came())
+    grad_held = lax.all_to_all(grad_held[..., :per_device], "seq", 0, 0, tiled=True)
     if per_device < LANES:
-        back = jnp.pad(back, ((0, 0), (0, 0), (0, LANES - per_device)))
-    back = lax.all_to_all(back, "seq", 0, 0, tiled=True).reshape(frames, LANES)
-    grad_held = attend_back(
-        held, back, head_out, log_sums, group_cos, group_sin, ends, heads, 1024, 512
-    )
-    grad_projected = lax.all_to_all(grad_held[..., :per_device], "seq", 0, 0, tiled=True)
-    grad_projected = grad_projected.transpose(2, 1, 0, 3).reshape(rows, 3 * width)
-    grad_qkv_w = scatter_sum(normed_one, grad_projected, low)
-    grad_normed_one = sum(
-        times_transpose(grad_projected[:, p * width : (p + 1) * width], full_qkv[p])
-        for p in range(3)
-    )
-    grad_stream = (
-        grad_mid + normalise_back(grad_normed_one * scale_one, unit_one, inverse_one)
-    ).astype(jnp.bfloat16)
-    grad_skip_w = scatter_sum(joined, grad_stream, high)
-    grad_joined = times_transpose(grad_stream, full_skip)
-    grad_inputs = grad_joined[:, :width].astype(jnp.bfloat16)
-    grad_skip_rows = grad_joined[:, width:].astype(jnp.bfloat16)
-
-    mod_one = jnp.concatenate(
-        [
-            jnp.dot(member_rows.T, grad_normed_one * unit_one, precision=highest),
-            jnp.dot(member_rows.T, grad_normed_one, precision=highest),
-        ],
-        axis=1,
-    )
-    grad_modulation = all_pieces(seq_total(jnp.concatenate([mod_one, mod_two], axis=1)))
-    grad_modulation = grad_modulation.reshape(batch * utts, 4 * width)
+        grad_held = grad_held.reshape(groups, 2, 3, rows, per_device).transpose(0, 2, 3, 1, 4)
+        grad_held = grad_held.reshape(groups, 3, rows, LANES)
+    waits = sums.keep(mark)
+
+    grad_projected, grad_stream, row_sums = tail(
+        grad_held, stream_in, info, modulation, grad_mid, early, skip_each, qkv_each,
+        mod_two, bup_terms, utts, waits,
+    )
+    row_sums = lax.all_gather(row_sums, BOTH, axis=0, tiled=False)
+    last_weights = [
+        pairs(joined_pair, pair(grad_stream)),
+        pairs(normed_one_pair, pair(grad_projected)),
+    ]
+    last_sums = Sums(last_weights, (low, high))
+    waits = last_sums.send()
+    waits = sums.spread(waits)
+    grad_inputs, grad_skip_rows = unjoin(grad_stream, early, skip_each, waits)
+    waits = last_sums.keep((grad_inputs,))
+    grad_down, grad_up, grad_out_w = sums.result(waits)
+    last_sums.spread((grad_down,))
+    grad_skip_w, grad_qkv_w = last_sums.result()
+
+    row_sums = jnp.sum(row_sums.reshape(seq, batch, utts + 1, 4 * width), axis=0)
+    grad_modulation = row_sums[:, :utts].reshape(batch * utts, 4 * width)
+    grad_bup = lax.dynamic_slice_in_dim(
+        jnp.sum(row_sums[:, utts], axis=0), device * up_bias.shape[0], up_bias.shape[0]
+    )
     grad_bmod = lax.dynamic_slice_in_dim(
         jnp.sum(grad_modulation, axis=0), device * mod_bias.shape[0], mod_bias.shape[0]
     )
     grad_mod_w = jnp.dot(time_vec.astype(jnp.float32).T, grad_modulation, precision=highest)
     grad_time_vec = jnp.dot(grad_modulation, mod_proj.astype(jnp.float32).T, precision=highest)
     grad_table = jnp.dot(step_pick.T, silu_pull(grad_time_vec)[0], precision=highest)
-    grad_bup = bias_total(jnp.sum(grad_pre.astype(jnp.float32), axis=0))
     return (
         result[None],
         grad_inputs[None],
@@ -614,29 +1116,6 @@
         grad_bup,
         grad_down,
     )
-
-
-def all_gather_bias(bias):
-    seq = lax.axis_size("seq")
-    pieces = all_pieces(bias.astype(jnp.float32)).reshape(1, -1)
-    bit = 1
-    out = jnp.zeros((seq, pieces.shape[1]), jnp.float32)
-    out = lax.dynamic_update_slice(out, pieces, (lax.axis_index("seq"), 0))
-    return seq_total(out).reshape(-1)
-
-
-def bias_total(terms):
-    batch = lax.axis_size("batch")
-    place = lax.axis_index("batch")
-    size = terms.shape[0] // (lax.axis_size("seq") * batch)
-    terms = seq_total(terms.reshape(-1, size))
-    total = lax.dynamic_slice_in_dim(terms, lax.axis_index("seq") * batch, batch, axis=0)
-    result = lax.dynamic_index_in_dim(total, place, 0, keepdims=False)
-    for step in range(1, batch):
-        result = result + ahead(
-            lax.dynamic_index_in_dim(total, (place + step) % batch, 0, keepdims=False), step
-        )
-    return result
 
 
 def solution(mesh):

time: 726 us -> 596 us (0.82)
  the two profiles are of different devices: /device:TPU:0 before, /device:TPU:9 now
where the time goes in v2:
time: 596 us; the launch traced here: 585 us
  Pallas kernels  248 us (42%)
  waiting for transfers between devices  160 us (27%)
  starting transfers between devices  50.1 us (8%)
  blocking collectives  49.2 us (8%)
  local copies, waits for them, and re-layouts  33.9 us (6%)
  other arithmetic  24.7 us (4%)
  between operations  14.7 us (2%)
    pallas_call x1, Pallas kernels, attend_back(): pl.pallas_call(functools.partial(bwd_kernel, heads=heads, utts=utts, bq=b...  65.3 us
    pallas_call x8, Pallas kernels, outer(): pl.pallas_call(functools.partial(outer_kernel, sizes=sizes, counts=counts...  63.5 us
    ppermute x12, waiting for transfers between devices, ahead(): lax.ppermute(value, 'batch', [(i, (i + step) % size) for i in range(size)])  50.3 us
    all_to_all x1, blocking collectives, shards(): held = lax.all_to_all(sent, 'seq', 0, 0, tiled=True)  49.2 us
    pallas_call x1, Pallas kernels, attend(): pl.pallas_call(functools.partial(fwd_kernel, heads=heads, utts=utts, bq=b...  44.1 us
    ppermute x21, waiting for transfers between devices, swap(): return lax.ppermute(value, 'seq', [(i, i ^ bit) for i in range(size)])  42.3 us
    all_gather x1, waiting for transfers between devices, shards(): early = lax.all_gather(early, BOTH, axis=0, tiled=False)  38.7 us
    pallas_call x1, Pallas kernels, middle(): pl.pallas_call(functools.partial(middle_kernel, utts=utts, blocks=blocks)...  30.7 us
  transfers between devices with their start and end apart: 39, of which 19 were waited for; matrix products, arithmetic and copies ran while one was open for 8% of the time, Pallas kernels for 35%

profile of v2, /device:TPU:9, one launch (start us, length us, event | category | flops | bytes accessed | tf_op | source)
XLA Modules:
  0.0 585.0 jit_solution(2536886839590418022)
XLA Ops:
  8.4 1.7 pad_maximum_fusion.1
  23.5 7.1 %fusion = (f32[3072,128]{1,0:T(8,128)}, f32[3072,128]{1,0:T(8,128)}) fusion(f32[128]{0:T(128)S(1)} %get-tuple-element.101, f32[128]{0:T(128)S(1)} %get-tuple-element.102, f32[3072]{0:T(1024)S(1)} %subtract_convert_fusion), kind=kLoop, calls=%fused_computation.3 | loop fusion | flops 786432 | bytes 3159040 | tf_op jit(solution)/shard_map/mul | solution.py:900
  32.5 1.7 reshape.149
  35.3 3.2 collective-permute-start.4
  38.5 6.1 %collective-permute-done.4 = f32[4,4096]{1,0:T(4,128)S(1)} collective-permute-done((f32[4,4096]{1,0:T(4,128)S(1)}, f32[4,4096]{1,0:T(4,128)S(1)}, u32[]{:S(2)}, u32[]{:S(2)}) %collective-permute-start.4) | collective-permute-done | bytes 65568 | tf_op jit(solution)/shard_map/ppermute | solution.py:808
  44.6 2.8 collective-permute-done.5
  48.3 4.0 collective-permute-start.6
  55.2 2.5 collective-permute-done.7
  61.6 38.7 %all-gather.8.cloned.1.call-done = bf16[5120,1024]{1,0:T(8,128)(2,1)} async-done(((bf16[160,1024]{1,0:T(8,128)(2,1)}), bf16[5120,1024]{1,0:T(8,128)(2,1)}) %all-gather.8.cloned.1.call-update) | async-done | bytes 10485776 | tf_op jit(solution)/shard_map/all_gather | solution.py:963
  100.3 18.8 %front.1 = (f32[384,1024]{1,0:T(8,128)}, bf16[8,3,384,128]{3,2,1,0:T(8,128)(2,1)}, bf16[1024,384]{1,0:T(8,128)(2,1)}) custom-call(bf16[384,1024]{1,0:T(8,128)(2,1)} %bitcast.92, bf16[384,1024]{1,0:T(8,128)(2,1)} %bitcast.93, f32[384,128]{1,0:T(8,128)} %pad_convert_fusion.info_ref, f32[3,4096]{1,0:T(4,128)} %bitcast.104, bf16[32,160,1024]{2,1,0:T(8,128)(2,1)} %bitcast.88, ...), custom_call_target="tpu_custom_call" | custom-call | flops 6442450944 | bytes 20971520 | tf_op jit(solution)/shard_map/front/pallas_call | solution.py:377
  119.0 49.2 %all_to_all.20.qkv_ref = bf16[8,3,384,128]{3,2,1,0:T(8,128)(2,1)} all-to-all(bf16[8,3,384,128]{3,2,1,0:T(8,128)(2,1)} %get-tuple-element.48), channel_id=1, replica_groups=mesh['seq'=8,'batch'=4] {'seq'}, dimensions={0} | all-to-all | bytes 4718592 | tf_op jit(solution)/shard_map/all_to_all | solution.py:1032
  168.2 44.1 %attend.1 = (bf16[3072,128]{1,0:T(8,128)(2,1)}, f32[3072,128]{1,0:T(8,128)}) custom-call(s32[3]{0:T(128)} %bitcast.114, bf16[8,3,384,128]{3,2,1,0:T(8,128)(2,1)} %all_to_all.20.qkv_ref), custom_call_target="tpu_custom_call" | custom-call | flops 48318382080 | bytes 4718592 | tf_op jit(solution)/shard_map/attend/pallas_call | solution.py:116
  212.3 5.4 all-to-all-start.1
  219.2 7.6 %all-to-all-done.1.att_ref = bf16[8,384,128]{2,1,0:T(8,128)(2,1)S(1)} async-done(((bf16[8,384,128]{2,1,0:T(8,128)(2,1)}), bf16[8,384,128]{2,1,0:T(8,128)(2,1)S(1)}, u32[]{:S(2)}, u32[]{:S(2)}) %all-to-all-start.1) | async-done | bytes 786464 | tf_op jit(solution)/shard_map/all_to_all | solution.py:1035
  226.7 16.7 %all-gather.10.cloned.1.call-done = bf16[9216,1024]{1,0:T(8,128)(2,1)} async-done(((bf16[288,1024]{1,0:T(8,128)(2,1)}), bf16[9216,1024]{1,0:T(8,128)(2,1)}) %all-gather.10.cloned.1.call-update) | async-done | bytes 18874384 | tf_op jit(solution)/shard_map/all_gather | solution.py:964
  243.5 30.7 %middle.1 = (bf16[384,1024]{1,0:T(8,128)(2,1)}, bf16[1024,384]{1,0:T(8,128)(2,1)}, bf16[1024,384]{1,0:T(8,128)(2,1)}, bf16[4096,384]{1,0:T(8,128)(2,1)}, bf16[38...) custom-call(bf16[8,384,128]{2,1,0:T(8,128)(2,1)} %copy-done.24, ...), custom_call_target="tpu_custom_call" | custom-call | flops 19327352832 | bytes 20971520 | tf_op jit(solution)/shard_map/middle/pallas_call | solution.py:495
  276.0 5.7 all-to-all-start.2
  282.3 3.6 collective-permute-done.12.refs_8_.refs_9_
  288.1 1.7 copy-done.10
  289.8 9.0 %outer.9.rest_1_ = bf16[2,4,288,512]{3,2,1,0:T(8,128)(2,1)} custom-call(s32[2]{0:T(128)} %fusion.32.pick_ref, bf16[4096,384]{1,0:T(8,128)(2,1)} %get-tuple-element.54.refs_0_.refs_1_, bf16[4096,384]{1,0:T(8,128)(2,1)} %get-tuple-element.54.refs_0_.refs_1_, bf16[4096,384]{1,0:T(8,128)(2,1)} %copy-done.10, bf16[4096,384]{1,0:T(8,128)(2,1)} %copy-done.10, ...), custom_call_target="tpu_custom_call" | custom-call | flops 3623878656 | bytes 6039797 | tf_op jit(solution)/shard_map/outer/pallas_call | solution.py:712
  300.1 9.0 %outer.8.rest_0_ = bf16[2,4,288,512]{3,2,1,0:T(8,128)(2,1)} custom-call(s32[2]{0:T(128)} %fusion.34.pick_ref, bf16[4096,384]{1,0:T(8,128)(2,1)} %get-tuple-element.54.refs_0_.refs_1_, bf16[4096,384]{1,0:T(8,128)(2,1)} %get-tuple-element.54.refs_0_.refs_1_, bf16[4096,384]{1,0:T(8,128)(2,1)} %copy-done.10, bf16[4096,384]{1,0:T(8,128)(2,1)} %copy-done.10, ...), custom_call_target="tpu_custom_call" | custom-call | flops 3623878656 | bytes 6039797 | tf_op jit(solution)/shard_map/outer/pallas_call | solution.py:712
  309.1 2.6 collective-permute-start.16
  311.7 65.3 %attend_back.1.refs_19_ = bf16[8,3,384,128]{3,2,1,0:T(8,128)(2,1)} custom-call(s32[3]{0:T(128)} %bitcast.115, bf16[8,3,384,128]{3,2,1,0:T(8,128)(2,1)} %all_to_all.20.qkv_ref, bf16[3072,128]{1,0:T(8,128)(2,1)} %bitcast.25.da_ref, bf16[3072,128]{1,0:T(8,128)(2,1)} %get-tuple-element.49.out_ref, f32[3072,128]{1,0:T(8,128)} %get-tuple-element.53.lse_ref, ...), custom_call_target="tpu_custom_call" | custom-call | flops 77309411328 | bytes 9437184 | tf_op jit(solution)/shard_map/attend_back/pallas_call | solution.py:227
  377.0 3.3 copy.89.refs_0_
  381.7 4.3 all-to-all-start.3
  387.3 9.9 %outer.11 = (bf16[4,288,512]{2,1,0:T(8,128)(2,1)}, bf16[4,288,512]{2,1,0:T(8,128)(2,1)}) custom-call(s32[2]{0:T(128)} %fusion.31.pick_ref, bf16[4096,384]{1,0:T(8,128)(2,1)} %get-tuple-element.54.refs_0_.refs_1_, bf16[4096,384]{1,0:T(8,128)(2,1)} %get-tuple-element.54.refs_0_.refs_1_, bf16[4096,384]{1,0:T(8,128)(2,1)} %copy-done.10, ...), custom_call_target="tpu_custom_call" | custom-call | flops 3623878656 | bytes 6039797 | tf_op jit(solution)/shard_map/outer/pallas_call | solution.py:712
  397.2 10.0 %outer.10 = (bf16[4,288,512]{2,1,0:T(8,128)(2,1)}, bf16[4,288,512]{2,1,0:T(8,128)(2,1)}) custom-call(s32[2]{0:T(128)} %fusion.33.pick_ref, bf16[4096,384]{1,0:T(8,128)(2,1)} %get-tuple-element.54.refs_0_.refs_1_, bf16[4096,384]{1,0:T(8,128)(2,1)} %get-tuple-element.54.refs_0_.refs_1_, bf16[4096,384]{1,0:T(8,128)(2,1)} %copy-done.10, ...), custom_call_target="tpu_custom_call" | custom-call | flops 3623878656 | bytes 6039797 | tf_op jit(solution)/shard_map/outer/pallas_call | solution.py:712
  407.1 4.9 all-to-all-done.3.held_ref
  413.4 10.8 %tail.1 = (bf16[384,3072]{1,0:T(8,128)(2,1)}, bf16[384,1024]{1,0:T(8,128)(2,1)}, f32[4,4096]{1,0:T(4,128)}) custom-call(bf16[8,3,384,128]{3,2,1,0:T(8,128)(2,1)} %copy-done.17, f32[384,1024]{1,0:T(8,128)} %get-tuple-element.50.stream_ref, f32[384,128]{1,0:T(8,128)} %pad_convert_fusion.info_ref, f32[3,4096]{1,0:T(4,128)} %bitcast.106, ...), custom_call_target="tpu_custom_call" | custom-call | flops 2415919104 | bytes 14680064 | tf_op jit(solution)/shard_map/tail/pallas_call | solution.py:591
  424.2 3.6 collective-permute-start.22
  429.0 5.1 collective-permute-done.21.refs_8_.refs_9_
  435.3 6.1 %outer.13.refs_5_ = bf16[2,4,160,512]{3,2,1,0:T(8,128)(2,1)} custom-call(s32[2]{0:T(128)} %fusion.32.pick_ref, bf16[2048,384]{1,0:T(8,128)(2,1)} %copy-done.11, bf16[2048,384]{1,0:T(8,128)(2,1)} %copy-done.11, bf16[2048,384]{1,0:T(8,128)(2,1)} %copy-done.12, bf16[2048,384]{1,0:T(8,128)(2,1)} %copy-done.12, ...), custom_call_target="tpu_custom_call" | custom-call | flops 2013265920 | bytes 3355443 | tf_op jit(solution)/shard_map/outer/pallas_call | solution.py:712
  441.8 6.3 %outer.12.refs_4_ = bf16[2,4,160,512]{3,2,1,0:T(8,128)(2,1)} custom-call(s32[2]{0:T(128)} %fusion.34.pick_ref, bf16[2048,384]{1,0:T(8,128)(2,1)} %copy-done.11, bf16[2048,384]{1,0:T(8,128)(2,1)} %copy-done.11, bf16[2048,384]{1,0:T(8,128)(2,1)} %copy-done.12, bf16[2048,384]{1,0:T(8,128)(2,1)} %copy-done.12, ...), custom_call_target="tpu_custom_call" | custom-call | flops 2013265920 | bytes 3355443 | tf_op jit(solution)/shard_map/outer/pallas_call | solution.py:712
  448.4 10.2 %collective-permute-done.19.refs_3_ = bf16[4,288,512]{2,1,0:T(8,128)(2,1)} collective-permute-done((bf16[4,288,512]{2,1,0:T(8,128)(2,1)}, bf16[4,288,512]{2,1,0:T(8,128)(2,1)}, u32[]{:S(2)}, u32[]{:S(2)}) %collective-permute-start.19) | collective-permute-done | bytes 1179680 | tf_op jit(solution)/shard_map/ppermute | solution.py:803
  459.9 3.2 merge.2
  466.6 5.8 unjoin.1
  472.3 17.1 %collective-permute-done.25.refs_12_ = bf16[2,4,160,512]{3,2,1,0:T(8,128)(2,1)} collective-permute-done((bf16[2,4,160,512]{3,2,1,0:T(8,128)(2,1)}, bf16[2,4,160,512]{3,2,1,0:T(8,128)(2,1)}, u32[]{:S(2)}, u32[]{:S(2)}) %collective-permute-start.25) | collective-permute-done | bytes 1310752 | tf_op jit(solution)/shard_map/ppermute | solution.py:803
  489.4 6.6 %outer.15 = (bf16[4,160,512]{2,1,0:T(8,128)(2,1)}, bf16[4,160,512]{2,1,0:T(8,128)(2,1)}) custom-call(s32[2]{0:T(128)} %fusion.31.pick_ref, bf16[2048,384]{1,0:T(8,128)(2,1)} %copy-done.11, bf16[2048,384]{1,0:T(8,128)(2,1)} %copy-done.11, bf16[2048,384]{1,0:T(8,128)(2,1)} %copy-done.12, bf16[2048,384]{1,0:T(8,128)(2,1)} %copy-done.12, ...), custom_call_target="tpu_custom_call" | custom-call | flops 2013265920 | bytes 3355443 | tf_op jit(solution)/shard_map/outer/pallas_call | solution.py:712
  497.2 6.6 %outer.14 = (bf16[4,160,512]{2,1,0:T(8,128)(2,1)}, bf16[4,160,512]{2,1,0:T(8,128)(2,1)}) custom-call(s32[2]{0:T(128)} %fusion.33.pick_ref, bf16[2048,384]{1,0:T(8,128)(2,1)} %copy-done.11, bf16[2048,384]{1,0:T(8,128)(2,1)} %copy-done.11, bf16[2048,384]{1,0:T(8,128)(2,1)} %copy-done.12, bf16[2048,384]{1,0:T(8,128)(2,1)} %copy-done.12, ...), custom_call_target="tpu_custom_call" | custom-call | flops 2013265920 | bytes 3355443 | tf_op jit(solution)/shard_map/outer/pallas_call | solution.py:712
  504.1 16.4 %collective-permute-done.28.rest_1_ = bf16[2,288,512]{2,1,0:T(8,128)(2,1)S(1)} collective-permute-done((bf16[2,288,512]{2,1,0:T(8,128)(2,1)}, bf16[2,288,512]{2,1,0:T(8,128)(2,1)S(1)}, u32[]{:S(2)}, u32[]{:S(2)}) %collective-permute-start.28) | collective-permute-done | bytes 589856 | tf_op jit(solution)/shard_map/ppermute | solution.py:808
  521.6 2.9 finish.2
  529.5 2.8 reduce_sum.67
  532.3 1.7 slice_reduce_fusion.1
  534.0 1.7 reshape.154
  539.6 3.0 collective-permute-start.31
  547.0 18.8 %collective-permute-done.31.rest_1_ = bf16[2,160,512]{2,1,0:T(8,128)(2,1)S(1)} collective-permute-done((bf16[2,160,512]{2,1,0:T(8,128)(2,1)S(1)}, bf16[2,160,512]{2,1,0:T(8,128)(2,1)S(1)}, u32[]{:S(2)}, u32[]{:S(2)}) %collective-permute-start.31) | collective-permute-done | bytes 327712 | tf_op jit(solution)/shard_map/ppermute | solution.py:808
  565.8 6.1 %collective-permute-done.32.rest_2_ = bf16[2,160,512]{2,1,0:T(8,128)(2,1)S(1)} collective-permute-done((bf16[2,160,512]{2,1,0:T(8,128)(2,1)S(1)}, bf16[2,160,512]{2,1,0:T(8,128)(2,1)S(1)}, u32[]{:S(2)}, u32[]{:S(2)}) %collective-permute-start.32) | collective-permute-done | bytes 327712 | tf_op jit(solution)/shard_map/ppermute | solution.py:808
  572.6 2.3 finish.3
  (217 shorter events, 63.8 us)
Async XLA Ops:
  7.2 24.4 %copy-start = (bf16[32,4096]{1,0:T(8,128)(2,1)S(1)}, bf16[32,4096]{1,0:T(8,128)(2,1)}, u32[]{:S(2)}) copy-start(bf16[32,4096]{1,0:T(8,128)(2,1)} %param.32) | copy-start | bytes 786436
  7.3 93.0 %all-gather.8.cloned.1.call-start = ((), (), s32[]{:S(2)}) async-start(), calls=%async_computation.4 | async-start | bytes 10813440 | tf_op jit(solution)/shard_map/all_gather | solution.py:963
  10.1 233.4 %all-gather.10.cloned.1.call-start = ((), (), s32[]{:S(2)}) async-start(), calls=%async_computation.5 | async-start | bytes 19464192 | tf_op jit(solution)/shard_map/all_gather | solution.py:964
  12.1 18.5 %collective-permute-start = (s32[3]{0:T(128)S(1)}, s32[3]{0:T(128)S(1)}, u32[]{:S(2)}, u32[]{:S(2)}) collective-permute-start(s32[3]{0:T(128)S(1)} %bitcast.118), channel_id=1, source_target_pairs={{0,1},{1,2},{2,3},{3,0},{4,5},{5,6},{6,7},{7,4},{8,9},{9,10},{10,1... | collective-permute-start | bytes 44 | tf_op jit(solution)/shard_map/ppermute | solution.py:808
  13.4 17.2 %collective-permute-start.1 = (s32[3]{0:T(128)S(1)}, s32[3]{0:T(128)S(1)}, u32[]{:S(2)}, u32[]{:S(2)}) collective-permute-start(s32[3]{0:T(128)S(1)} %bitcast.119), channel_id=1, source_target_pairs={{0,2},{1,3},{2,0},{3,1},{4,6},{5,7},{6,4},{7,5},{8,10},{9,11},{10,... | collective-permute-start | bytes 44 | tf_op jit(solution)/shard_map/ppermute | solution.py:808
  14.5 16.1 %collective-permute-start.2 = (s32[3]{0:T(128)S(1)}, s32[3]{0:T(128)S(1)}, u32[]{:S(2)}, u32[]{:S(2)}) collective-permute-start(s32[3]{0:T(128)S(1)} %bitcast.120), channel_id=1, source_target_pairs={{0,3},{1,0},{2,1},{3,2},{4,7},{5,4},{6,5},{7,6},{8,11},{9,8},{10,9... | collective-permute-start | bytes 44 | tf_op jit(solution)/shard_map/ppermute | solution.py:808
  16.1 39.0 %copy-start.35 = (s32[3,1]{0,1:T(1,128)}, s32[3,1]{0,1:T(1,128)S(1)}, u32[]{:S(2)}) copy-start(s32[3,1]{0,1:T(1,128)S(1)} %reduce-window.4) | copy-start | bytes 40
  17.6 44.0 %collective-permute-start.9 = (bf16[384,1024]{1,0:T(8,128)(2,1)}, bf16[384,1024]{1,0:T(8,128)(2,1)}, u32[]{:S(2)}, u32[]{:S(2)}) collective-permute-start(bf16[384,1024]{1,0:T(8,128)(2,1)} %fusion.1.branch_ref.refs_4_), channel_id=1, source_target_pairs={{0,4},{4,0},{8,12},{12,8},{16,20},{20,16},{24,28},{28,24},{1,5},{5... | collective-permute-start | bytes 2359304 | tf_op jit(solution)/shard_map/ppermute | solution.py:803
  22.8 38.8 %collective-permute-start.10 = (bf16[2048,384]{1,0:T(8,128)(2,1)S(1)}, bf16[2048,384]{1,0:T(8,128)(2,1)S(1)}, u32[]{:S(2)}, u32[]{:S(2)}) collective-permute-start(bf16[2048,384]{1,0:T(8,128)(2,1)S(1)} %pad_maximum_fusion.refs_0_.refs_1_), channel_id=1, source_target_pairs={{0,4},{4,0},{8,12},{12,8},{16,20},{20,16},{24,28},{28,24},{1,5},{5... | collective-permute-start | bytes 4718600 | tf_op jit(solution)/shard_map/ppermute | solution.py:803
  30.8 26.9 %copy-start.38 = (s32[12]{0:T(128)}, s32[12]{0:T(128)S(1)}, u32[]{:S(2)}) copy-start(s32[12]{0:T(128)S(1)} %eq.27) | copy-start | bytes 148
  35.3 3.2 collective-permute-start.3
  35.3 9.3 %collective-permute-start.4 = (f32[4,4096]{1,0:T(4,128)S(1)}, f32[4,4096]{1,0:T(4,128)S(1)}, u32[]{:S(2)}, u32[]{:S(2)}) collective-permute-start(f32[4,4096]{1,0:T(4,128)S(1)} %get-tuple-element.90), channel_id=1, source_target_pairs={{0,2},{1,3},{2,0},{3,1},{4,6},{5,7},{6,4},{7,5},{8,10},{9,11},{10,... | collective-permute-start | bytes 196616 | tf_op jit(solution)/shard_map/ppermute | solution.py:808
  38.5 8.9 %collective-permute-start.5 = (f32[4,4096]{1,0:T(4,128)S(1)}, f32[4,4096]{1,0:T(4,128)S(1)}, u32[]{:S(2)}, u32[]{:S(2)}) collective-permute-start(f32[4,4096]{1,0:T(4,128)S(1)} %get-tuple-element.91), channel_id=1, source_target_pairs={{0,3},{1,0},{2,1},{3,2},{4,7},{5,4},{6,5},{7,6},{8,11},{9,8},{10,9... | collective-permute-start | bytes 196616 | tf_op jit(solution)/shard_map/ppermute | solution.py:808
  48.3 5.5 collective-permute-start.6
  53.8 3.9 collective-permute-start.7
  57.7 3.2 collective-permute-start.8
  61.6 38.7 %copy-start.12 = (bf16[2048,384]{1,0:T(8,128)(2,1)}, bf16[2048,384]{1,0:T(8,128)(2,1)S(1)}, u32[]{:S(2)}) copy-start(bf16[2048,384]{1,0:T(8,128)(2,1)S(1)} %collective-permute-done.10.rest_3_.refs_2_.refs_3_) | copy-start | bytes 4718596
  212.3 14.4 %all-to-all-start.1 = ((bf16[8,384,128]{2,1,0:T(8,128)(2,1)}), bf16[8,384,128]{2,1,0:T(8,128)(2,1)S(1)}, u32[]{:S(2)}, u32[]{:S(2)}) async-start(bf16[8,384,128]{2,1,0:T(8,128)(2,1)} %bitcast.103), calls=%async_computation.1 | async-start | bytes 1572864 | tf_op jit(solution)/shard_map/all_to_all | solution.py:1035
  226.7 16.7 %copy-start.24 = (bf16[8,384,128]{2,1,0:T(8,128)(2,1)}, bf16[8,384,128]{2,1,0:T(8,128)(2,1)S(1)}, u32[]{:S(2)}) copy-start(bf16[8,384,128]{2,1,0:T(8,128)(2,1)S(1)} %all-to-all-done.1.att_ref) | copy-start | bytes 2359300
  274.2 13.9 %collective-permute-start.11 = (bf16[4096,384]{1,0:T(8,128)(2,1)}, bf16[4096,384]{1,0:T(8,128)(2,1)S(1)}, u32[]{:S(2)}, u32[]{:S(2)}) collective-permute-start(bf16[4096,384]{1,0:T(8,128)(2,1)} %get-tuple-element.54.refs_0_.refs_1_), channel_id=1, source_target_pairs={{0,4},{4,0},{8,12},{12,8},{16,20},{20,16},{24,28},{28,24},{1,5},{5... | collective-permute-start | bytes 9437192 | tf_op jit(solution)/shard_map/ppermute | solution.py:803
  274.5 13.6 %collective-permute-start.13 = (bf16[384,4096]{1,0:T(8,128)(2,1)}, bf16[384,4096]{1,0:T(8,128)(2,1)}, u32[]{:S(2)}, u32[]{:S(2)}) collective-permute-start(bf16[384,4096]{1,0:T(8,128)(2,1)} %get-tuple-element.56.refs_10_), channel_id=1, source_target_pairs={{0,4},{4,0},{8,12},{12,8},{16,20},{20,16},{24,28},{28,24},{1,5},{5... | collective-permute-start | bytes 9437192 | tf_op jit(solution)/shard_map/ppermute | solution.py:803
  274.8 11.1 %collective-permute-start.12 = (bf16[1024,384]{1,0:T(8,128)(2,1)}, bf16[1024,384]{1,0:T(8,128)(2,1)}, u32[]{:S(2)}, u32[]{:S(2)}) collective-permute-start(bf16[1024,384]{1,0:T(8,128)(2,1)} %get-tuple-element.55.refs_6_.refs_7_), channel_id=1, source_target_pairs={{0,4},{4,0},{8,12},{12,8},{16,20},{20,16},{24,28},{28,24},{1,5},{5... | collective-permute-start | bytes 2359304 | tf_op jit(solution)/shard_map/ppermute | solution.py:803
  275.0 12.0 %collective-permute-start.14 = (bf16[1024,384]{1,0:T(8,128)(2,1)}, bf16[1024,384]{1,0:T(8,128)(2,1)}, u32[]{:S(2)}, u32[]{:S(2)}) collective-permute-start(bf16[1024,384]{1,0:T(8,128)(2,1)} %get-tuple-element.57.refs_12_.refs_13_), channel_id=1, source_target_pairs={{0,4},{4,0},{8,12},{12,8},{16,20},{20,16},{24,28},{28,24},{1,5},{5... | collective-permute-start | bytes 2359304 | tf_op jit(solution)/shard_map/ppermute | solution.py:803
  275.3 12.9 %collective-permute-start.15 = (bf16[384,1024]{1,0:T(8,128)(2,1)}, bf16[384,1024]{1,0:T(8,128)(2,1)}, u32[]{:S(2)}, u32[]{:S(2)}) collective-permute-start(bf16[384,1024]{1,0:T(8,128)(2,1)} %get-tuple-element.58.refs_16_), channel_id=1, source_target_pairs={{0,4},{4,0},{8,12},{12,8},{16,20},{20,16},{24,28},{28,24},{1,5},{5... | collective-permute-start | bytes 2359304 | tf_op jit(solution)/shard_map/ppermute | solution.py:803
  276.0 35.6 %all-to-all-start.2 = ((bf16[8,384,128]{2,1,0:T(8,128)(2,1)}), bf16[8,384,128]{2,1,0:T(8,128)(2,1)}, u32[]{:S(2)}, u32[]{:S(2)}) async-start(bf16[8,384,128]{2,1,0:T(8,128)(2,1)} %get-tuple-element.52), calls=%async_computation.2 | async-start | bytes 1572864 | tf_op jit(solution)/shard_map/all_to_all | solution.py:1047
  298.8 81.6 %collective-permute-start.17 = (bf16[2,4,288,512]{3,2,1,0:T(8,128)(2,1)}, bf16[2,4,288,512]{3,2,1,0:T(8,128)(2,1)}, u32[]{:S(2)}, u32[]{:S(2)}) collective-permute-start(bf16[2,4,288,512]{3,2,1,0:T(8,128)(2,1)} %outer.9.rest_1_), channel_id=1, source_target_pairs={{0,16},{4,20},{8,24},{12,28},{16,0},{20,4},{24,8},{28,12},{1,17},{... | collective-permute-start | bytes 7077896 | tf_op jit(solution)/shard_map/ppermute | solution.py:803
  309.1 71.3 %collective-permute-start.16 = (bf16[2,4,288,512]{3,2,1,0:T(8,128)(2,1)}, bf16[2,4,288,512]{3,2,1,0:T(8,128)(2,1)S(1)}, u32[]{:S(2)}, u32[]{:S(2)}) collective-permute-start(bf16[2,4,288,512]{3,2,1,0:T(8,128)(2,1)} %outer.8.rest_0_), channel_id=1, source_target_pairs={{0,8},{4,12},{8,0},{12,4},{16,24},{20,28},{24,16},{28,20},{1,9},{5... | collective-permute-start | bytes 7077896 | tf_op jit(solution)/shard_map/ppermute | solution.py:803
  381.7 30.3 %all-to-all-start.3 = ((bf16[8,3,384,128]{3,2,1,0:T(8,128)(2,1)}), bf16[8,3,384,128]{3,2,1,0:T(8,128)(2,1)S(1)}, u32[]{:S(2)}, u32[]{:S(2)}) async-start(bf16[8,3,384,128]{3,2,1,0:T(8,128)(2,1)} %tie.1), calls=%async_computation.3 | async-start | bytes 4718592 | tf_op jit(solution)/shard_map/all_to_all | solution.py:1070
  386.1 143.4 %all-gather.12.cloned.1.call-start = ((), (), s32[]{:S(2)}) async-start(), calls=%async_computation.6 | async-start | bytes 2162688 | tf_op jit(solution)/shard_map/all_gather | solution.py:1080
  424.2 10.3 %collective-permute-start.22 = (bf16[384,3072]{1,0:T(8,128)(2,1)}, bf16[384,3072]{1,0:T(8,128)(2,1)}, u32[]{:S(2)}, u32[]{:S(2)}) collective-permute-start(bf16[384,3072]{1,0:T(8,128)(2,1)} %get-tuple-element.68.refs_10_), channel_id=1, source_target_pairs={{0,4},{4,0},{8,12},{12,8},{16,20},{20,16},{24,28},{28,24},{1,5},{5... | collective-permute-start | bytes 7077896 | tf_op jit(solution)/shard_map/ppermute | solution.py:803
  427.8 6.2 %collective-permute-start.21 = (bf16[1024,384]{1,0:T(8,128)(2,1)S(1)}, bf16[1024,384]{1,0:T(8,128)(2,1)S(1)}, u32[]{:S(2)}, u32[]{:S(2)}) collective-permute-start(bf16[1024,384]{1,0:T(8,128)(2,1)S(1)} %copy-done.13), channel_id=1, source_target_pairs={{0,4},{4,0},{8,12},{12,8},{16,20},{20,16},{24,28},{28,24},{1,5},{5... | collective-permute-start | bytes 2359304 | tf_op jit(solution)/shard_map/ppermute | solution.py:803
  427.9 6.5 %collective-permute-start.20 = (bf16[384,1024]{1,0:T(8,128)(2,1)}, bf16[384,1024]{1,0:T(8,128)(2,1)S(1)}, u32[]{:S(2)}, u32[]{:S(2)}) collective-permute-start(bf16[384,1024]{1,0:T(8,128)(2,1)} %get-tuple-element.64.refs_4_.grad_ref), channel_id=1, source_target_pairs={{0,4},{4,0},{8,12},{12,8},{16,20},{20,16},{24,28},{28,24},{1,5},{5... | collective-permute-start | bytes 2359304 | tf_op jit(solution)/shard_map/ppermute | solution.py:803
  428.4 30.2 %collective-permute-start.19 = (bf16[4,288,512]{2,1,0:T(8,128)(2,1)}, bf16[4,288,512]{2,1,0:T(8,128)(2,1)}, u32[]{:S(2)}, u32[]{:S(2)}) collective-permute-start(bf16[4,288,512]{2,1,0:T(8,128)(2,1)} %get-tuple-element.63.rest_1_), channel_id=1, source_target_pairs={{0,8},{4,12},{8,0},{12,4},{16,24},{20,28},{24,16},{28,20},{1,9},{5... | collective-permute-start | bytes 3538952 | tf_op jit(solution)/shard_map/ppermute | solution.py:803
  428.7 30.0 %collective-permute-start.18 = (bf16[4,288,512]{2,1,0:T(8,128)(2,1)}, bf16[4,288,512]{2,1,0:T(8,128)(2,1)}, u32[]{:S(2)}, u32[]{:S(2)}) collective-permute-start(bf16[4,288,512]{2,1,0:T(8,128)(2,1)} %get-tuple-element.62.rest_0_), channel_id=1, source_target_pairs={{0,16},{4,20},{8,24},{12,28},{16,0},{20,4},{24,8},{28,12},{1,17},{... | collective-permute-start | bytes 3538952 | tf_op jit(solution)/shard_map/ppermute | solution.py:803
  441.4 17.2 %copy-start.2 = (bf16[2,4,160,512]{3,2,1,0:T(8,128)(2,1)S(1)}, bf16[2,4,160,512]{3,2,1,0:T(8,128)(2,1)}, u32[]{:S(2)}) copy-start(bf16[2,4,160,512]{3,2,1,0:T(8,128)(2,1)} %outer.13.refs_5_) | copy-start | bytes 3932164
  441.4 17.2 %copy-start.4 = (bf16[4,288,512]{2,1,0:T(8,128)(2,1)S(1)}, bf16[4,288,512]{2,1,0:T(8,128)(2,1)}, u32[]{:S(2)}) copy-start(bf16[4,288,512]{2,1,0:T(8,128)(2,1)} %get-tuple-element.66.refs_2_) | copy-start | bytes 3538948
  441.4 17.2 %copy-start.5 = (bf16[4,288,512]{2,1,0:T(8,128)(2,1)S(1)}, bf16[4,288,512]{2,1,0:T(8,128)(2,1)}, u32[]{:S(2)}) copy-start(bf16[4,288,512]{2,1,0:T(8,128)(2,1)} %get-tuple-element.65.refs_0_) | copy-start | bytes 3538948
  441.4 47.9 %collective-permute-start.25 = (bf16[2,4,160,512]{3,2,1,0:T(8,128)(2,1)}, bf16[2,4,160,512]{3,2,1,0:T(8,128)(2,1)}, u32[]{:S(2)}, u32[]{:S(2)}) collective-permute-start(bf16[2,4,160,512]{3,2,1,0:T(8,128)(2,1)} %outer.13.refs_5_), channel_id=1, source_target_pairs={{0,16},{4,20},{8,24},{12,28},{16,0},{20,4},{24,8},{28,12},{1,17},{... | collective-permute-start | bytes 3932168 | tf_op jit(solution)/shard_map/ppermute | solution.py:803
  448.0 49.2 %collective-permute-start.23 = (bf16[2,4,160,512]{3,2,1,0:T(8,128)(2,1)}, bf16[2,4,160,512]{3,2,1,0:T(8,128)(2,1)}, u32[]{:S(2)}, u32[]{:S(2)}) collective-permute-start(bf16[2,4,160,512]{3,2,1,0:T(8,128)(2,1)} %outer.12.refs_4_), channel_id=1, source_target_pairs={{0,8},{4,12},{8,0},{12,4},{16,24},{20,28},{24,16},{28,20},{1,9},{5... | collective-permute-start | bytes 3932168 | tf_op jit(solution)/shard_map/ppermute | solution.py:803
  464.0 40.1 %collective-permute-start.27 = (bf16[2,288,512]{2,1,0:T(8,128)(2,1)}, bf16[2,288,512]{2,1,0:T(8,128)(2,1)S(1)}, u32[]{:S(2)}, u32[]{:S(2)}) collective-permute-start(bf16[2,288,512]{2,1,0:T(8,128)(2,1)} %get-tuple-element.69.rest_0_), channel_id=1, source_target_pairs={{0,1},{1,2},{2,3},{3,0},{4,5},{5,6},{6,7},{7,4},{8,9},{9,10},{10,1... | collective-permute-start | bytes 1769480 | tf_op jit(solution)/shard_map/ppermute | solution.py:808
  465.2 55.3 %collective-permute-start.28 = (bf16[2,288,512]{2,1,0:T(8,128)(2,1)}, bf16[2,288,512]{2,1,0:T(8,128)(2,1)S(1)}, u32[]{:S(2)}, u32[]{:S(2)}) collective-permute-start(bf16[2,288,512]{2,1,0:T(8,128)(2,1)} %get-tuple-element.70.rest_1_), channel_id=1, source_target_pairs={{0,2},{1,3},{2,0},{3,1},{4,6},{5,7},{6,4},{7,5},{8,10},{9,11},{10,... | collective-permute-start | bytes 1769480 | tf_op jit(solution)/shard_map/ppermute | solution.py:808
  465.2 55.4 %collective-permute-start.29 = (bf16[2,288,512]{2,1,0:T(8,128)(2,1)}, bf16[2,288,512]{2,1,0:T(8,128)(2,1)S(1)}, u32[]{:S(2)}, u32[]{:S(2)}) collective-permute-start(bf16[2,288,512]{2,1,0:T(8,128)(2,1)} %get-tuple-element.71.rest_2_), channel_id=1, source_target_pairs={{0,3},{1,0},{2,1},{3,2},{4,7},{5,4},{6,5},{7,6},{8,11},{9,8},{10,9... | collective-permute-start | bytes 1769480 | tf_op jit(solution)/shard_map/ppermute | solution.py:808
  496.0 42.6 %collective-permute-start.26 = (bf16[4,160,512]{2,1,0:T(8,128)(2,1)}, bf16[4,160,512]{2,1,0:T(8,128)(2,1)S(1)}, u32[]{:S(2)}, u32[]{:S(2)}) collective-permute-start(bf16[4,160,512]{2,1,0:T(8,128)(2,1)} %get-tuple-element.78.rest_4_), channel_id=1, source_target_pairs={{0,8},{4,12},{8,0},{12,4},{16,24},{20,28},{24,16},{28,20},{1,9},{5... | collective-permute-start | bytes 1966088 | tf_op jit(solution)/shard_map/ppermute | solution.py:803
  503.8 34.7 %collective-permute-start.24 = (bf16[4,160,512]{2,1,0:T(8,128)(2,1)}, bf16[4,160,512]{2,1,0:T(8,128)(2,1)S(1)}, u32[]{:S(2)}, u32[]{:S(2)}) collective-permute-start(bf16[4,160,512]{2,1,0:T(8,128)(2,1)} %get-tuple-element.76.rest_3_), channel_id=1, source_target_pairs={{0,16},{4,20},{8,24},{12,28},{16,0},{20,4},{24,8},{28,12},{1,17},{... | collective-permute-start | bytes 1966088 | tf_op jit(solution)/shard_map/ppermute | solution.py:803
  539.6 7.3 %collective-permute-start.30 = (bf16[2,160,512]{2,1,0:T(8,128)(2,1)S(1)}, bf16[2,160,512]{2,1,0:T(8,128)(2,1)S(1)}, u32[]{:S(2)}, u32[]{:S(2)}) collective-permute-start(bf16[2,160,512]{2,1,0:T(8,128)(2,1)S(1)} %get-tuple-element.81), channel_id=1, source_target_pairs={{0,1},{1,2},{2,3},{3,0},{4,5},{5,6},{6,7},{7,4},{8,9},{9,10},{10,1... | collective-permute-start | bytes 983048 | tf_op jit(solution)/shard_map/ppermute | solution.py:808
  539.6 26.1 %collective-permute-start.31 = (bf16[2,160,512]{2,1,0:T(8,128)(2,1)S(1)}, bf16[2,160,512]{2,1,0:T(8,128)(2,1)S(1)}, u32[]{:S(2)}, u32[]{:S(2)}) collective-permute-start(bf16[2,160,512]{2,1,0:T(8,128)(2,1)S(1)} %get-tuple-element.82), channel_id=1, source_target_pairs={{0,2},{1,3},{2,0},{3,1},{4,6},{5,7},{6,4},{7,5},{8,10},{9,11},{10,... | collective-permute-start | bytes 983048 | tf_op jit(solution)/shard_map/ppermute | solution.py:808
  542.6 29.3 %collective-permute-start.32 = (bf16[2,160,512]{2,1,0:T(8,128)(2,1)S(1)}, bf16[2,160,512]{2,1,0:T(8,128)(2,1)S(1)}, u32[]{:S(2)}, u32[]{:S(2)}) collective-permute-start(bf16[2,160,512]{2,1,0:T(8,128)(2,1)S(1)} %get-tuple-element.83), channel_id=1, source_target_pairs={{0,3},{1,0},{2,1},{3,2},{4,7},{5,4},{6,5},{7,6},{8,11},{9,8},{10,9... | collective-permute-start | bytes 983048 | tf_op jit(solution)/shard_map/ppermute | solution.py:808
  547.0 24.9 %copy-start.28 = (bf16[2,160,512]{2,1,0:T(8,128)(2,1)}, bf16[2,160,512]{2,1,0:T(8,128)(2,1)S(1)}, u32[]{:S(2)}) copy-start(bf16[2,160,512]{2,1,0:T(8,128)(2,1)S(1)} %collective-permute-done.30.rest_0_) | copy-start | bytes 983044
  (37 other events, 186.6 us)
Sparse Core Ops, SparseCore 0:
  11.5 88.6 all-gather.7
  103.1 140.3 all-gather.9
  428.0 71.0 all-gather.11

commit v3 on v2

--- a/solution.py
+++ b/solution.py
@@ -13,6 +13,7 @@
 LANES = 128
 MASKED = -(2.0 ** 100)
 NORM_EPS = 1e-06
+SMALL = pl.CostEstimate(flops=1024, bytes_accessed=1024, transcendentals=0)
 VMEM = 60 * 1024 * 1024
 BOTH = ("seq", "batch")
 NT = (((1,), (1,)), ((), ()))
@@ -242,6 +243,60 @@
     )(ends, qkv, grad_out, out, lse, cos, sin, *after)
 
 
+def outgoing_kernel(rel_ref, grad_ref, low_ref, high_ref, *rest):
+    out_ref, total_s = rest[-2:]
+    src = pl.program_id(0)
+    rows = grad_ref.shape[2]
+    grads = jnp.concatenate([grad_ref[0, part] for part in range(3)], axis=1)
+    normed = jnp.concatenate([low_ref[0], high_ref[0]], axis=1)
+    term = mm(normed, grads, TN)
+    for part in range(3):
+        out_ref[src, part, 0:rows] = grad_ref[0, part]
+
+    @pl.when(src == 0)
+    def _():
+        total_s[...] = term
+
+    @pl.when(src > 0)
+    def _():
+        total_s[...] += term
+
+    @pl.when(src == pl.num_programs(0) - 1)
+    def _():
+        total = total_s[...].astype(jnp.bfloat16)
+        each = out_ref.shape[2] - rows
+        for dest in range(out_ref.shape[0]):
+            for part in range(3):
+                out_ref[dest, part, rows:] = total[
+                    dest * each : (dest + 1) * each, part * LANES : (part + 1) * LANES
+                ]
+
+
+def outgoing(rel, grads, halves, after):
+    sources, _, rows, _ = grads.shape
+    half = halves[0].shape[2]
+    each = 2 * half // sources
+    shape = (sources, 3, rows + each, LANES)
+    side = pl.BlockSpec((1, rows, half), lambda i, rel: (rel[i], 0, 0))
+    return pl.pallas_call(
+        outgoing_kernel,
+        grid_spec=pltpu.PrefetchScalarGridSpec(
+            num_scalar_prefetch=1,
+            grid=(sources,),
+            in_specs=[pl.BlockSpec((1, 3, rows, LANES), lambda i, rel: (i, 0, 0, 0)), side, side]
+            + [pl.BlockSpec(memory_space=pl.ANY)] * len(after),
+            out_specs=pl.BlockSpec(shape, lambda i, rel: (0, 0, 0, 0)),
+            scratch_shapes=[pltpu.VMEM((2 * half, 3 * LANES), jnp.float32)],
+        ),
+        out_shape=jax.ShapeDtypeStruct(shape, jnp.bfloat16),
+        cost_estimate=pl.CostEstimate(
+            flops=12 * rows * sources * half * LANES, bytes_accessed=16 * half * half, transcendentals=0
+        ),
+        compiler_params=pltpu.CompilerParams(vmem_limit_bytes=VMEM),
+        name="outgoing",
+    )(rel, grads, *halves, *after)
+
+
 def unjoin_kernel(grad_ref, weight_ref, *rest):
     width = grad_ref.shape[1]
     i = pl.program_id(0)
@@ -318,20 +373,19 @@
     return value, slope
 
 
-def front_kernel(frames_ref, skip_ref, info_ref, mod_ref, wskip_ref, wqkv_ref, cos_ref, sin_ref,
-                 *rest, utts, steps, parts):
-    stream_ref, out_ref, flipped_ref, normed_ref = rest[-4:]
+def front_kernel(frames_ref, skip_ref, info_ref, mod_ref, weight_ref, *rest, utts, steps):
+    stream_ref, normed_low_ref, normed_high_ref = rest[-3:]
     i = pl.program_id(0)
     width = stream_ref.shape[1]
-    weight = wskip_ref[...].reshape(-1, width)
+    half = width // 2
+    weight = weight_ref[...].reshape(-1, width)
     depth = weight.shape[0]
 
     for n in range(steps):
         @pl.when(i == n)
         def _(n=n):
-            at = n * depth
-            source = frames_ref if at < width else skip_ref
-            at = at % width
+            source = frames_ref if n * depth < width else skip_ref
+            at = n * depth % width
             term = mm(source[:, at : at + depth], weight, NN)
             stream_ref[...] = term if n == 0 else stream_ref[...] + term
 
@@ -342,72 +396,80 @@
         scale = per_row(info, 1.0 + mod_ref[:, :width], utts)
         shift = per_row(info, mod_ref[:, width : 2 * width], utts)
         normed = (unit * scale + shift).astype(jnp.bfloat16)
-        normed_ref[...] = normed
-        flipped_ref[...] = normed.T
-
-    @pl.when(i >= steps)
-    def _():
-        part = (i - steps) // parts
-        w = wqkv_ref[...].reshape(width, -1)
-        turned = mm(normed_ref[...], w, NN)
-        lane = lax.broadcasted_iota(jnp.int32, (turned.shape[0], LANES), 1)
-        first = (lane % HD) < HD // 2
-        scale = jnp.where(part == 0, HD ** -0.5, 1.0)
-        for at in range(out_ref.shape[0]):
-            x = turned[:, at * LANES : (at + 1) * LANES]
-            partner = jnp.where(first, pltpu.roll(x, LANES - HD // 2, 1), pltpu.roll(x, HD // 2, 1))
-            rotated = (x * cos_ref[...] + partner * sin_ref[...]) * scale
-            out_ref[at, 0] = jnp.where(part == 2, x, rotated).astype(jnp.bfloat16)
-
-
-def front(frames, skip, info, modulation, early, skip_each, qkv_each, cos, sin, utts, after):
+        normed_low_ref[...] = normed[:, :half]
+        normed_high_ref[...] = normed[:, half:]
+
+
+def front(frames, skip, info, modulation, weights, utts, after):
     rows, width = frames.shape
-    devices = early.shape[0]
-    steps, parts = 4, 4
-    targets = width // LANES
-    each = targets // parts
-    first = skip_each // qkv_each
+    devices, each, _ = weights.shape
+    half = width // 2
+    steps = 4
 
     def fixed(*shape):
         return pl.BlockSpec(shape, lambda i: (0,) * len(shape))
 
-    def later(i):
-        return jnp.maximum(i - steps, 0)
-
     return pl.pallas_call(
-        functools.partial(front_kernel, utts=utts, steps=steps, parts=parts),
-        grid=(steps + 3 * parts,),
-        out_shape=(
-            jax.ShapeDtypeStruct((rows, width), jnp.float32),
-            jax.ShapeDtypeStruct((targets, 3, rows, LANES), jnp.bfloat16),
-            jax.ShapeDtypeStruct((width, rows), jnp.bfloat16),
-        ),
+        functools.partial(front_kernel, utts=utts, steps=steps),
+        grid=(steps,),
         in_specs=[
             fixed(rows, width),
             fixed(rows, width),
             fixed(rows, LANES),
             fixed(utts, 4 * width),
-            pl.BlockSpec((devices // steps, skip_each, width), lambda i: (jnp.minimum(i, steps - 1), 0, 0)),
-            pl.BlockSpec(
-                (devices, qkv_each, each * LANES),
-                lambda i: (0, first + later(i) // parts, later(i) % parts),
-            ),
-            fixed(rows, LANES),
-            fixed(rows, LANES),
+            pl.BlockSpec((devices // steps, each, width), lambda i: (i, 0, 0)),
         ]
         + [pl.BlockSpec(memory_space=pl.ANY)] * len(after),
-        out_specs=(
-            fixed(rows, width),
-            pl.BlockSpec((each, 1, rows, LANES), lambda i: (later(i) % parts, later(i) // parts, 0, 0)),
-            fixed(width, rows),
-        ),
-        scratch_shapes=[pltpu.VMEM((rows, width), jnp.bfloat16)],
+        out_specs=(fixed(rows, width), fixed(rows, half), fixed(rows, half)),
+        out_shape=(
+            jax.ShapeDtypeStruct((rows, width), jnp.float32),
+            jax.ShapeDtypeStruct((rows, half), jnp.bfloat16),
+            jax.ShapeDtypeStruct((rows, half), jnp.bfloat16),
+        ),
         compiler_params=pltpu.CompilerParams(vmem_limit_bytes=VMEM),
         cost_estimate=pl.CostEstimate(
-            flops=16 * rows * width * width, bytes_accessed=20 * width * width, transcendentals=0
+            flops=4 * rows * width * width, bytes_accessed=8 * width * width, transcendentals=0
         ),
         name="front",
-    )(frames, skip, info, modulation, early, early, cos, sin, *after)
+    )(frames, skip, info, modulation, weights, *after)
+
+
+def project_kernel(rel_ref, low_ref, high_ref, weight_ref, cos_ref, sin_ref, *rest):
+    out_ref = rest[-1]
+    normed = jnp.concatenate([low_ref[0], high_ref[0]], axis=1)
+    turned = mm(normed, weight_ref[...], NN)
+    lane = lax.broadcasted_iota(jnp.int32, (turned.shape[0], LANES), 1)
+    first = (lane % HD) < HD // 2
+    for part in range(3):
+        x = turned[:, part * LANES : (part + 1) * LANES]
+        if part < 2:
+            partner = jnp.where(first, pltpu.roll(x, LANES - HD // 2, 1), pltpu.roll(x, HD // 2, 1))
+            x = x * cos_ref[...] + partner * sin_ref[...]
+        if part == 0:
+            x = x * HD ** -0.5
+        out_ref[0, part] = x.astype(jnp.bfloat16)
+
+
+def project(rel, halves, weight, cos, sin, after):
+    sources, rows, half = halves[0].shape
+    side = pl.BlockSpec((1, rows, half), lambda i, rel: (rel[i], 0, 0))
+    table = pl.BlockSpec((rows, LANES), lambda i, rel: (i, 0))
+    return pl.pallas_call(
+        project_kernel,
+        grid_spec=pltpu.PrefetchScalarGridSpec(
+            num_scalar_prefetch=1,
+            grid=(sources,),
+            in_specs=[side, side, pl.BlockSpec(weight.shape, lambda i, rel: (0, 0)), table, table]
+            + [pl.BlockSpec(memory_space=pl.ANY)] * len(after),
+            out_specs=pl.BlockSpec((1, 3, rows, LANES), lambda i, rel: (i, 0, 0, 0)),
+        ),
+        out_shape=jax.ShapeDtypeStruct((sources, 3, rows, LANES), jnp.bfloat16),
+        compiler_params=pltpu.CompilerParams(vmem_limit_bytes=VMEM),
+        cost_estimate=pl.CostEstimate(
+            flops=12 * rows * sources * half * LANES, bytes_accessed=16 * half * half, transcendentals=0
+        ),
+        name="project",
+    )(rel, *halves, weight, cos, sin, *after)
 
 
 def middle_kernel(att_ref, stream_ref, info_ref, mod_ref, branch_ref, wout_ref, wup_ref, wdown_ref, bias_ref,
@@ -550,13 +612,13 @@
 
 def tail_kernel(held_ref, stream_ref, info_ref, mod_ref, mid_ref, w_ref, two_ref, bup_ref,
                 *rest, utts):
-    proj_ref, out_ref, sums_ref, gn_s = rest[-4:]
+    out_ref, sums_ref, proj_s, gn_s = rest[-4:]
     p = pl.program_id(0)
     rows, width = stream_ref.shape
     groups = held_ref.shape[0]
     for s in range(groups):
-        proj_ref[:, s * LANES : (s + 1) * LANES] = held_ref[s, 0]
-    term = mm(proj_ref[...], w_ref[...].reshape(width, width), NT)
+        proj_s[:, s * LANES : (s + 1) * LANES] = held_ref[s, 0]
+    term = mm(proj_s[...], w_ref[...].reshape(width, width), NT)
 
     @pl.when(p == 0)
     def _():
@@ -592,7 +654,6 @@
         functools.partial(tail_kernel, utts=utts),
         grid=(3,),
         out_shape=(
-            jax.ShapeDtypeStruct((rows, 3 * width), jnp.bfloat16),
             jax.ShapeDtypeStruct((rows, width), jnp.bfloat16),
             jax.ShapeDtypeStruct((utts + 1, 4 * width), jnp.float32),
         ),
@@ -608,11 +669,13 @@
         ]
         + [pl.BlockSpec(memory_space=pl.ANY)] * len(after),
         out_specs=(
-            pl.BlockSpec((rows, width), lambda p: (0, p)),
             fixed(rows, width),
             fixed(utts + 1, 4 * width),
         ),
-        scratch_shapes=[pltpu.VMEM((rows, width), jnp.float32)],
+        scratch_shapes=[
+            pltpu.VMEM((rows, width), jnp.bfloat16),
+            pltpu.VMEM((rows, width), jnp.float32),
+        ],
         compiler_params=pltpu.CompilerParams(vmem_limit_bytes=VMEM),
         cost_estimate=pl.CostEstimate(
             flops=6 * rows * width * width, bytes_accessed=14 * width * width, transcendentals=0
@@ -729,53 +792,87 @@
     )(picks, *operands, *(() if add is None else (add,)), *after)
 
 
-def merge_kernel(at_ref, *refs, sums, count):
-    outs = refs[len(refs) - count :]
-    for n in range(count):
-        z = lax.rem(at_ref[0] + n, count)
+def merge_kernel(*refs, sums, held):
+    out = refs[-1]
+    batch, height, wide = refs[0].shape
+    for z in range(batch):
         for h in range(sums):
             total = refs[2 * h][z].astype(jnp.float32) + refs[2 * h + 1][z].astype(jnp.float32)
-            outs[n][h] = total.astype(jnp.bfloat16)
-
-
-def merge(pairs, after):
+            out[z, h, 0:height] = total.astype(jnp.bfloat16)
+    if held:
+        held_ref = refs[2 * sums]
+        groups, _, rows, _ = held_ref.shape
+        each = rows // batch
+        blocks = 3 * groups * LANES // wide // sums
+        for z in range(batch):
+            for part in range(3):
+                for g in range(groups):
+                    low = (part * groups + g) * LANES
+                    h, j = divmod(low // wide, blocks)
+                    at = height + j * each
+                    out[z, h, at : at + each, low % wide : low % wide + LANES] = held_ref[
+                        g, part, z * each : (z + 1) * each
+                    ]
+
+
+def merge(pairs, held, rows, after):
     batch, height, wide = pairs[0][0].shape
-    at = lax.axis_index("batch").reshape(1).astype(jnp.int32)
     vmem = pl.BlockSpec(memory_space=pltpu.VMEM)
     sums = len(pairs)
-    size = sums * batch * height * wide
-    return list(pl.pallas_call(
-        functools.partial(merge_kernel, sums=sums, count=batch),
-        out_shape=[jax.ShapeDtypeStruct((sums, height, wide), jnp.bfloat16)] * batch,
-        in_specs=[pl.BlockSpec(memory_space=pltpu.SMEM)]
-        + [vmem] * (2 * sums)
-        + [pl.BlockSpec(memory_space=pl.ANY)] * len(after),
-        out_specs=[vmem] * batch,
-        cost_estimate=pl.CostEstimate(flops=size, bytes_accessed=6 * size, transcendentals=0),
-        compiler_params=pltpu.CompilerParams(vmem_limit_bytes=VMEM // 2),
+    operands = [one for pair in pairs for one in pair]
+    specs = [pl.BlockSpec((batch, height, wide), lambda i: (0, 0, 0))] * (2 * sums)
+    if held is not None:
+        groups, _, total_rows, _ = held.shape
+        more = total_rows - rows
+        if rows % more:
+            held = held[:, :, rows:]
+            rows = 0
+        at = rows // more
+        operands.append(held)
+        specs.append(pl.BlockSpec((groups, 3, more, LANES), lambda i: (0, 0, at, 0)))
+        height += 3 * groups * LANES // wide // sums * (more // batch)
+    shape = (batch, sums, height, wide)
+    return pl.pallas_call(
+        functools.partial(merge_kernel, sums=sums, held=held is not None),
+        grid=(1,),
+        out_shape=jax.ShapeDtypeStruct(shape, jnp.bfloat16),
+        in_specs=specs + [pl.BlockSpec(memory_space=pl.ANY)] * len(after),
+        out_specs=pl.BlockSpec(shape, lambda i: (0, 0, 0, 0)),
+        cost_estimate=SMALL,
+        compiler_params=pltpu.CompilerParams(vmem_limit_bytes=VMEM),
         name="merge",
-    )(at, *[one for pair in pairs for one in pair], *after))
-
-
-def finish_kernel(own_ref, *rest, count):
-    total = own_ref[...].astype(jnp.float32)
-    for n in range(count):
-        total = total + rest[n][...].astype(jnp.float32)
-    rest[-1][...] = total
-
-
-def finish(own, came, after):
+    )(*operands, *after)
+
+
+def finish_kernel(came_ref, *rest, sizes, counts):
+    outs = rest[len(rest) - len(sizes) :]
+    batch, halves, _, wide = came_ref.shape
+    for h in range(halves):
+        at = 0
+        for out, each, blocks in zip(outs, sizes, counts):
+            for j in range(blocks):
+                total = came_ref[0, h, at : at + each].astype(jnp.float32)
+                for z in range(1, batch):
+                    total = total + came_ref[z, h, at : at + each].astype(jnp.float32)
+                low = (h * blocks + j) * wide
+                out[:, low : low + wide] = total
+                at += each
+
+
+def finish(came, sizes, counts, after):
     vmem = pl.BlockSpec(memory_space=pltpu.VMEM)
+    _, halves, _, wide = came.shape
     return pl.pallas_call(
-        functools.partial(finish_kernel, count=len(came)),
-        out_shape=jax.ShapeDtypeStruct(own.shape, jnp.float32),
-        in_specs=[vmem] * (1 + len(came)) + [pl.BlockSpec(memory_space=pl.ANY)] * len(after),
-        out_specs=vmem,
-        cost_estimate=pl.CostEstimate(
-            flops=4 * own.size, bytes_accessed=12 * own.size, transcendentals=0
-        ),
+        functools.partial(finish_kernel, sizes=sizes, counts=counts),
+        out_shape=[
+            jax.ShapeDtypeStruct((each, halves * count * wide), jnp.float32)
+            for each, count in zip(sizes, counts)
+        ],
+        in_specs=[vmem] + [pl.BlockSpec(memory_space=pl.ANY)] * len(after),
+        out_specs=[vmem] * len(sizes),
+        cost_estimate=SMALL,
         name="finish",
-    )(own, *came, *after)
+    )(came, *after)
 
 
 def tie_kernel(*refs):
@@ -859,36 +956,35 @@
         return sum([one.send(after) for one in self.halves], [])
 
     def came(self):
-        return [one.came for one in self.halves]
-
-    def keep(self, after=()):
+        return jax.tree.leaves([one.came for one in self.halves])
+
+    def keep(self, after=(), after_last=()):
         for one in self.halves:
-            one.keep(after)
+            one.keep(tuple(after) + (tuple(after_last) if one is self.halves[-1] else ()))
         return sum([one.pass_on() for one in self.halves], [])
 
-    def spread(self, after=()):
+    def spread(self, after=(), held=None, rows=0):
         for one in self.halves:
             while one.next < len(one.bits):
                 one.take()
                 one.pass_on()
-        pieces = merge([(one.total[0], one.came[0]) for one in self.halves], tuple(after))
-        self.own = pieces[0]
-        self.pieces = [ahead(piece, step) for step, piece in enumerate(pieces) if step]
-        return pieces[1:]
+        pieces = merge(
+            [(one.total[0], one.came[0]) for one in self.halves], held, rows, tuple(after)
+        )
+        self.spread_out = lax.all_to_all(pieces, "batch", 0, 0, tiled=True)
+        self.held = held
+        self.rows = rows
+        return [pieces]
 
     def result(self, after=()):
-        total = finish(self.own, self.pieces, tuple(after))
         devices = lax.axis_size("seq") * lax.axis_size("batch")
-        made = []
-        at = 0
-        for first, _, second, _ in self.weights:
-            each = first.shape[0] // devices
-            columns = second.shape[1] // 2
-            count = columns // Sum.wide
-            piece = total[:, at : at + each * count].reshape(2, count, each, Sum.wide)
-            made.append(piece.transpose(2, 0, 1, 3).reshape(each, 2 * columns))
-            at += each * count
-        return made
+        sizes = [first.shape[0] // devices for first, _, _, _ in self.weights]
+        counts = [second.shape[1] // 2 // Sum.wide for _, _, second, _ in self.weights]
+        if self.held is not None:
+            groups, _, height, _ = self.held.shape
+            sizes.append((height - self.rows) // lax.axis_size("batch"))
+            counts.append(3 * groups * LANES // 2 // Sum.wide)
+        return finish(self.spread_out, sizes, counts, tuple(after))
 
 
 def turn_tables(position):
@@ -910,6 +1006,15 @@
             out, ahead(value, step), (place - step) % batch, 0
         )
     return out
+
+
+def seq_pieces(value, bits):
+    have = []
+    for bit in bits:
+        came = swap(value, bit)
+        value = jnp.stack([value, came], axis=sum(b > bit for b in have))
+        have.append(bit)
+    return value.reshape((lax.axis_size("seq"),) + value.shape[len(have) :])
 
 
 def seq_total(value):
@@ -952,16 +1057,10 @@
     heads = HEADS // seq
     utts = lengths.shape[1]
 
-    early = jnp.concatenate(
-        [skip_proj] + [qkv_proj[:, p * width : (p + 1) * width] for p in range(3)], axis=0
-    )
-    late = jnp.concatenate(
-        [down_proj, out_proj]
-        + [up_proj[:, p * width : (p + 1) * width] for p in range(hidden // width)],
-        axis=0,
-    )
-    early = lax.all_gather(early, BOTH, axis=0, tiled=False)
-    late = lax.all_gather(late, BOTH, axis=0, tiled=False)
+    high = [seq >> (i + 1) for i in range(seq.bit_length() - 2)]
+    low = high[::-1]
+    rel = (jnp.arange(seq, dtype=jnp.int32) ^ seq_at).astype(jnp.int32)
+    half = width // 2
     skip_each, qkv_each, out_each, up_each, down_each = (
         skip_proj.shape[0],
         qkv_proj.shape[0],
@@ -969,6 +1068,22 @@
         up_proj.shape[0],
         down_proj.shape[0],
     )
+    per_device = width // seq
+    groups = width // LANES
+    full_skip = lax.all_gather(skip_proj, BOTH, axis=0, tiled=False)
+    own_qkv = all_pieces(qkv_proj).reshape(batch, qkv_each, 3, seq, per_device)
+    own_qkv = lax.all_to_all(own_qkv.transpose(3, 2, 0, 1, 4), "seq", 0, 0, tiled=True)
+    own_qkv = jnp.pad(own_qkv, ((0, 0),) * 4 + ((0, LANES - per_device),))
+    own_qkv = own_qkv.transpose(0, 2, 3, 1, 4).reshape(width, 3 * LANES)
+    late = jnp.concatenate(
+        [down_proj, out_proj]
+        + [up_proj[:, p * width : (p + 1) * width] for p in range(hidden // width)],
+        axis=0,
+    )
+    late = lax.all_gather(late, BOTH, axis=0, tiled=False)
+    full_qkv = jnp.concatenate([qkv_proj[:, p * width : (p + 1) * width] for p in range(3)], axis=0)
+    full_qkv = lax.all_gather(full_qkv, BOTH, axis=0, tiled=False)
+
     utt_lengths = lengths[0]
     ends = jnp.cumsum(utt_lengths).astype(jnp.int32)
     starts = ends - utt_lengths
@@ -986,7 +1101,6 @@
     in_span = ((position >= span_first) & (position < span_after)).astype(jnp.float32)
     member_rows = member.astype(jnp.float32)
     group_position = group_ids - jnp.sum(members(group_ids).astype(jnp.int32) * starts[None, :], axis=1)
-    cos, sin = turn_tables(position)
     group_cos, group_sin = turn_tables(group_position)
 
     steps = all_pieces(timestep[0]).reshape(-1)
@@ -1019,18 +1133,12 @@
     branch_pair = (branch, swap(branch, 1))
     joined_pair = (joined, swap(joined, 1))
 
-    stream_in, sent, normed_one = front(
-        inputs, skip_rows, info, modulation, early, skip_each, qkv_each, cos, sin, utts,
-        (group_cos, group_sin, branch_pair[1], joined_pair[1]),
+    stream_in, *normed_one = front(
+        inputs, skip_rows, info, modulation, full_skip, utts,
+        (group_cos, group_sin, own_qkv, branch_pair[1], joined_pair[1]),
     )
-    per_device = width // seq
-    groups = width // LANES
-    if per_device < LANES:
-        sent = sent.reshape(groups, 3, rows, 2, per_device).transpose(0, 3, 1, 2, 4)
-        sent = sent.reshape(seq, 3, rows, per_device)
-        sent = jnp.pad(sent, ((0, 0), (0, 0), (0, 0), (0, LANES - per_device)))
-    held = lax.all_to_all(sent, "seq", 0, 0, tiled=True)
-    normed_one_pair = (normed_one, swap(normed_one, 1))
+    normed_halves = [seq_pieces(normed_one[0], low + [1]), seq_pieces(normed_one[1], high + [1])]
+    held = project(rel, normed_halves, own_qkv, group_cos, group_sin, ())
     head_out, log_sums = attend(held, ends, heads, 1024, 512)
     att = lax.all_to_all(
         head_out.reshape(seq, rows, LANES)[:, :, :per_device], "seq", 0, 0, tiled=True
@@ -1045,8 +1153,6 @@
         back = back.reshape(groups, rows, 2, per_device).transpose(0, 2, 1, 3).reshape(seq, rows, per_device)
         back = jnp.pad(back, ((0, 0), (0, 0), (0, LANES - per_device)))
     back = lax.all_to_all(back, "seq", 0, 0, tiled=True).reshape(frames, LANES)
-    high = [seq >> (i + 1) for i in range(seq.bit_length() - 2)]
-    low = high[::-1]
 
     def pairs(first, second):
         return (first[0], first[1], second[0], second[1])
@@ -1065,33 +1171,34 @@
     grad_held = attend_back(
         held, back, head_out, log_sums, group_cos, group_sin, ends, heads, waits, 1024, 512
     )
+    grad_held = outgoing(rel, grad_held, normed_halves, tuple(sums.came()))
     mark = (grad_held,)
-    grad_held = tie(grad_held, sums.came())
     grad_held = lax.all_to_all(grad_held[..., :per_device], "seq", 0, 0, tiled=True)
     if per_device < LANES:
-        grad_held = grad_held.reshape(groups, 2, 3, rows, per_device).transpose(0, 2, 3, 1, 4)
-        grad_held = grad_held.reshape(groups, 3, rows, LANES)
-    waits = sums.keep(mark)
-
-    grad_projected, grad_stream, row_sums = tail(
-        grad_held, stream_in, info, modulation, grad_mid, early, skip_each, qkv_each,
+        grad_held = grad_held.reshape(groups, 2, 3, -1, per_device).transpose(0, 2, 3, 1, 4)
+        grad_held = grad_held.reshape(groups, 3, -1, LANES)
+    sums.keep(mark)
+    waits = sums.spread((), grad_held, rows)
+
+    grad_stream, row_sums = tail(
+        grad_held, stream_in, info, modulation, grad_mid, full_qkv, 0, qkv_each,
         mod_two, bup_terms, utts, waits,
     )
-    row_sums = lax.all_gather(row_sums, BOTH, axis=0, tiled=False)
-    last_weights = [
-        pairs(joined_pair, pair(grad_stream)),
-        pairs(normed_one_pair, pair(grad_projected)),
-    ]
-    last_sums = Sums(last_weights, (low, high))
-    waits = last_sums.send()
-    waits = sums.spread(waits)
-    grad_inputs, grad_skip_rows = unjoin(grad_stream, early, skip_each, waits)
-    waits = last_sums.keep((grad_inputs,))
-    grad_down, grad_up, grad_out_w = sums.result(waits)
-    last_sums.spread((grad_down,))
-    grad_skip_w, grad_qkv_w = last_sums.result()
-
-    row_sums = jnp.sum(row_sums.reshape(seq, batch, utts + 1, 4 * width), axis=0)
+    last_sums = Sums([pairs(joined_pair, pair(grad_stream))], (low, high))
+    row_sums = row_sums + swap(row_sums, 1)
+    waits = last_sums.send((row_sums,))
+    row_sums = tie(row_sums, waits)
+    row_sums = row_sums + swap(row_sums, 2)
+    grad_inputs, grad_skip_rows = unjoin(grad_stream, full_skip, skip_each, waits)
+    waits = last_sums.keep((grad_inputs,), (row_sums,))
+    row_sums = tie(row_sums, waits)
+    for bit in low[1:]:
+        row_sums = row_sums + swap(row_sums, bit)
+    waits = last_sums.spread((row_sums, sums.spread_out))
+    row_sums = all_pieces(tie(row_sums, waits))
+    grad_down, grad_up, grad_out_w, grad_qkv_w = sums.result(waits)
+    (grad_skip_w,) = last_sums.result()
+
     grad_modulation = row_sums[:, :utts].reshape(batch * utts, 4 * width)
     grad_bup = lax.dynamic_slice_in_dim(
         jnp.sum(row_sums[:, utts], axis=0), device * up_bias.shape[0], up_bias.shape[0]

time: 596 us -> 557 us (0.935)
  the two profiles are of different devices: /device:TPU:9 before, /device:TPU:0 now
where the time goes in v3:
time: 557 us; the launch traced here: 551 us
  Pallas kernels  250 us (45%)
  waiting for transfers between devices  161 us (29%)
  starting transfers between devices  63.9 us (11%)
  local copies, waits for them, and re-layouts  37 us (7%)
  other arithmetic  21.9 us (4%)
  between operations  14.6 us (3%)
    ppermute x28, waiting for transfers between devices, swap(): return lax.ppermute(value, 'seq', [(i, i ^ bit) for i in range(size)])  112 us
    pallas_call x1, Pallas kernels, attend_back(): pl.pallas_call(functools.partial(bwd_kernel, heads=heads, utts=utts, bq=b...  65.4 us
    pallas_call x8, Pallas kernels, outer(): pl.pallas_call(functools.partial(outer_kernel, sizes=sizes, counts=counts...  52.1 us
    pallas_call x1, Pallas kernels, attend(): pl.pallas_call(functools.partial(fwd_kernel, heads=heads, utts=utts, bq=b...  44.1 us
    pallas_call x1, Pallas kernels, middle(): pl.pallas_call(functools.partial(middle_kernel, utts=utts, blocks=blocks)...  30.6 us
    ppermute x28, starting transfers between devices, swap(): return lax.ppermute(value, 'seq', [(i, i ^ bit) for i in range(size)])  22.6 us
    all_to_all x2, waiting for transfers between devices, spread(): self.spread_out = lax.all_to_all(pieces, 'batch', 0, 0, tiled=True)  19.7 us
    unnamed x71, local copies, waits for them, and re-layouts  18.1 us
  transfers between devices with their start and end apart: 49, of which 23 were waited for; matrix products, arithmetic and copies ran while one was open for 9% of the time, Pallas kernels for 39%

profile of v3, /device:TPU:0, one launch (start us, length us, event | category | flops | bytes accessed | tf_op | source)
XLA Modules:
  0.0 551.0 jit_solution(15225001411633170672)
XLA Ops:
  14.1 3.1 collective-permute-start.9
  17.2 2.6 collective-permute-start.10
  21.7 1.9 collective-permute-start.2
  30.8 4.7 collective-permute-done.1
  40.6 2.4 collective-permute-done.3
  49.7 2.9 collective-permute-done.11
  55.6 4.7 all-to-all-start
  60.4 7.8 %fusion = (f32[3072,128]{1,0:T(8,128)}, f32[3072,128]{1,0:T(8,128)}) fusion(f32[128]{0:T(128)} %get-tuple-element.95, f32[128]{0:T(128)} %get-tuple-element.96, f32[3072]{0:T(1024)S(1)} %subtract_convert_fusion), kind=kLoop, calls=%fused_computation.5 | loop fusion | flops 786432 | bytes 3159040 | tf_op jit(solution)/shard_map/mul | solution.py:996
  68.2 2.0 collective-permute-start.7
  70.4 10.4 %collective-permute-done.7 = f32[4,4096]{1,0:T(4,128)S(1)} collective-permute-done((f32[4,4096]{1,0:T(4,128)S(1)}, f32[4,4096]{1,0:T(4,128)S(1)}, u32[]{:S(2)}, u32[]{:S(2)}) %collective-permute-start.7) | collective-permute-done | bytes 65568 | tf_op jit(solution)/shard_map/ppermute | solution.py:900
  83.1 2.1 collective-permute-done.8
  89.9 7.3 %front.1 = (f32[384,1024]{1,0:T(8,128)}, bf16[384,512]{1,0:T(8,128)(2,1)}, bf16[384,512]{1,0:T(8,128)(2,1)}) custom-call(bf16[384,1024]{1,0:T(8,128)(2,1)} %bitcast.110, bf16[384,1024]{1,0:T(8,128)(2,1)} %bitcast.111, f32[384,128]{1,0:T(8,128)} %pad_convert_fusion.info_ref, f32[3,4096]{1,0:T(4,128)} %bitcast.120, bf16[32,64,1024]{2,1,0:T(8,128)(2,1)} %bitcast.103, ...), custom_call_target="tpu_custom_call" | custom-call | flops 1610612736 | bytes 8388608 | tf_op jit(solution)/shard_map/front/pallas_call | solution.py:412
  99.3 12.6 %collective-permute-done.17 = bf16[384,512]{1,0:T(8,128)(2,1)S(1)} collective-permute-done((bf16[384,512]{1,0:T(8,128)(2,1)}, bf16[384,512]{1,0:T(8,128)(2,1)S(1)}, u32[]{:S(2)}, u32[]{:S(2)}) %collective-permute-start.17) | collective-permute-done | bytes 393248 | tf_op jit(solution)/shard_map/ppermute | solution.py:900
  115.5 24.1 %collective-permute-done.18 = bf16[2,384,512]{2,1,0:T(8,128)(2,1)S(1)} collective-permute-done((bf16[2,384,512]{2,1,0:T(8,128)(2,1)S(1)}, bf16[2,384,512]{2,1,0:T(8,128)(2,1)S(1)}, u32[]{:S(2)}, u32[]{:S(2)}) %collective-permute-start.18) | collective-permute-done | bytes 786464 | tf_op jit(solution)/shard_map/ppermute | solution.py:900
  139.9 2.2 collective-permute-done.15
  147.9 11.1 %project.1.qkv_ref = bf16[8,3,384,128]{3,2,1,0:T(8,128)(2,1)} custom-call(s32[8]{0:T(128)} %iota_xor_fusion.rel_ref, bf16[8,384,512]{2,1,0:T(8,128)(2,1)} %bitcast.101, bf16[8,384,512]{2,1,0:T(8,128)(2,1)} %bitcast.99, bf16[1024,384]{1,0:T(8,128)(2,1)} %bitcast.106, f32[3072,128]{1,0:T(8,128)} %get-tuple-element.94.rest_0_.cos_ref, ...), custom_call_target="tpu_custom_call" | custom-call | flops 2415919104 | bytes 4194304 | tf_op jit(solution)/shard_map/project/pallas_call | solution.py:457
  159.0 44.1 %attend.1 = (bf16[3072,128]{1,0:T(8,128)(2,1)}, f32[3072,128]{1,0:T(8,128)}) custom-call(s32[3]{0:T(128)} %bitcast.129, bf16[8,3,384,128]{3,2,1,0:T(8,128)(2,1)} %project.1.qkv_ref), custom_call_target="tpu_custom_call" | custom-call | flops 48318382080 | bytes 4718592 | tf_op jit(solution)/shard_map/attend/pallas_call | solution.py:117
  203.1 3.6 all-to-all-start.1
  208.3 10.9 %all-to-all-done.1.att_ref = bf16[8,384,128]{2,1,0:T(8,128)(2,1)S(1)} async-done(((bf16[8,384,128]{2,1,0:T(8,128)(2,1)}), bf16[8,384,128]{2,1,0:T(8,128)(2,1)S(1)}, u32[]{:S(2)}, u32[]{:S(2)}) %all-to-all-start.1) | async-done | bytes 786464 | tf_op jit(solution)/shard_map/all_to_all | solution.py:1143
  219.2 5.2 all-gather.9.cloned.1.call-done
  224.5 30.6 %middle.1 = (bf16[384,1024]{1,0:T(8,128)(2,1)}, bf16[1024,384]{1,0:T(8,128)(2,1)}, bf16[1024,384]{1,0:T(8,128)(2,1)}, bf16[4096,384]{1,0:T(8,128)(2,1)}, bf16[38...) custom-call(bf16[8,384,128]{2,1,0:T(8,128)(2,1)} %copy-done.14, ...), custom_call_target="tpu_custom_call" | custom-call | flops 19327352832 | bytes 20971520 | tf_op jit(solution)/shard_map/middle/pallas_call | solution.py:557
  258.6 4.4 all-to-all-start.2
  263.6 3.2 collective-permute-done.21.refs_8_.refs_9_
  270.8 9.1 %outer.9.rest_1_ = bf16[2,4,288,512]{3,2,1,0:T(8,128)(2,1)} custom-call(s32[2]{0:T(128)} %fusion.31.pick_ref, bf16[4096,384]{1,0:T(8,128)(2,1)} %get-tuple-element.50.refs_0_.refs_1_, bf16[4096,384]{1,0:T(8,128)(2,1)} %get-tuple-element.50.refs_0_.refs_1_, bf16[4096,384]{1,0:T(8,128)(2,1)} %copy-done.1, bf16[4096,384]{1,0:T(8,128)(2,1)} %copy-done.1, ...), custom_call_target="tpu_custom_call" | custom-call | flops 3623878656 | bytes 6039797 | tf_op jit(solution)/shard_map/outer/pallas_call | solution.py:775
  281.4 9.1 %outer.8.rest_0_ = bf16[2,4,288,512]{3,2,1,0:T(8,128)(2,1)} custom-call(s32[2]{0:T(128)} %fusion.33.pick_ref, bf16[4096,384]{1,0:T(8,128)(2,1)} %get-tuple-element.50.refs_0_.refs_1_, bf16[4096,384]{1,0:T(8,128)(2,1)} %get-tuple-element.50.refs_0_.refs_1_, bf16[4096,384]{1,0:T(8,128)(2,1)} %copy-done.1, bf16[4096,384]{1,0:T(8,128)(2,1)} %copy-done.1, ...), custom_call_target="tpu_custom_call" | custom-call | flops 3623878656 | bytes 6039797 | tf_op jit(solution)/shard_map/outer/pallas_call | solution.py:775
  291.2 65.4 %attend_back.1.grad_ref = bf16[8,3,384,128]{3,2,1,0:T(8,128)(2,1)} custom-call(s32[3]{0:T(128)} %bitcast.130, bf16[8,3,384,128]{3,2,1,0:T(8,128)(2,1)} %project.1.qkv_ref, bf16[3072,128]{1,0:T(8,128)(2,1)} %bitcast.45.da_ref, bf16[3072,128]{1,0:T(8,128)(2,1)} %get-tuple-element.45.out_ref, f32[3072,128]{1,0:T(8,128)} %get-tuple-element.49.lse_ref, ...), custom_call_target="tpu_custom_call" | custom-call | flops 77309411328 | bytes 9437184 | tf_op jit(solution)/shard_map/attend_back/pallas_call | solution.py:228
  358.0 11.7 %outgoing.1.refs_19_ = bf16[8,3,512,128]{3,2,1,0:T(8,128)(2,1)} custom-call(s32[8]{0:T(128)} %iota_xor_fusion.rel_ref, bf16[8,3,384,128]{3,2,1,0:T(8,128)(2,1)} %attend_back.1.grad_ref, bf16[8,384,512]{2,1,0:T(8,128)(2,1)} %bitcast.102, bf16[8,384,512]{2,1,0:T(8,128)(2,1)} %bitcast.100, bf16[2,4,288,512]{3,2,1,0:T(8,128)(2,1)} %copy-done.6, ...), custom_call_target="tpu_custom_call" | custom-call | flops 2415919104 | bytes 4194304 | tf_op jit(solution)/shard_map/outgoing/pallas_call | solution.py:281
  369.8 3.9 all-to-all-start.3
  374.2 10.0 %outer.11 = (bf16[4,288,512]{2,1,0:T(8,128)(2,1)}, bf16[4,288,512]{2,1,0:T(8,128)(2,1)}) custom-call(s32[2]{0:T(128)} %get-tuple-element.97.pick_ref, bf16[4096,384]{1,0:T(8,128)(2,1)} %get-tuple-element.50.refs_0_.refs_1_, bf16[4096,384]{1,0:T(8,128)(2,1)} %get-tuple-element.50.refs_0_.refs_1_, bf16[4096,384]{1,0:T(8,128)(2,1)} %copy-done.1, ...), custom_call_target="tpu_custom_call" | custom-call | flops 3623878656 | bytes 6039797 | tf_op jit(solution)/shard_map/outer/pallas_call | solution.py:775
  384.1 2.0 collective-permute-start.28
  386.2 10.0 %outer.10 = (bf16[4,288,512]{2,1,0:T(8,128)(2,1)}, bf16[4,288,512]{2,1,0:T(8,128)(2,1)}) custom-call(s32[2]{0:T(128)} %get-tuple-element.98.pick_ref, bf16[4096,384]{1,0:T(8,128)(2,1)} %get-tuple-element.50.refs_0_.refs_1_, bf16[4096,384]{1,0:T(8,128)(2,1)} %get-tuple-element.50.refs_0_.refs_1_, bf16[4096,384]{1,0:T(8,128)(2,1)} %copy-done.1, ...), custom_call_target="tpu_custom_call" | custom-call | flops 3623878656 | bytes 6039797 | tf_op jit(solution)/shard_map/outer/pallas_call | solution.py:775
  397.7 38.2 %collective-permute-done.28.refs_3_ = bf16[4,288,512]{2,1,0:T(8,128)(2,1)} collective-permute-done((bf16[4,288,512]{2,1,0:T(8,128)(2,1)}, bf16[4,288,512]{2,1,0:T(8,128)(2,1)}, u32[]{:S(2)}, u32[]{:S(2)}) %collective-permute-start.28) | collective-permute-done | bytes 1179680 | tf_op jit(solution)/shard_map/ppermute | solution.py:900
  437.7 4.9 merge.2.rest_0_
  442.7 3.7 all-to-all-start.4
  446.4 10.0 %tail.1 = (bf16[384,1024]{1,0:T(8,128)(2,1)}, f32[4,4096]{1,0:T(4,128)}) custom-call(bf16[8,3,512,128]{3,2,1,0:T(8,128)(2,1)} %copy-done.5, f32[384,1024]{1,0:T(8,128)} %get-tuple-element.46.stream_ref, f32[384,128]{1,0:T(8,128)} %pad_convert_fusion.info_ref, f32[3,4096]{1,0:T(4,128)} %bitcast.122, f32[384,1024]{1,0:T(8,128)} %get-tuple-element.55.mid_ref, ...), custom_call_target="tpu_custom_call" | custom-call | flops 2415919104 | bytes 14680064 | tf_op jit(solution)/shard_map/tail/pallas_call | solution.py:653
  460.1 3.5 outer.13.rest_1_.refs_2_
  465.1 3.5 outer.12.rest_0_.refs_1_
  470.6 5.7 %unjoin.1 = (bf16[384,1024]{1,0:T(8,128)(2,1)}, bf16[384,1024]{1,0:T(8,128)(2,1)}) custom-call(bf16[384,1024]{1,0:T(8,128)(2,1)} %get-tuple-element.62.refs_4_.grad_ref, bf16[32,64,1024]{2,1,0:T(8,128)(2,1)} %bitcast.104, bf16[2,4,64,512]{3,2,1,0:T(8,128)(2,1)} %outer.12.rest_0_.refs_1_, bf16[2,4,64,512]{3,2,1,0:T(8,128)(2,1)} %outer.13.rest_1_.refs_2_), custom_call_target="tpu_custom_call" | custom-call | flops 1610612736 | bytes 6291456 | tf_op jit(solution)/shard_map/unjoin/pallas_call | solution.py:318
  476.3 7.8 %collective-permute-done.31 = f32[4,4096]{1,0:T(4,128)S(1)} collective-permute-done((f32[4,4096]{1,0:T(4,128)}, f32[4,4096]{1,0:T(4,128)S(1)}, u32[]{:S(2)}, u32[]{:S(2)}) %collective-permute-start.31) | collective-permute-done | bytes 65568 | tf_op jit(solution)/shard_map/ppermute | solution.py:900
  484.8 3.6 outer.15
  488.9 3.5 outer.14
  494.4 6.9 %collective-permute-done.34 = f32[4,4096]{1,0:T(4,128)S(1)} collective-permute-done((f32[4,4096]{1,0:T(4,128)}, f32[4,4096]{1,0:T(4,128)S(1)}, u32[]{:S(2)}, u32[]{:S(2)}) %collective-permute-start.34) | collective-permute-done | bytes 65568 | tf_op jit(solution)/shard_map/ppermute | solution.py:900
  502.8 14.3 %all-to-all-done.4.refs_5_.came_ref = bf16[4,2,384,512]{3,2,1,0:T(8,128)(2,1)S(1)} async-done(((bf16[4,2,384,512]{3,2,1,0:T(8,128)(2,1)}), bf16[4,2,384,512]{3,2,1,0:T(8,128)(2,1)S(1)}, u32[]{:S(2)}, u32[]{:S(2)}) %all-to-all-start.4) | async-done | bytes 3145760 | tf_op jit(solution)/shard_map/all_to_all | solution.py:974
  518.7 2.1 merge.3.refs_1_.rest_0_
  520.9 2.0 collective-permute-start.38
  524.7 3.5 all-to-all-start.5
  529.1 3.2 finish.3
  536.3 5.3 all-to-all-done.5.came_ref
  (218 shorter events, 89.5 us)
Async XLA Ops:
  7.2 81.6 %all-gather.7.cloned.1.call-start = ((), (), s32[]{:S(2)}) async-start(), calls=%async_computation.6 | async-start | bytes 4325376 | tf_op jit(solution)/shard_map/all_gather | solution.py:1073
  8.0 216.5 %all-gather.9.cloned.1.call-start = ((), (), s32[]{:S(2)}) async-start(), calls=%async_computation.7 | async-start | bytes 19464192 | tf_op jit(solution)/shard_map/all_gather | solution.py:1083
  14.1 32.2 %collective-permute-start.9 = (bf16[32,3072]{1,0:T(8,128)(2,1)}, bf16[32,3072]{1,0:T(8,128)(2,1)}, u32[]{:S(2)}, u32[]{:S(2)}) collective-permute-start(bf16[32,3072]{1,0:T(8,128)(2,1)} %param.34), channel_id=1, source_target_pairs={{0,1},{1,2},{2,3},{3,0},{4,5},{5,6},{6,7},{7,4},{8,9},{9,10},{10,1... | collective-permute-start | bytes 589832 | tf_op jit(solution)/shard_map/ppermute | solution.py:905
  17.2 30.9 %collective-permute-start.10 = (bf16[32,3072]{1,0:T(8,128)(2,1)}, bf16[32,3072]{1,0:T(8,128)(2,1)}, u32[]{:S(2)}, u32[]{:S(2)}) collective-permute-start(bf16[32,3072]{1,0:T(8,128)(2,1)} %param.34), channel_id=1, source_target_pairs={{0,2},{1,3},{2,0},{3,1},{4,6},{5,7},{6,4},{7,5},{8,10},{9,11},{10,... | collective-permute-start | bytes 589832 | tf_op jit(solution)/shard_map/ppermute | solution.py:905
  19.8 10.9 %collective-permute-start = (s32[3]{0:T(128)S(1)}, s32[3]{0:T(128)S(1)}, u32[]{:S(2)}, u32[]{:S(2)}) collective-permute-start(s32[3]{0:T(128)S(1)} %bitcast.134), channel_id=1, source_target_pairs={{0,1},{1,2},{2,3},{3,0},{4,5},{5,6},{6,7},{7,4},{8,9},{9,10},{10,1... | collective-permute-start | bytes 44 | tf_op jit(solution)/shard_map/ppermute | solution.py:905
  19.9 15.6 %collective-permute-start.1 = (s32[3]{0:T(128)S(1)}, s32[3]{0:T(128)S(1)}, u32[]{:S(2)}, u32[]{:S(2)}) collective-permute-start(s32[3]{0:T(128)S(1)} %bitcast.135), channel_id=1, source_target_pairs={{0,2},{1,3},{2,0},{3,1},{4,6},{5,7},{6,4},{7,5},{8,10},{9,11},{10,... | collective-permute-start | bytes 44 | tf_op jit(solution)/shard_map/ppermute | solution.py:905
  21.7 13.8 %collective-permute-start.2 = (s32[3]{0:T(128)S(1)}, s32[3]{0:T(128)S(1)}, u32[]{:S(2)}, u32[]{:S(2)}) collective-permute-start(s32[3]{0:T(128)S(1)} %bitcast.136), channel_id=1, source_target_pairs={{0,3},{1,0},{2,1},{3,2},{4,7},{5,4},{6,5},{7,6},{8,11},{9,8},{10,9... | collective-permute-start | bytes 44 | tf_op jit(solution)/shard_map/ppermute | solution.py:905
  36.2 6.8 %collective-permute-start.3 = (f32[4,4096]{1,0:T(4,128)S(1)}, f32[4,4096]{1,0:T(4,128)S(1)}, u32[]{:S(2)}, u32[]{:S(2)}) collective-permute-start(f32[4,4096]{1,0:T(4,128)S(1)} %get-tuple-element.85), channel_id=1, source_target_pairs={{0,1},{1,2},{2,3},{3,0},{4,5},{5,6},{6,7},{7,4},{8,9},{9,10},{10,1... | collective-permute-start | bytes 196616 | tf_op jit(solution)/shard_map/ppermute | solution.py:905
  36.7 8.1 %collective-permute-start.4 = (f32[4,4096]{1,0:T(4,128)S(1)}, f32[4,4096]{1,0:T(4,128)S(1)}, u32[]{:S(2)}, u32[]{:S(2)}) collective-permute-start(f32[4,4096]{1,0:T(4,128)S(1)} %get-tuple-element.86), channel_id=1, source_target_pairs={{0,2},{1,3},{2,0},{3,1},{4,6},{5,7},{6,4},{7,5},{8,10},{9,11},{10,... | collective-permute-start | bytes 196616 | tf_op jit(solution)/shard_map/ppermute | solution.py:905
  38.2 6.6 %collective-permute-start.5 = (f32[4,4096]{1,0:T(4,128)S(1)}, f32[4,4096]{1,0:T(4,128)S(1)}, u32[]{:S(2)}, u32[]{:S(2)}) collective-permute-start(f32[4,4096]{1,0:T(4,128)S(1)} %get-tuple-element.87), channel_id=1, source_target_pairs={{0,3},{1,0},{2,1},{3,2},{4,7},{5,4},{6,5},{7,6},{8,11},{9,8},{10,9... | collective-permute-start | bytes 196616 | tf_op jit(solution)/shard_map/ppermute | solution.py:905
  43.1 9.5 %collective-permute-start.11 = (bf16[32,3072]{1,0:T(8,128)(2,1)}, bf16[32,3072]{1,0:T(8,128)(2,1)S(1)}, u32[]{:S(2)}, u32[]{:S(2)}) collective-permute-start(bf16[32,3072]{1,0:T(8,128)(2,1)} %param.34), channel_id=1, source_target_pairs={{0,3},{1,0},{2,1},{3,2},{4,7},{5,4},{6,5},{7,6},{8,11},{9,8},{10,9... | collective-permute-start | bytes 589832 | tf_op jit(solution)/shard_map/ppermute | solution.py:905
  44.8 43.8 %collective-permute-start.12 = (bf16[384,1024]{1,0:T(8,128)(2,1)}, bf16[384,1024]{1,0:T(8,128)(2,1)}, u32[]{:S(2)}, u32[]{:S(2)}) collective-permute-start(bf16[384,1024]{1,0:T(8,128)(2,1)} %fusion.1.branch_ref.refs_4_), channel_id=1, source_target_pairs={{0,4},{4,0},{8,12},{12,8},{16,20},{20,16},{24,28},{28,24},{1,5},{5... | collective-permute-start | bytes 2359304 | tf_op jit(solution)/shard_map/ppermute | solution.py:900
  44.9 43.8 %collective-permute-start.13 = (bf16[2048,384]{1,0:T(8,128)(2,1)S(1)}, bf16[2048,384]{1,0:T(8,128)(2,1)S(1)}, u32[]{:S(2)}, u32[]{:S(2)}) collective-permute-start(bf16[2048,384]{1,0:T(8,128)(2,1)S(1)} %pad_maximum_fusion.2.refs_0_.refs_1_), channel_id=1, source_target_pairs={{0,4},{4,0},{8,12},{12,8},{16,20},{20,16},{24,28},{28,24},{1,5},{5... | collective-permute-start | bytes 4718600 | tf_op jit(solution)/shard_map/ppermute | solution.py:900
  46.4 21.9 %collective-permute-start.6 = (f32[4,4096]{1,0:T(4,128)S(1)}, f32[4,4096]{1,0:T(4,128)S(1)}, u32[]{:S(2)}, u32[]{:S(2)}) collective-permute-start(f32[4,4096]{1,0:T(4,128)S(1)} %fusion.11), channel_id=1, source_target_pairs={{0,4},{4,0},{8,12},{12,8},{16,20},{20,16},{24,28},{28,24},{1,5},{5... | collective-permute-start | bytes 196616 | tf_op jit(solution)/shard_map/ppermute | solution.py:900
  55.6 30.2 %all-to-all-start = ((bf16[8,3,4,32,128]{4,3,2,1,0:T(8,128)(2,1)}), bf16[8,3,4,32,128]{4,3,2,1,0:T(8,128)(2,1)}, u32[]{:S(2)}, u32[]{:S(2)}) async-start(bf16[8,3,4,32,128]{4,3,2,1,0:T(8,128)(2,1)} %copy.69), calls=%async_computation | async-start | bytes 1572864 | tf_op jit(solution)/shard_map/all_to_all | solution.py:1075
  68.2 12.6 %collective-permute-start.7 = (f32[4,4096]{1,0:T(4,128)S(1)}, f32[4,4096]{1,0:T(4,128)S(1)}, u32[]{:S(2)}, u32[]{:S(2)}) collective-permute-start(f32[4,4096]{1,0:T(4,128)S(1)} %add.186), channel_id=1, source_target_pairs={{0,8},{4,12},{8,0},{12,4},{16,24},{20,28},{24,16},{28,20},{1,9},{5... | collective-permute-start | bytes 196616 | tf_op jit(solution)/shard_map/ppermute | solution.py:900
  80.9 4.3 collective-permute-start.8
  97.2 14.7 %collective-permute-start.17 = (bf16[384,512]{1,0:T(8,128)(2,1)}, bf16[384,512]{1,0:T(8,128)(2,1)S(1)}, u32[]{:S(2)}, u32[]{:S(2)}) collective-permute-start(bf16[384,512]{1,0:T(8,128)(2,1)} %get-tuple-element.44), channel_id=1, source_target_pairs={{0,16},{4,20},{8,24},{12,28},{16,0},{20,4},{24,8},{28,12},{1,17},{... | collective-permute-start | bytes 1179656 | tf_op jit(solution)/shard_map/ppermute | solution.py:900
  98.8 16.0 %collective-permute-start.14 = (bf16[384,512]{1,0:T(8,128)(2,1)}, bf16[384,512]{1,0:T(8,128)(2,1)S(1)}, u32[]{:S(2)}, u32[]{:S(2)}) collective-permute-start(bf16[384,512]{1,0:T(8,128)(2,1)} %get-tuple-element.43), channel_id=1, source_target_pairs={{0,8},{4,12},{8,0},{12,4},{16,24},{20,28},{24,16},{28,20},{1,9},{5... | collective-permute-start | bytes 1179656 | tf_op jit(solution)/shard_map/ppermute | solution.py:900
  113.0 26.6 %collective-permute-start.18 = (bf16[2,384,512]{2,1,0:T(8,128)(2,1)S(1)}, bf16[2,384,512]{2,1,0:T(8,128)(2,1)S(1)}, u32[]{:S(2)}, u32[]{:S(2)}) collective-permute-start(bf16[2,384,512]{2,1,0:T(8,128)(2,1)S(1)} %get-tuple-element.82), channel_id=1, source_target_pairs={{0,8},{4,12},{8,0},{12,4},{16,24},{20,28},{24,16},{28,20},{1,9},{5... | collective-permute-start | bytes 2359304 | tf_op jit(solution)/shard_map/ppermute | solution.py:900
  114.9 27.2 %collective-permute-start.15 = (bf16[2,384,512]{2,1,0:T(8,128)(2,1)S(1)}, bf16[2,384,512]{2,1,0:T(8,128)(2,1)S(1)}, u32[]{:S(2)}, u32[]{:S(2)}) collective-permute-start(bf16[2,384,512]{2,1,0:T(8,128)(2,1)S(1)} %get-tuple-element.84), channel_id=1, source_target_pairs={{0,16},{4,20},{8,24},{12,28},{16,0},{20,4},{24,8},{28,12},{1,17},{... | collective-permute-start | bytes 2359304 | tf_op jit(solution)/shard_map/ppermute | solution.py:900
  139.8 3.5 collective-permute-start.19
  142.3 3.5 collective-permute-start.16
  203.1 16.2 %all-to-all-start.1 = ((bf16[8,384,128]{2,1,0:T(8,128)(2,1)}), bf16[8,384,128]{2,1,0:T(8,128)(2,1)S(1)}, u32[]{:S(2)}, u32[]{:S(2)}) async-start(bf16[8,384,128]{2,1,0:T(8,128)(2,1)} %bitcast.119), calls=%async_computation.1 | async-start | bytes 1572864 | tf_op jit(solution)/shard_map/all_to_all | solution.py:1143
  206.6 239.8 %all-gather.11.cloned.1.call-start = ((), (), s32[]{:S(2)}) async-start(), calls=%async_computation.8 | async-start | bytes 6488064 | tf_op jit(solution)/shard_map/all_gather | solution.py:1085
  255.1 13.9 %collective-permute-start.20 = (bf16[4096,384]{1,0:T(8,128)(2,1)}, bf16[4096,384]{1,0:T(8,128)(2,1)S(1)}, u32[]{:S(2)}, u32[]{:S(2)}) collective-permute-start(bf16[4096,384]{1,0:T(8,128)(2,1)} %get-tuple-element.50.refs_0_.refs_1_), channel_id=1, source_target_pairs={{0,4},{4,0},{8,12},{12,8},{16,20},{20,16},{24,28},{28,24},{1,5},{5... | collective-permute-start | bytes 9437192 | tf_op jit(solution)/shard_map/ppermute | solution.py:900
  255.5 13.6 %collective-permute-start.22 = (bf16[384,4096]{1,0:T(8,128)(2,1)}, bf16[384,4096]{1,0:T(8,128)(2,1)}, u32[]{:S(2)}, u32[]{:S(2)}) collective-permute-start(bf16[384,4096]{1,0:T(8,128)(2,1)} %get-tuple-element.52.refs_10_), channel_id=1, source_target_pairs={{0,4},{4,0},{8,12},{12,8},{16,20},{20,16},{24,28},{28,24},{1,5},{5... | collective-permute-start | bytes 9437192 | tf_op jit(solution)/shard_map/ppermute | solution.py:900
  255.7 11.1 %collective-permute-start.21 = (bf16[1024,384]{1,0:T(8,128)(2,1)}, bf16[1024,384]{1,0:T(8,128)(2,1)}, u32[]{:S(2)}, u32[]{:S(2)}) collective-permute-start(bf16[1024,384]{1,0:T(8,128)(2,1)} %get-tuple-element.51.refs_6_.refs_7_), channel_id=1, source_target_pairs={{0,4},{4,0},{8,12},{12,8},{16,20},{20,16},{24,28},{28,24},{1,5},{5... | collective-permute-start | bytes 2359304 | tf_op jit(solution)/shard_map/ppermute | solution.py:900
  256.0 12.0 %collective-permute-start.23 = (bf16[1024,384]{1,0:T(8,128)(2,1)}, bf16[1024,384]{1,0:T(8,128)(2,1)}, u32[]{:S(2)}, u32[]{:S(2)}) collective-permute-start(bf16[1024,384]{1,0:T(8,128)(2,1)} %get-tuple-element.53.refs_12_.refs_13_), channel_id=1, source_target_pairs={{0,4},{4,0},{8,12},{12,8},{16,20},{20,16},{24,28},{28,24},{1,5},{5... | collective-permute-start | bytes 2359304 | tf_op jit(solution)/shard_map/ppermute | solution.py:900
  256.2 12.9 %collective-permute-start.24 = (bf16[384,1024]{1,0:T(8,128)(2,1)}, bf16[384,1024]{1,0:T(8,128)(2,1)}, u32[]{:S(2)}, u32[]{:S(2)}) collective-permute-start(bf16[384,1024]{1,0:T(8,128)(2,1)} %get-tuple-element.54.refs_16_), channel_id=1, source_target_pairs={{0,4},{4,0},{8,12},{12,8},{16,20},{20,16},{24,28},{28,24},{1,5},{5... | collective-permute-start | bytes 2359304 | tf_op jit(solution)/shard_map/ppermute | solution.py:900
  258.6 32.6 %all-to-all-start.2 = ((bf16[8,384,128]{2,1,0:T(8,128)(2,1)}), bf16[8,384,128]{2,1,0:T(8,128)(2,1)}, u32[]{:S(2)}, u32[]{:S(2)}) async-start(bf16[8,384,128]{2,1,0:T(8,128)(2,1)} %get-tuple-element.48), calls=%async_computation.2 | async-start | bytes 1572864 | tf_op jit(solution)/shard_map/all_to_all | solution.py:1155
  279.9 76.7 %collective-permute-start.26 = (bf16[2,4,288,512]{3,2,1,0:T(8,128)(2,1)}, bf16[2,4,288,512]{3,2,1,0:T(8,128)(2,1)}, u32[]{:S(2)}, u32[]{:S(2)}) collective-permute-start(bf16[2,4,288,512]{3,2,1,0:T(8,128)(2,1)} %outer.9.rest_1_), channel_id=1, source_target_pairs={{0,16},{4,20},{8,24},{12,28},{16,0},{20,4},{24,8},{28,12},{1,17},{... | collective-permute-start | bytes 7077896 | tf_op jit(solution)/shard_map/ppermute | solution.py:900
  290.5 66.1 %collective-permute-start.25 = (bf16[2,4,288,512]{3,2,1,0:T(8,128)(2,1)}, bf16[2,4,288,512]{3,2,1,0:T(8,128)(2,1)S(1)}, u32[]{:S(2)}, u32[]{:S(2)}) collective-permute-start(bf16[2,4,288,512]{3,2,1,0:T(8,128)(2,1)} %outer.8.rest_0_), channel_id=1, source_target_pairs={{0,8},{4,12},{8,0},{12,4},{16,24},{20,28},{24,16},{28,20},{1,9},{5... | collective-permute-start | bytes 7077896 | tf_op jit(solution)/shard_map/ppermute | solution.py:900
  369.8 66.2 %all-to-all-start.3 = ((bf16[8,3,512,128]{3,2,1,0:T(8,128)(2,1)}), bf16[8,3,512,128]{3,2,1,0:T(8,128)(2,1)S(1)}, u32[]{:S(2)}, u32[]{:S(2)}) async-start(bf16[8,3,512,128]{3,2,1,0:T(8,128)(2,1)} %outgoing.1.refs_19_), calls=%async_computation.3 | async-start | bytes 6291456 | tf_op jit(solution)/shard_map/all_to_all | solution.py:1176
  384.1 51.8 %collective-permute-start.28 = (bf16[4,288,512]{2,1,0:T(8,128)(2,1)}, bf16[4,288,512]{2,1,0:T(8,128)(2,1)}, u32[]{:S(2)}, u32[]{:S(2)}) collective-permute-start(bf16[4,288,512]{2,1,0:T(8,128)(2,1)} %get-tuple-element.61), channel_id=1, source_target_pairs={{0,8},{4,12},{8,0},{12,4},{16,24},{20,28},{24,16},{28,20},{1,9},{5... | collective-permute-start | bytes 3538952 | tf_op jit(solution)/shard_map/ppermute | solution.py:900
  396.2 39.8 %collective-permute-start.27 = (bf16[4,288,512]{2,1,0:T(8,128)(2,1)}, bf16[4,288,512]{2,1,0:T(8,128)(2,1)}, u32[]{:S(2)}, u32[]{:S(2)}) collective-permute-start(bf16[4,288,512]{2,1,0:T(8,128)(2,1)} %get-tuple-element.59), channel_id=1, source_target_pairs={{0,16},{4,20},{8,24},{12,28},{16,0},{20,4},{24,8},{28,12},{1,17},{... | collective-permute-start | bytes 3538952 | tf_op jit(solution)/shard_map/ppermute | solution.py:900
  442.7 74.4 %all-to-all-start.4 = ((bf16[4,2,384,512]{3,2,1,0:T(8,128)(2,1)}), bf16[4,2,384,512]{3,2,1,0:T(8,128)(2,1)S(1)}, u32[]{:S(2)}, u32[]{:S(2)}) async-start(bf16[4,2,384,512]{3,2,1,0:T(8,128)(2,1)} %merge.2.rest_0_), calls=%async_computation.4 | async-start | bytes 6291456 | tf_op jit(solution)/shard_map/all_to_all | solution.py:974
  456.4 3.7 collective-permute-start.29
  463.6 21.2 %collective-permute-start.33 = (bf16[2,4,64,512]{3,2,1,0:T(8,128)(2,1)}, bf16[2,4,64,512]{3,2,1,0:T(8,128)(2,1)}, u32[]{:S(2)}, u32[]{:S(2)}) collective-permute-start(bf16[2,4,64,512]{3,2,1,0:T(8,128)(2,1)} %outer.13.rest_1_.refs_2_), channel_id=1, source_target_pairs={{0,16},{4,20},{8,24},{12,28},{16,0},{20,4},{24,8},{28,12},{1,17},{... | collective-permute-start | bytes 1572872 | tf_op jit(solution)/shard_map/ppermute | solution.py:900
  468.6 20.3 %collective-permute-start.32 = (bf16[2,4,64,512]{3,2,1,0:T(8,128)(2,1)}, bf16[2,4,64,512]{3,2,1,0:T(8,128)(2,1)}, u32[]{:S(2)}, u32[]{:S(2)}) collective-permute-start(bf16[2,4,64,512]{3,2,1,0:T(8,128)(2,1)} %outer.12.rest_0_.refs_1_), channel_id=1, source_target_pairs={{0,8},{4,12},{8,0},{12,4},{16,24},{20,28},{24,16},{28,20},{1,9},{5... | collective-permute-start | bytes 1572872 | tf_op jit(solution)/shard_map/ppermute | solution.py:900
  469.2 15.0 %collective-permute-start.31 = (f32[4,4096]{1,0:T(4,128)}, f32[4,4096]{1,0:T(4,128)S(1)}, u32[]{:S(2)}, u32[]{:S(2)}) collective-permute-start(f32[4,4096]{1,0:T(4,128)} %tie.3), channel_id=1, source_target_pairs={{0,8},{4,12},{8,0},{12,4},{16,24},{20,28},{24,16},{28,20},{1,9},{5... | collective-permute-start | bytes 196616 | tf_op jit(solution)/shard_map/ppermute | solution.py:900
  488.3 14.4 %collective-permute-start.36 = (bf16[4,64,512]{2,1,0:T(8,128)(2,1)}, bf16[4,64,512]{2,1,0:T(8,128)(2,1)}, u32[]{:S(2)}, u32[]{:S(2)}) collective-permute-start(bf16[4,64,512]{2,1,0:T(8,128)(2,1)} %get-tuple-element.67.refs_2_), channel_id=1, source_target_pairs={{0,8},{4,12},{8,0},{12,4},{16,24},{20,28},{24,16},{28,20},{1,9},{5... | collective-permute-start | bytes 786440 | tf_op jit(solution)/shard_map/ppermute | solution.py:900
  492.4 10.4 %collective-permute-start.35 = (bf16[4,64,512]{2,1,0:T(8,128)(2,1)}, bf16[4,64,512]{2,1,0:T(8,128)(2,1)}, u32[]{:S(2)}, u32[]{:S(2)}) collective-permute-start(bf16[4,64,512]{2,1,0:T(8,128)(2,1)} %get-tuple-element.66.refs_1_), channel_id=1, source_target_pairs={{0,16},{4,20},{8,24},{12,28},{16,0},{20,4},{24,8},{28,12},{1,17},{... | collective-permute-start | bytes 786440 | tf_op jit(solution)/shard_map/ppermute | solution.py:900
  493.8 7.5 %collective-permute-start.34 = (f32[4,4096]{1,0:T(4,128)}, f32[4,4096]{1,0:T(4,128)S(1)}, u32[]{:S(2)}, u32[]{:S(2)}) collective-permute-start(f32[4,4096]{1,0:T(4,128)} %tie.4), channel_id=1, source_target_pairs={{0,16},{4,20},{8,24},{12,28},{16,0},{20,4},{24,8},{28,12},{1,17},{... | collective-permute-start | bytes 196616 | tf_op jit(solution)/shard_map/ppermute | solution.py:900
  520.9 11.4 %collective-permute-start.37 = (f32[4,4096]{1,0:T(4,128)}, f32[4,4096]{1,0:T(4,128)S(1)}, u32[]{:S(2)}, u32[]{:S(2)}) collective-permute-start(f32[4,4096]{1,0:T(4,128)} %tie.5), channel_id=1, source_target_pairs={{0,1},{1,2},{2,3},{3,0},{4,5},{5,6},{6,7},{7,4},{8,9},{9,10},{10,1... | collective-permute-start | bytes 196616 | tf_op jit(solution)/shard_map/ppermute | solution.py:905
  520.9 11.4 %collective-permute-start.38 = (f32[4,4096]{1,0:T(4,128)}, f32[4,4096]{1,0:T(4,128)S(1)}, u32[]{:S(2)}, u32[]{:S(2)}) collective-permute-start(f32[4,4096]{1,0:T(4,128)} %tie.5), channel_id=1, source_target_pairs={{0,2},{1,3},{2,0},{3,1},{4,6},{5,7},{6,4},{7,5},{8,10},{9,11},{10,... | collective-permute-start | bytes 196616 | tf_op jit(solution)/shard_map/ppermute | solution.py:905
  522.9 9.4 %collective-permute-start.39 = (f32[4,4096]{1,0:T(4,128)}, f32[4,4096]{1,0:T(4,128)S(1)}, u32[]{:S(2)}, u32[]{:S(2)}) collective-permute-start(f32[4,4096]{1,0:T(4,128)} %tie.5), channel_id=1, source_target_pairs={{0,3},{1,0},{2,1},{3,2},{4,7},{5,4},{6,5},{7,6},{8,11},{9,8},{10,9... | collective-permute-start | bytes 196616 | tf_op jit(solution)/shard_map/ppermute | solution.py:905
  524.7 16.9 %all-to-all-start.5 = ((bf16[4,2,64,512]{3,2,1,0:T(8,128)(2,1)}), bf16[4,2,64,512]{3,2,1,0:T(8,128)(2,1)S(1)}, u32[]{:S(2)}, u32[]{:S(2)}) async-start(bf16[4,2,64,512]{3,2,1,0:T(8,128)(2,1)} %merge.3.refs_1_.rest_0_), calls=%async_computation.5 | async-start | bytes 1048576 | tf_op jit(solution)/shard_map/all_to_all | solution.py:974
  (32 other events, 225.1 us)
Sparse Core Ops, SparseCore 0:
  11.1 77.7 all-gather.6
  92.2 132.2 all-gather.8
  258.2 83.6 all-gather.10

commit v4 on v3

--- a/solution.py
+++ b/solution.py
@@ -66,9 +66,11 @@
             qf = jnp.where(is_slot & (slot != utt), MASKED, 0.0)
             kf = jnp.where(slot == utt, 1.0, 0.0)
             vf = jnp.where(slot == 0, 1.0, 0.0)
-            for part, feat, dst in ((0, qf, q_s), (1, kf, k_s), (2, vf, v_s)):
+            for part, feat, dst in ((0, qf, q_s), (1, kf, k_s)):
                 x = qkv_ref[src, part].astype(jnp.float32)
                 dst[h, pl.ds(at, rows), :] = jnp.where(mine, x, feat).astype(jnp.bfloat16)
+            x = jnp.where(mine, qkv_ref[src, 2].astype(jnp.float32), vf)
+            v_s[h, :, pl.ds(at, rows)] = x.T.astype(jnp.bfloat16)
         return carry
 
     lax.fori_loop(0, sources, build, 0)
@@ -82,29 +84,29 @@
         def k_block(j, inner):
             kat = pl.multiple_of(j * bk, bk)
             for h in range(heads):
-                s = mm(q_s[h, pl.ds(at, bq), :], k_s[h, pl.ds(kat, bk), :], NT)
+                s = mm(k_s[h, pl.ds(kat, bk), :], q_s[h, pl.ds(at, bq), :], NT)
                 old = m_s[h]
-                top = jnp.maximum(old, jnp.max(s, axis=1, keepdims=True))
+                top = jnp.maximum(old, jnp.max(s, axis=0, keepdims=True))
                 alpha = jnp.exp(old - top)
-                p = jnp.exp(s - top[:, :1]).astype(jnp.bfloat16)
-                acc_s[h] = acc_s[h] * alpha + mm(p, v_s[h, pl.ds(kat, bk), :], NN)
+                p = jnp.exp(s - top).astype(jnp.bfloat16)
+                acc_s[h] = acc_s[h] * alpha + mm(v_s[h, :, pl.ds(kat, bk)], p, NN)
                 m_s[h] = top
             return inner
 
         lax.fori_loop(low // bk, (high + bk - 1) // bk, k_block, 0)
-        lane = lax.broadcasted_iota(jnp.int32, (bq, LANES), 1)
+        lane = lax.broadcasted_iota(jnp.int32, (LANES, bq), 0)
         out = None
         lse = None
         for h in range(heads):
             spare = (1 - h) * HD
             acc = acc_s[h]
-            total = acc[:, spare : spare + 1]
+            total = acc[spare : spare + 1, :]
             o = acc / total
-            l = m_s[h] + jnp.log(total)
+            l = jnp.broadcast_to(m_s[h] + jnp.log(total), (LANES, bq))
             out = o if out is None else jnp.where(lane < HD, out, o)
             lse = l if lse is None else jnp.where(lane < HD, lse, l)
-        out_ref[pl.ds(at, bq), :] = out.astype(jnp.bfloat16)
-        lse_ref[pl.ds(at, bq), :] = lse
+        out_ref[pl.ds(at, bq), :] = out.T.astype(jnp.bfloat16)
+        lse_ref[pl.ds(at, bq), :] = lse.T
         return carry
 
     lax.fori_loop(0, frames // bq, q_block, 0)
@@ -122,8 +124,12 @@
         ),
         in_specs=[pl.BlockSpec(memory_space=pltpu.SMEM), pl.BlockSpec(memory_space=pltpu.VMEM)],
         out_specs=(pl.BlockSpec(memory_space=pltpu.VMEM), pl.BlockSpec(memory_space=pltpu.VMEM)),
-        scratch_shapes=[pltpu.VMEM((heads, frames, LANES), jnp.bfloat16)] * 3
-        + [pltpu.VMEM((heads, bq, LANES), jnp.float32)] * 2,
+        scratch_shapes=[pltpu.VMEM((heads, frames, LANES), jnp.bfloat16)] * 2
+        + [
+            pltpu.VMEM((heads, LANES, frames), jnp.bfloat16),
+            pltpu.VMEM((heads, 1, bq), jnp.float32),
+            pltpu.VMEM((heads, LANES, bq), jnp.float32),
+        ],
         compiler_params=pltpu.CompilerParams(vmem_limit_bytes=VMEM),
         cost_estimate=pl.CostEstimate(
             flops=40 * heads * frames * frames * HD, bytes_accessed=frames * LANES * 12,
@@ -136,7 +142,7 @@
 def bwd_kernel(
     ends_ref, qkv_ref, da_ref, out_ref, lse_ref, cos_ref, sin_ref, *rest, heads, utts, bq, bk
 ):
-    grad_ref, q_s, k_s, v_s, d_s, gq_s, gk_s, gv_s = rest[-8:]
+    grad_ref, q_s, k_s, kt_s, v_s, d_s, gq_s, gk_s, gv_s = rest[-9:]
     sources, _, rows, _ = qkv_ref.shape
     frames = sources * rows
 
@@ -168,7 +174,8 @@
             ):
                 dst[h, pl.ds(at, rows), :] = jnp.where(mine, x.astype(jnp.float32), feat).astype(jnp.bfloat16)
             d_s[h, pl.ds(at, rows), :] = jnp.where(mine, da, df).astype(jnp.bfloat16)
-        gq_s[:, pl.ds(at, rows), :] = jnp.zeros((heads, rows, LANES), jnp.float32)
+            kt_s[h, :, pl.ds(at, rows)] = qkv_ref[src, 1].T
+        gq_s[:, :, pl.ds(at, rows)] = jnp.zeros((heads, LANES, rows), jnp.float32)
         return carry
 
     lax.fori_loop(0, sources, build, 0)
@@ -189,7 +196,7 @@
                 ds = (p * mm(v_s[h, pl.ds(kat, bk), :], d, NT)).astype(jnp.bfloat16)
                 gv_s[h, pl.ds(kat, bk), :] += mm(p.astype(jnp.bfloat16), d, NN)
                 gk_s[h, pl.ds(kat, bk), :] += mm(ds, q, NN)
-                gq_s[h, pl.ds(at, bq), :] += mm(ds, k, TN)
+                gq_s[h, :, pl.ds(at, bq)] += mm(kt_s[h, :, pl.ds(kat, bk)], ds, NN)
             return inner
 
         lax.fori_loop(low // bq, (high + bq - 1) // bq, q_block, 0)
@@ -208,11 +215,18 @@
             x = ref[0, pl.ds(at, rows), :]
             return jnp.where(lane < HD, x, ref[1, pl.ds(at, rows), :]) if heads == 2 else x
 
+        def both_flipped(ref):
+            x = ref[0, :, pl.ds(at, rows)]
+            if heads == 2:
+                row = lax.broadcasted_iota(jnp.int32, (LANES, rows), 0)
+                x = jnp.where(row < HD, x, ref[1, :, pl.ds(at, rows)])
+            return x.T
+
         def unturn(x):
             partner = jnp.where(first, pltpu.roll(x, LANES - HD // 2, 1), pltpu.roll(x, HD // 2, 1))
             return x * cos - partner * sin
 
-        grad_ref[src, 0] = (unturn(both(gq_s)) * HD ** -0.5).astype(jnp.bfloat16)
+        grad_ref[src, 0] = (unturn(both_flipped(gq_s)) * HD ** -0.5).astype(jnp.bfloat16)
         grad_ref[src, 1] = unturn(both(gk_s)).astype(jnp.bfloat16)
         grad_ref[src, 2] = both(gv_s).astype(jnp.bfloat16)
         return carry
@@ -232,8 +246,11 @@
         + [vmem] * 6
         + [pl.BlockSpec(memory_space=pl.ANY)] * len(after),
         out_specs=vmem,
-        scratch_shapes=[pltpu.VMEM((heads, frames, LANES), jnp.bfloat16)] * 4
-        + [pltpu.VMEM((heads, frames, LANES), jnp.float32)] * 3,
+        scratch_shapes=[pltpu.VMEM((heads, frames, LANES), jnp.bfloat16)] * 2
+        + [pltpu.VMEM((heads, LANES, frames), jnp.bfloat16)]
+        + [pltpu.VMEM((heads, frames, LANES), jnp.bfloat16)] * 2
+        + [pltpu.VMEM((heads, LANES, frames), jnp.float32)]
+        + [pltpu.VMEM((heads, frames, LANES), jnp.float32)] * 2,
         compiler_params=pltpu.CompilerParams(vmem_limit_bytes=VMEM),
         cost_estimate=pl.CostEstimate(
             flops=64 * heads * frames * frames * HD, bytes_accessed=frames * LANES * 24,
@@ -540,7 +557,7 @@
     rows, width = stream.shape
     devices = late.shape[0]
     hidden = down_each * devices
-    block = 512
+    block = 1024
     blocks = hidden // block
     halves = width // block
     groups = width // LANES
@@ -641,11 +658,10 @@
         sums_by_utt(sums_ref, width, info, gn, utts)
 
 
-def tail(held, stream, info, modulation, mid, early, skip_each, qkv_each, two, bup, utts, after):
+def tail(held, stream, info, modulation, mid, early, qkv_each, two, bup, utts, after):
     rows, width = stream.shape
     devices = early.shape[0]
     groups = held.shape[0]
-    first = skip_each // qkv_each
 
     def fixed(*shape):
         return pl.BlockSpec(shape, lambda p: (0,) * len(shape))
@@ -663,7 +679,7 @@
             fixed(rows, LANES),
             fixed(utts, 4 * width),
             fixed(rows, width),
-            pl.BlockSpec((devices, qkv_each, width), lambda p: (0, first + p, 0)),
+            pl.BlockSpec((devices, qkv_each, width), lambda p: (0, 0, p)),
             fixed(utts, 2 * width),
             fixed(1, 4 * width),
         ]
@@ -792,56 +808,37 @@
     )(picks, *operands, *(() if add is None else (add,)), *after)
 
 
-def merge_kernel(*refs, sums, held):
+def merge_kernel(*refs, sums):
     out = refs[-1]
-    batch, height, wide = refs[0].shape
-    for z in range(batch):
+    for z in range(out.shape[0]):
         for h in range(sums):
             total = refs[2 * h][z].astype(jnp.float32) + refs[2 * h + 1][z].astype(jnp.float32)
-            out[z, h, 0:height] = total.astype(jnp.bfloat16)
-    if held:
-        held_ref = refs[2 * sums]
-        groups, _, rows, _ = held_ref.shape
-        each = rows // batch
-        blocks = 3 * groups * LANES // wide // sums
-        for z in range(batch):
-            for part in range(3):
-                for g in range(groups):
-                    low = (part * groups + g) * LANES
-                    h, j = divmod(low // wide, blocks)
-                    at = height + j * each
-                    out[z, h, at : at + each, low % wide : low % wide + LANES] = held_ref[
-                        g, part, z * each : (z + 1) * each
-                    ]
-
-
-def merge(pairs, held, rows, after):
+            out[z, h] = total.astype(jnp.bfloat16)
+
+
+def merge(pairs, after):
     batch, height, wide = pairs[0][0].shape
-    vmem = pl.BlockSpec(memory_space=pltpu.VMEM)
     sums = len(pairs)
-    operands = [one for pair in pairs for one in pair]
-    specs = [pl.BlockSpec((batch, height, wide), lambda i: (0, 0, 0))] * (2 * sums)
-    if held is not None:
-        groups, _, total_rows, _ = held.shape
-        more = total_rows - rows
-        if rows % more:
-            held = held[:, :, rows:]
-            rows = 0
-        at = rows // more
-        operands.append(held)
-        specs.append(pl.BlockSpec((groups, 3, more, LANES), lambda i: (0, 0, at, 0)))
-        height += 3 * groups * LANES // wide // sums * (more // batch)
     shape = (batch, sums, height, wide)
     return pl.pallas_call(
-        functools.partial(merge_kernel, sums=sums, held=held is not None),
+        functools.partial(merge_kernel, sums=sums),
         grid=(1,),
         out_shape=jax.ShapeDtypeStruct(shape, jnp.bfloat16),
-        in_specs=specs + [pl.BlockSpec(memory_space=pl.ANY)] * len(after),
+        in_specs=[pl.BlockSpec((batch, height, wide), lambda i: (0, 0, 0))] * (2 * sums)
+        + [pl.BlockSpec(memory_space=pl.ANY)] * len(after),
         out_specs=pl.BlockSpec(shape, lambda i: (0, 0, 0, 0)),
         cost_estimate=SMALL,
         compiler_params=pltpu.CompilerParams(vmem_limit_bytes=VMEM),
         name="merge",
-    )(*operands, *after)
+    )(*[one for pair in pairs for one in pair], *after)
+
+
+def cut(held, rows):
+    groups, _, height, _ = held.shape
+    batch = lax.axis_size("batch")
+    each = (height - rows) // batch
+    piece = held[:, :, rows:].reshape(groups, 3, batch, each, LANES)
+    return piece.transpose(2, 3, 1, 0, 4).reshape(batch, each, 3 * groups * LANES)
 
 
 def finish_kernel(came_ref, *rest, sizes, counts):
@@ -875,6 +872,25 @@
     )(came, *after)
 
 
+def total_kernel(*refs, count):
+    total = refs[0][...].astype(jnp.float32)
+    for n in range(1, count):
+        total = total + refs[n][...].astype(jnp.float32)
+    refs[-1][...] = total
+
+
+def totalled(pieces, after):
+    vmem = pl.BlockSpec(memory_space=pltpu.VMEM)
+    return pl.pallas_call(
+        functools.partial(total_kernel, count=len(pieces)),
+        out_shape=jax.ShapeDtypeStruct(pieces[0].shape, jnp.float32),
+        in_specs=[vmem] * len(pieces) + [pl.BlockSpec(memory_space=pl.ANY)] * len(after),
+        out_specs=vmem,
+        cost_estimate=SMALL,
+        name="total",
+    )(*pieces, *after)
+
+
 def tie_kernel(*refs):
     pass
 
@@ -963,27 +979,19 @@
             one.keep(tuple(after) + (tuple(after_last) if one is self.halves[-1] else ()))
         return sum([one.pass_on() for one in self.halves], [])
 
-    def spread(self, after=(), held=None, rows=0):
+    def spread(self, after=()):
         for one in self.halves:
             while one.next < len(one.bits):
                 one.take()
                 one.pass_on()
-        pieces = merge(
-            [(one.total[0], one.came[0]) for one in self.halves], held, rows, tuple(after)
-        )
+        pieces = merge([(one.total[0], one.came[0]) for one in self.halves], tuple(after))
         self.spread_out = lax.all_to_all(pieces, "batch", 0, 0, tiled=True)
-        self.held = held
-        self.rows = rows
         return [pieces]
 
     def result(self, after=()):
         devices = lax.axis_size("seq") * lax.axis_size("batch")
         sizes = [first.shape[0] // devices for first, _, _, _ in self.weights]
         counts = [second.shape[1] // 2 // Sum.wide for _, _, second, _ in self.weights]
-        if self.held is not None:
-            groups, _, height, _ = self.held.shape
-            sizes.append((height - self.rows) // lax.axis_size("batch"))
-            counts.append(3 * groups * LANES // 2 // Sum.wide)
         return finish(self.spread_out, sizes, counts, tuple(after))
 
 
@@ -1006,6 +1014,16 @@
             out, ahead(value, step), (place - step) % batch, 0
         )
     return out
+
+
+def all_pieces_for(value):
+    batch = lax.axis_size("batch")
+    place = lax.axis_index("batch")
+    pieces = [
+        lax.dynamic_index_in_dim(value, (place + step) % batch, 0, keepdims=False)
+        for step in range(batch)
+    ]
+    return [ahead(piece, step) if step else piece for step, piece in enumerate(pieces)]
 
 
 def seq_pieces(value, bits):
@@ -1070,8 +1088,9 @@
     )
     per_device = width // seq
     groups = width // LANES
-    full_skip = lax.all_gather(skip_proj, BOTH, axis=0, tiled=False)
-    own_qkv = all_pieces(qkv_proj).reshape(batch, qkv_each, 3, seq, per_device)
+    full_skip = lax.all_gather(all_pieces(skip_proj), "seq", axis=0, tiled=True)
+    own_rows = all_pieces(qkv_proj)
+    own_qkv = own_rows.reshape(batch, qkv_each, 3, seq, per_device)
     own_qkv = lax.all_to_all(own_qkv.transpose(3, 2, 0, 1, 4), "seq", 0, 0, tiled=True)
     own_qkv = jnp.pad(own_qkv, ((0, 0),) * 4 + ((0, LANES - per_device),))
     own_qkv = own_qkv.transpose(0, 2, 3, 1, 4).reshape(width, 3 * LANES)
@@ -1081,8 +1100,7 @@
         axis=0,
     )
     late = lax.all_gather(late, BOTH, axis=0, tiled=False)
-    full_qkv = jnp.concatenate([qkv_proj[:, p * width : (p + 1) * width] for p in range(3)], axis=0)
-    full_qkv = lax.all_gather(full_qkv, BOTH, axis=0, tiled=False)
+    full_qkv = lax.all_gather(own_rows, "seq", axis=0, tiled=True)
 
     utt_lengths = lengths[0]
     ends = jnp.cumsum(utt_lengths).astype(jnp.int32)
@@ -1139,7 +1157,7 @@
     )
     normed_halves = [seq_pieces(normed_one[0], low + [1]), seq_pieces(normed_one[1], high + [1])]
     held = project(rel, normed_halves, own_qkv, group_cos, group_sin, ())
-    head_out, log_sums = attend(held, ends, heads, 1024, 512)
+    head_out, log_sums = attend(held, ends, heads, 1536, 1536)
     att = lax.all_to_all(
         head_out.reshape(seq, rows, LANES)[:, :, :per_device], "seq", 0, 0, tiled=True
     )
@@ -1169,7 +1187,7 @@
     waits = sums.send()
 
     grad_held = attend_back(
-        held, back, head_out, log_sums, group_cos, group_sin, ends, heads, waits, 1024, 512
+        held, back, head_out, log_sums, group_cos, group_sin, ends, heads, waits + [full_qkv], 1024, 1024
     )
     grad_held = outgoing(rel, grad_held, normed_halves, tuple(sums.came()))
     mark = (grad_held,)
@@ -1178,25 +1196,25 @@
         grad_held = grad_held.reshape(groups, 2, 3, -1, per_device).transpose(0, 2, 3, 1, 4)
         grad_held = grad_held.reshape(groups, 3, -1, LANES)
     sums.keep(mark)
-    waits = sums.spread((), grad_held, rows)
+    waits = sums.spread()
 
     grad_stream, row_sums = tail(
-        grad_held, stream_in, info, modulation, grad_mid, full_qkv, 0, qkv_each,
+        grad_held, stream_in, info, modulation, grad_mid, full_qkv, qkv_each,
         mod_two, bup_terms, utts, waits,
     )
     last_sums = Sums([pairs(joined_pair, pair(grad_stream))], (low, high))
     row_sums = row_sums + swap(row_sums, 1)
     waits = last_sums.send((row_sums,))
+    grad_inputs, grad_skip_rows = unjoin(grad_stream, full_skip, skip_each, waits)
+    waits = last_sums.keep((grad_inputs,))
     row_sums = tie(row_sums, waits)
-    row_sums = row_sums + swap(row_sums, 2)
-    grad_inputs, grad_skip_rows = unjoin(grad_stream, full_skip, skip_each, waits)
-    waits = last_sums.keep((grad_inputs,), (row_sums,))
-    row_sums = tie(row_sums, waits)
-    for bit in low[1:]:
+    for bit in low:
         row_sums = row_sums + swap(row_sums, bit)
+    qkv_came = all_pieces_for(cut(tie(grad_held, waits), rows))
     waits = last_sums.spread((row_sums, sums.spread_out))
     row_sums = all_pieces(tie(row_sums, waits))
-    grad_down, grad_up, grad_out_w, grad_qkv_w = sums.result(waits)
+    grad_down, grad_up, grad_out_w = sums.result(waits)
+    grad_qkv_w = totalled(qkv_came, (last_sums.spread_out,))
     (grad_skip_w,) = last_sums.result()
 
     grad_modulation = row_sums[:, :utts].reshape(batch * utts, 4 * width)

time: 557 us -> 530 us (0.952)
  waiting for transfers between devices: 161 us -> 130 us
  Pallas kernels: 250 us -> 231 us
  starting transfers between devices: 63.9 us -> 80.2 us
    ppermute x28, waiting for transfers between devices: 112 us -> 96.1 us  [swap(): return lax.ppermute(value, 'seq', [(i, i ^ bit) for i in range(size)])]
    ppermute x12 -> x18, starting transfers between devices: 17.2 us -> 31.8 us  [ahead(): lax.ppermute(value, 'batch', [(i, (i + step) % size) for i in range(size)])]
    pallas_call x1, Pallas kernels: 44.1 us -> 31.8 us  [attend(): pl.pallas_call(functools.partial(fwd_kernel, heads=heads, utts=utts, bq=b...]
    all_to_all x2, waiting for transfers between devices: 19.7 us -> 8.43 us  [spread(): self.spread_out = lax.all_to_all(pieces, 'batch', 0, 0, tiled=True)]
    pallas_call x1, Pallas kernels: 65.4 us -> 59.7 us  [attend_back(): pl.pallas_call(functools.partial(bwd_kernel, heads=heads, utts=utts, bq=b...]
    another operation x6, other arithmetic: 2.19 us -> 7.78 us  [seq_pieces(): value = jnp.stack([value, came], axis=sum((b > bit for b in have)))]
    ppermute x12 -> x18, waiting for transfers between devices: 11.8 us -> 14.1 us  [ahead(): lax.ppermute(value, 'batch', [(i, (i + step) % size) for i in range(size)])]
    unnamed x71 -> x95, local copies, waits for them, and re-layouts: 18.1 us -> 16.9 us
  transfers between devices with their start and end apart: 49 -> 55, of which waited for: 23 -> 23; matrix products, arithmetic and copies ran while one was open for 9% -> 10% of each run, Pallas kernels for 39% -> 42%
where the time goes in v4:
time: 530 us; the launch traced here: 522 us
  Pallas kernels  231 us (44%)
  waiting for transfers between devices  130 us (25%)
  starting transfers between devices  80.2 us (15%)
  local copies, waits for them, and re-layouts  37.9 us (7%)
  other arithmetic  25.4 us (5%)
  between operations  15 us (3%)
    ppermute x28, waiting for transfers between devices, swap(): return lax.ppermute(value, 'seq', [(i, i ^ bit) for i in range(size)])  96.1 us
    pallas_call x1, Pallas kernels, attend_back(): pl.pallas_call(functools.partial(bwd_kernel, heads=heads, utts=utts, bq=b...  59.7 us
    pallas_call x8, Pallas kernels, outer(): pl.pallas_call(functools.partial(outer_kernel, sizes=sizes, counts=counts...  52.1 us
    pallas_call x1, Pallas kernels, attend(): pl.pallas_call(functools.partial(fwd_kernel, heads=heads, utts=utts, bq=b...  31.8 us
    ppermute x18, starting transfers between devices, ahead(): lax.ppermute(value, 'batch', [(i, (i + step) % size) for i in range(size)])  31.8 us
    pallas_call x1, Pallas kernels, middle(): pl.pallas_call(functools.partial(middle_kernel, utts=utts, blocks=blocks)...  28.7 us
    ppermute x28, starting transfers between devices, swap(): return lax.ppermute(value, 'seq', [(i, i ^ bit) for i in range(size)])  20.8 us
    unnamed x95, local copies, waits for them, and re-layouts  16.9 us
  transfers between devices with their start and end apart: 55, of which 23 were waited for; matrix products, arithmetic and copies ran while one was open for 10% of the time, Pallas kernels for 42%

profile of v4, /device:TPU:0, one launch (start us, length us, event | category | flops | bytes accessed | tf_op | source)
XLA Modules:
  0.0 522.2 jit_solution(14667656439766530722)
XLA Ops:
  7.3 3.1 collective-permute-start.9
  10.3 2.6 collective-permute-start.10
  17.0 4.8 collective-permute-done.10
  23.7 3.3 collective-permute-start
  45.6 2.6 collective-permute-start.14
  48.2 2.9 collective-permute-done.4
  59.0 4.2 all-to-all-start
  63.6 7.8 %fusion = (f32[3072,128]{1,0:T(8,128)}, f32[3072,128]{1,0:T(8,128)}) fusion(f32[128]{0:T(128)} %get-tuple-element.94, f32[128]{0:T(128)} %get-tuple-element.95, f32[3072]{0:T(1024)S(1)} %subtract_convert_fusion), kind=kLoop, calls=%fused_computation.5 | loop fusion | flops 786432 | bytes 3159040 | tf_op jit(solution)/shard_map/mul | solution.py:1004
  73.5 2.9 collective-permute-done.7
  78.7 3.4 collective-permute-done.8
  86.8 7.4 %front.1 = (f32[384,1024]{1,0:T(8,128)}, bf16[384,512]{1,0:T(8,128)(2,1)}, bf16[384,512]{1,0:T(8,128)(2,1)}) custom-call(bf16[384,1024]{1,0:T(8,128)(2,1)} %bitcast.126, bf16[384,1024]{1,0:T(8,128)(2,1)} %bitcast.127, f32[384,128]{1,0:T(8,128)} %pad_convert_fusion.info_ref, f32[3,4096]{1,0:T(4,128)} %bitcast.135, ...), custom_call_target="tpu_custom_call" | custom-call | flops 1610612736 | bytes 8388608 | tf_op jit(solution)/shard_map/front/pallas_call | solution.py:429
  96.8 16.2 %collective-permute-done.17 = bf16[384,512]{1,0:T(8,128)(2,1)S(1)} collective-permute-done((bf16[384,512]{1,0:T(8,128)(2,1)}, bf16[384,512]{1,0:T(8,128)(2,1)S(1)}, u32[]{:S(2)}, u32[]{:S(2)}) %collective-permute-start.17) | collective-permute-done | bytes 393248 | tf_op jit(solution)/shard_map/ppermute | solution.py:916
  116.4 14.6 %collective-permute-done.18 = bf16[2,384,512]{2,1,0:T(8,128)(2,1)S(1)} collective-permute-done((bf16[2,384,512]{2,1,0:T(8,128)(2,1)S(1)}, bf16[2,384,512]{2,1,0:T(8,128)(2,1)S(1)}, u32[]{:S(2)}, u32[]{:S(2)}) %collective-permute-start.18) | collective-permute-done | bytes 786464 | tf_op jit(solution)/shard_map/ppermute | solution.py:916
  132.4 5.9 %collective-permute-done.21 = bf16[2,384,512]{2,1,0:T(8,128)(2,1)S(1)} collective-permute-done((bf16[2,384,512]{2,1,0:T(8,128)(2,1)S(1)}, bf16[2,384,512]{2,1,0:T(8,128)(2,1)S(1)}, u32[]{:S(2)}, u32[]{:S(2)}) %collective-permute-start.21) | collective-permute-done | bytes 786464 | tf_op jit(solution)/shard_map/ppermute | solution.py:916
  143.7 2.2 pad_maximum_fusion.1
  147.7 11.1 %project.1.qkv_ref = bf16[8,3,384,128]{3,2,1,0:T(8,128)(2,1)} custom-call(s32[8]{0:T(128)} %iota_xor_fusion.rel_ref, bf16[8,384,512]{2,1,0:T(8,128)(2,1)} %bitcast.118, bf16[8,384,512]{2,1,0:T(8,128)(2,1)} %bitcast.120, bf16[1024,384]{1,0:T(8,128)(2,1)} %bitcast.123, f32[3072,128]{1,0:T(8,128)} %get-tuple-element.93.rest_0_.cos_ref, ...), custom_call_target="tpu_custom_call" | custom-call | flops 2415919104 | bytes 4194304 | tf_op jit(solution)/shard_map/project/pallas_call | solution.py:474
  158.8 31.8 %attend.1 = (bf16[3072,128]{1,0:T(8,128)(2,1)}, f32[3072,128]{1,0:T(8,128)}) custom-call(s32[3]{0:T(128)} %bitcast.144, bf16[8,3,384,128]{3,2,1,0:T(8,128)(2,1)} %project.1.qkv_ref), custom_call_target="tpu_custom_call" | custom-call | flops 48318382080 | bytes 4718592 | tf_op jit(solution)/shard_map/attend/pallas_call | solution.py:119
  190.6 3.7 all-to-all-start.1
  195.8 11.1 %all-to-all-done.1.att_ref = bf16[8,384,128]{2,1,0:T(8,128)(2,1)S(1)} async-done(((bf16[8,384,128]{2,1,0:T(8,128)(2,1)}), bf16[8,384,128]{2,1,0:T(8,128)(2,1)S(1)}, u32[]{:S(2)}, u32[]{:S(2)}) %all-to-all-start.1) | async-done | bytes 786464 | tf_op jit(solution)/shard_map/all_to_all | solution.py:1161
  207.7 28.7 %middle.1 = (bf16[384,1024]{1,0:T(8,128)(2,1)}, bf16[1024,384]{1,0:T(8,128)(2,1)}, bf16[1024,384]{1,0:T(8,128)(2,1)}, bf16[4096,384]{1,0:T(8,128)(2,1)}, bf16[38...) custom-call(bf16[8,384,128]{2,1,0:T(8,128)(2,1)} %copy-done.17, ...), custom_call_target="tpu_custom_call" | custom-call | flops 19327352832 | bytes 20971520 | tf_op jit(solution)/shard_map/middle/pallas_call | solution.py:574
  238.1 4.4 all-to-all-start.2
  243.1 6.3 %collective-permute-done.24.refs_8_.refs_9_ = bf16[1024,384]{1,0:T(8,128)(2,1)} collective-permute-done((bf16[1024,384]{1,0:T(8,128)(2,1)}, bf16[1024,384]{1,0:T(8,128)(2,1)}, u32[]{:S(2)}, u32[]{:S(2)}) %collective-permute-start.24) | collective-permute-done | bytes 786464 | tf_op jit(solution)/shard_map/ppermute | solution.py:916
  253.7 9.1 %outer.8.rest_0_ = bf16[2,4,288,512]{3,2,1,0:T(8,128)(2,1)} custom-call(s32[2]{0:T(128)} %fusion.33.pick_ref, bf16[4096,384]{1,0:T(8,128)(2,1)} %get-tuple-element.49.refs_0_.refs_1_, bf16[4096,384]{1,0:T(8,128)(2,1)} %get-tuple-element.49.refs_0_.refs_1_, bf16[4096,384]{1,0:T(8,128)(2,1)} %copy-done.1, bf16[4096,384]{1,0:T(8,128)(2,1)} %copy-done.1, ...), custom_call_target="tpu_custom_call" | custom-call | flops 3623878656 | bytes 6039797 | tf_op jit(solution)/shard_map/outer/pallas_call | solution.py:791
  262.9 9.2 %outer.9.rest_1_ = bf16[2,4,288,512]{3,2,1,0:T(8,128)(2,1)} custom-call(s32[2]{0:T(128)} %fusion.31.pick_ref, bf16[4096,384]{1,0:T(8,128)(2,1)} %get-tuple-element.49.refs_0_.refs_1_, bf16[4096,384]{1,0:T(8,128)(2,1)} %get-tuple-element.49.refs_0_.refs_1_, bf16[4096,384]{1,0:T(8,128)(2,1)} %copy-done.1, bf16[4096,384]{1,0:T(8,128)(2,1)} %copy-done.1, ...), custom_call_target="tpu_custom_call" | custom-call | flops 3623878656 | bytes 6039797 | tf_op jit(solution)/shard_map/outer/pallas_call | solution.py:791
  272.4 59.7 %attend_back.1.grad_ref = bf16[8,3,384,128]{3,2,1,0:T(8,128)(2,1)} custom-call(s32[3]{0:T(128)} %bitcast.145, bf16[8,3,384,128]{3,2,1,0:T(8,128)(2,1)} %project.1.qkv_ref, bf16[3072,128]{1,0:T(8,128)(2,1)} %bitcast.48.da_ref, bf16[3072,128]{1,0:T(8,128)(2,1)} %get-tuple-element.44.out_ref, f32[3072,128]{1,0:T(8,128)} %get-tuple-element.48.lse_ref, ...), custom_call_target="tpu_custom_call" | custom-call | flops 77309411328 | bytes 9437184 | tf_op jit(solution)/shard_map/attend_back/pallas_call | solution.py:242
  333.6 11.8 %outgoing.1.refs_19_ = bf16[8,3,512,128]{3,2,1,0:T(8,128)(2,1)} custom-call(s32[8]{0:T(128)} %iota_xor_fusion.rel_ref, bf16[8,3,384,128]{3,2,1,0:T(8,128)(2,1)} %attend_back.1.grad_ref, bf16[8,384,512]{2,1,0:T(8,128)(2,1)} %bitcast.119, bf16[8,384,512]{2,1,0:T(8,128)(2,1)} %bitcast.121, bf16[2,4,288,512]{3,2,1,0:T(8,128)(2,1)} %collective-permute-done.28.rest_0_.refs_18_, ...), custom_call_target="tpu_custom_call" | custom-call | flops 2415919104 | bytes 4194304 | tf_op jit(solution)/shard_map/outgoing/pallas_call | solution.py:298
  345.4 4.7 all-to-all-start.3
  350.6 9.9 %outer.10 = (bf16[4,288,512]{2,1,0:T(8,128)(2,1)}, bf16[4,288,512]{2,1,0:T(8,128)(2,1)}) custom-call(s32[2]{0:T(128)} %get-tuple-element.97.pick_ref, bf16[4096,384]{1,0:T(8,128)(2,1)} %get-tuple-element.49.refs_0_.refs_1_, bf16[4096,384]{1,0:T(8,128)(2,1)} %get-tuple-element.49.refs_0_.refs_1_, bf16[4096,384]{1,0:T(8,128)(2,1)} %copy-done.1, ...), custom_call_target="tpu_custom_call" | custom-call | flops 3623878656 | bytes 6039797 | tf_op jit(solution)/shard_map/outer/pallas_call | solution.py:791
  360.5 2.1 collective-permute-start.30
  362.6 9.9 %outer.11 = (bf16[4,288,512]{2,1,0:T(8,128)(2,1)}, bf16[4,288,512]{2,1,0:T(8,128)(2,1)}) custom-call(s32[2]{0:T(128)} %get-tuple-element.96.pick_ref, bf16[4096,384]{1,0:T(8,128)(2,1)} %get-tuple-element.49.refs_0_.refs_1_, bf16[4096,384]{1,0:T(8,128)(2,1)} %get-tuple-element.49.refs_0_.refs_1_, bf16[4096,384]{1,0:T(8,128)(2,1)} %copy-done.1, ...), custom_call_target="tpu_custom_call" | custom-call | flops 3623878656 | bytes 6039797 | tf_op jit(solution)/shard_map/outer/pallas_call | solution.py:791
  374.1 38.3 %collective-permute-done.30.refs_1_ = bf16[4,288,512]{2,1,0:T(8,128)(2,1)} collective-permute-done((bf16[4,288,512]{2,1,0:T(8,128)(2,1)}, bf16[4,288,512]{2,1,0:T(8,128)(2,1)}, u32[]{:S(2)}, u32[]{:S(2)}) %collective-permute-start.30) | collective-permute-done | bytes 1179680 | tf_op jit(solution)/shard_map/ppermute | solution.py:916
  412.5 4.3 merge.2.rest_0_
  418.4 4.5 all-to-all-start.4
  422.9 10.0 %tail.1 = (bf16[384,1024]{1,0:T(8,128)(2,1)}, f32[4,4096]{1,0:T(4,128)}) custom-call(bf16[8,3,512,128]{3,2,1,0:T(8,128)(2,1)} %copy-done.4, f32[384,1024]{1,0:T(8,128)} %get-tuple-element.45.stream_ref, f32[384,128]{1,0:T(8,128)} %pad_convert_fusion.info_ref, f32[3,4096]{1,0:T(4,128)} %bitcast.137, f32[384,1024]{1,0:T(8,128)} %get-tuple-element.54.mid_ref, ...), custom_call_target="tpu_custom_call" | custom-call | flops 2415919104 | bytes 14680064 | tf_op jit(solution)/shard_map/tail/pallas_call | solution.py:669
  433.5 2.1 collective-permute-done.33
  437.9 3.5 outer.12.rest_0_
  442.8 3.5 outer.13.rest_1_
  447.0 5.7 %unjoin.1 = (bf16[384,1024]{1,0:T(8,128)(2,1)}, bf16[384,1024]{1,0:T(8,128)(2,1)}) custom-call(bf16[384,1024]{1,0:T(8,128)(2,1)} %get-tuple-element.61.refs_4_.grad_ref, bf16[32,64,1024]{2,1,0:T(8,128)(2,1)} %all-gather.5.cloned.1.call-done.weight_ref, bf16[2,4,64,512]{3,2,1,0:T(8,128)(2,1)} %outer.12.rest_0_, bf16[2,4,64,512]{3,2,1,0:T(8,128)(2,1)} %outer.13.rest_1_), custom_call_target="tpu_custom_call" | custom-call | flops 1610612736 | bytes 6291456 | tf_op jit(solution)/shard_map/unjoin/pallas_call | solution.py:335
  452.6 3.0 collective-permute-done.34.refs_6_
  456.4 3.5 outer.14
  461.0 3.6 outer.15
  473.7 2.4 collective-permute-start.44
  478.7 7.7 %all-to-all-done.4.refs_5_.came_ref = bf16[4,2,288,512]{3,2,1,0:T(8,128)(2,1)} async-done(((bf16[4,2,288,512]{3,2,1,0:T(8,128)(2,1)}), bf16[4,2,288,512]{3,2,1,0:T(8,128)(2,1)}, u32[]{:S(2)}, u32[]{:S(2)}) %all-to-all-start.4) | async-done | bytes 2359328 | tf_op jit(solution)/shard_map/all_to_all | solution.py:988
  486.4 2.1 merge.3.refs_1_.rest_0_
  488.5 5.6 %all-to-all-start.5 = ((bf16[4,2,64,512]{3,2,1,0:T(8,128)(2,1)}), bf16[4,2,64,512]{3,2,1,0:T(8,128)(2,1)S(1)}, u32[]{:S(2)}, u32[]{:S(2)}) async-start(bf16[4,2,64,512]{3,2,1,0:T(8,128)(2,1)} %merge.3.refs_1_.rest_0_), calls=%async_computation.5 | async-start | bytes 1048576 | tf_op jit(solution)/shard_map/all_to_all | solution.py:988
  495.1 2.8 finish.3
  498.0 3.9 collective-permute-start.42
  513.2 2.1 total.1
  (262 shorter events, 101.6 us)
Async XLA Ops:
  7.2 78.4 %all-gather.5.cloned.1.call-start = ((), (), s32[]{:S(2)}) async-start(), calls=%async_computation.6 | async-start | bytes 4718592 | tf_op jit(solution)/shard_map/all_gather | solution.py:1091
  7.3 9.7 %collective-permute-start.9 = (bf16[64,1024]{1,0:T(8,128)(2,1)}, bf16[64,1024]{1,0:T(8,128)(2,1)S(1)}, u32[]{:S(2)}, u32[]{:S(2)}) collective-permute-start(bf16[64,1024]{1,0:T(8,128)(2,1)} %param.31), channel_id=1, source_target_pairs={{0,1},{1,2},{2,3},{3,0},{4,5},{5,6},{6,7},{7,4},{8,9},{9,10},{10,1... | collective-permute-start | bytes 393224 | tf_op jit(solution)/shard_map/ppermute | solution.py:921
  10.3 11.4 %collective-permute-start.10 = (bf16[64,1024]{1,0:T(8,128)(2,1)}, bf16[64,1024]{1,0:T(8,128)(2,1)S(1)}, u32[]{:S(2)}, u32[]{:S(2)}) collective-permute-start(bf16[64,1024]{1,0:T(8,128)(2,1)} %param.31), channel_id=1, source_target_pairs={{0,2},{1,3},{2,0},{3,1},{4,6},{5,7},{6,4},{7,5},{8,10},{9,11},{10,... | collective-permute-start | bytes 393224 | tf_op jit(solution)/shard_map/ppermute | solution.py:921
  12.9 8.9 %collective-permute-start.11 = (bf16[64,1024]{1,0:T(8,128)(2,1)}, bf16[64,1024]{1,0:T(8,128)(2,1)S(1)}, u32[]{:S(2)}, u32[]{:S(2)}) collective-permute-start(bf16[64,1024]{1,0:T(8,128)(2,1)} %param.31), channel_id=1, source_target_pairs={{0,3},{1,0},{2,1},{3,2},{4,7},{5,4},{6,5},{7,6},{8,11},{9,8},{10,9... | collective-permute-start | bytes 393224 | tf_op jit(solution)/shard_map/ppermute | solution.py:921
  22.7 184.2 %all-gather.9.cloned.1.call-start = ((), (), s32[]{:S(2)}) async-start(), calls=%async_computation.8 | async-start | bytes 19464192 | tf_op jit(solution)/shard_map/all_gather | solution.py:1102
  23.7 15.4 %collective-permute-start = (s32[3]{0:T(128)S(1)}, s32[3]{0:T(128)S(1)}, u32[]{:S(2)}, u32[]{:S(2)}) collective-permute-start(s32[3]{0:T(128)S(1)} %bitcast.149), channel_id=1, source_target_pairs={{0,1},{1,2},{2,3},{3,0},{4,5},{5,6},{6,7},{7,4},{8,9},{9,10},{10,1... | collective-permute-start | bytes 44 | tf_op jit(solution)/shard_map/ppermute | solution.py:921
  27.0 12.1 %collective-permute-start.1 = (s32[3]{0:T(128)S(1)}, s32[3]{0:T(128)S(1)}, u32[]{:S(2)}, u32[]{:S(2)}) collective-permute-start(s32[3]{0:T(128)S(1)} %bitcast.150), channel_id=1, source_target_pairs={{0,2},{1,3},{2,0},{3,1},{4,6},{5,7},{6,4},{7,5},{8,10},{9,11},{10,... | collective-permute-start | bytes 44 | tf_op jit(solution)/shard_map/ppermute | solution.py:921
  28.7 10.5 %collective-permute-start.2 = (s32[3]{0:T(128)S(1)}, s32[3]{0:T(128)S(1)}, u32[]{:S(2)}, u32[]{:S(2)}) collective-permute-start(s32[3]{0:T(128)S(1)} %bitcast.151), channel_id=1, source_target_pairs={{0,3},{1,0},{2,1},{3,2},{4,7},{5,4},{6,5},{7,6},{8,11},{9,8},{10,9... | collective-permute-start | bytes 44 | tf_op jit(solution)/shard_map/ppermute | solution.py:921
  29.4 23.2 %collective-permute-start.12 = (bf16[32,3072]{1,0:T(8,128)(2,1)}, bf16[32,3072]{1,0:T(8,128)(2,1)}, u32[]{:S(2)}, u32[]{:S(2)}) collective-permute-start(bf16[32,3072]{1,0:T(8,128)(2,1)} %param.34), channel_id=1, source_target_pairs={{0,1},{1,2},{2,3},{3,0},{4,5},{5,6},{6,7},{7,4},{8,9},{9,10},{10,1... | collective-permute-start | bytes 589832 | tf_op jit(solution)/shard_map/ppermute | solution.py:921
  30.7 23.6 %collective-permute-start.13 = (bf16[32,3072]{1,0:T(8,128)(2,1)}, bf16[32,3072]{1,0:T(8,128)(2,1)}, u32[]{:S(2)}, u32[]{:S(2)}) collective-permute-start(bf16[32,3072]{1,0:T(8,128)(2,1)} %param.34), channel_id=1, source_target_pairs={{0,2},{1,3},{2,0},{3,1},{4,6},{5,7},{6,4},{7,5},{8,10},{9,11},{10,... | collective-permute-start | bytes 589832 | tf_op jit(solution)/shard_map/ppermute | solution.py:921
  41.4 9.7 %collective-permute-start.4 = (f32[4,4096]{1,0:T(4,128)S(1)}, f32[4,4096]{1,0:T(4,128)S(1)}, u32[]{:S(2)}, u32[]{:S(2)}) collective-permute-start(f32[4,4096]{1,0:T(4,128)S(1)} %get-tuple-element.88), channel_id=1, source_target_pairs={{0,2},{1,3},{2,0},{3,1},{4,6},{5,7},{6,4},{7,5},{8,10},{9,11},{10,... | collective-permute-start | bytes 196616 | tf_op jit(solution)/shard_map/ppermute | solution.py:921
  43.4 7.8 %collective-permute-start.3 = (f32[4,4096]{1,0:T(4,128)S(1)}, f32[4,4096]{1,0:T(4,128)S(1)}, u32[]{:S(2)}, u32[]{:S(2)}) collective-permute-start(f32[4,4096]{1,0:T(4,128)S(1)} %get-tuple-element.87), channel_id=1, source_target_pairs={{0,1},{1,2},{2,3},{3,0},{4,5},{5,6},{6,7},{7,4},{8,9},{9,10},{10,1... | collective-permute-start | bytes 196616 | tf_op jit(solution)/shard_map/ppermute | solution.py:921
  45.6 10.4 %collective-permute-start.14 = (bf16[32,3072]{1,0:T(8,128)(2,1)}, bf16[32,3072]{1,0:T(8,128)(2,1)S(1)}, u32[]{:S(2)}, u32[]{:S(2)}) collective-permute-start(bf16[32,3072]{1,0:T(8,128)(2,1)} %param.34), channel_id=1, source_target_pairs={{0,3},{1,0},{2,1},{3,2},{4,7},{5,4},{6,5},{7,6},{8,11},{9,8},{10,9... | collective-permute-start | bytes 589832 | tf_op jit(solution)/shard_map/ppermute | solution.py:921
  51.1 34.5 %collective-permute-start.15 = (bf16[384,1024]{1,0:T(8,128)(2,1)}, bf16[384,1024]{1,0:T(8,128)(2,1)}, u32[]{:S(2)}, u32[]{:S(2)}) collective-permute-start(bf16[384,1024]{1,0:T(8,128)(2,1)} %fusion.1.branch_ref.refs_4_), channel_id=1, source_target_pairs={{0,4},{4,0},{8,12},{12,8},{16,20},{20,16},{24,28},{28,24},{1,5},{5... | collective-permute-start | bytes 2359304 | tf_op jit(solution)/shard_map/ppermute | solution.py:916
  51.1 34.5 %collective-permute-start.16 = (bf16[2048,384]{1,0:T(8,128)(2,1)S(1)}, bf16[2048,384]{1,0:T(8,128)(2,1)S(1)}, u32[]{:S(2)}, u32[]{:S(2)}) collective-permute-start(bf16[2048,384]{1,0:T(8,128)(2,1)S(1)} %pad_maximum_fusion.2.refs_0_.refs_1_), channel_id=1, source_target_pairs={{0,4},{4,0},{8,12},{12,8},{16,20},{20,16},{24,28},{28,24},{1,5},{5... | collective-permute-start | bytes 4718600 | tf_op jit(solution)/shard_map/ppermute | solution.py:916
  52.6 18.8 %collective-permute-start.6 = (f32[4,4096]{1,0:T(4,128)S(1)}, f32[4,4096]{1,0:T(4,128)S(1)}, u32[]{:S(2)}, u32[]{:S(2)}) collective-permute-start(f32[4,4096]{1,0:T(4,128)S(1)} %fusion.11), channel_id=1, source_target_pairs={{0,4},{4,0},{8,12},{12,8},{16,20},{20,16},{24,28},{28,24},{1,5},{5... | collective-permute-start | bytes 196616 | tf_op jit(solution)/shard_map/ppermute | solution.py:916
  59.0 23.8 %all-to-all-start = ((bf16[8,3,4,32,128]{4,3,2,1,0:T(8,128)(2,1)}), bf16[8,3,4,32,128]{4,3,2,1,0:T(8,128)(2,1)}, u32[]{:S(2)}, u32[]{:S(2)}) async-start(bf16[8,3,4,32,128]{4,3,2,1,0:T(8,128)(2,1)} %copy.74), calls=%async_computation | async-start | bytes 1572864 | tf_op jit(solution)/shard_map/all_to_all | solution.py:1094
  63.2 209.2 %all-gather.7.cloned.1.call-start = ((), (), s32[]{:S(2)}) async-start(), calls=%async_computation.7 | async-start | bytes 7077888 | tf_op jit(solution)/shard_map/all_gather | solution.py:1103
  94.2 18.8 %collective-permute-start.17 = (bf16[384,512]{1,0:T(8,128)(2,1)}, bf16[384,512]{1,0:T(8,128)(2,1)S(1)}, u32[]{:S(2)}, u32[]{:S(2)}) collective-permute-start(bf16[384,512]{1,0:T(8,128)(2,1)} %get-tuple-element.42), channel_id=1, source_target_pairs={{0,8},{4,12},{8,0},{12,4},{16,24},{20,28},{24,16},{28,20},{1,9},{5... | collective-permute-start | bytes 1179656 | tf_op jit(solution)/shard_map/ppermute | solution.py:916
  95.6 18.8 %collective-permute-start.20 = (bf16[384,512]{1,0:T(8,128)(2,1)}, bf16[384,512]{1,0:T(8,128)(2,1)S(1)}, u32[]{:S(2)}, u32[]{:S(2)}) collective-permute-start(bf16[384,512]{1,0:T(8,128)(2,1)} %get-tuple-element.43), channel_id=1, source_target_pairs={{0,16},{4,20},{8,24},{12,28},{16,0},{20,4},{24,8},{28,12},{1,17},{... | collective-permute-start | bytes 1179656 | tf_op jit(solution)/shard_map/ppermute | solution.py:916
  114.0 17.0 %collective-permute-start.18 = (bf16[2,384,512]{2,1,0:T(8,128)(2,1)S(1)}, bf16[2,384,512]{2,1,0:T(8,128)(2,1)S(1)}, u32[]{:S(2)}, u32[]{:S(2)}) collective-permute-start(bf16[2,384,512]{2,1,0:T(8,128)(2,1)S(1)} %get-tuple-element.86), channel_id=1, source_target_pairs={{0,16},{4,20},{8,24},{12,28},{16,0},{20,4},{24,8},{28,12},{1,17},{... | collective-permute-start | bytes 2359304 | tf_op jit(solution)/shard_map/ppermute | solution.py:916
  114.6 23.6 %collective-permute-start.21 = (bf16[2,384,512]{2,1,0:T(8,128)(2,1)S(1)}, bf16[2,384,512]{2,1,0:T(8,128)(2,1)S(1)}, u32[]{:S(2)}, u32[]{:S(2)}) collective-permute-start(bf16[2,384,512]{2,1,0:T(8,128)(2,1)S(1)} %get-tuple-element.84), channel_id=1, source_target_pairs={{0,8},{4,12},{8,0},{12,4},{16,24},{20,28},{24,16},{28,20},{1,9},{5... | collective-permute-start | bytes 2359304 | tf_op jit(solution)/shard_map/ppermute | solution.py:916
  132.3 7.8 %collective-permute-start.19 = (bf16[2,2,384,512]{3,2,1,0:T(8,128)(2,1)}, bf16[2,2,384,512]{3,2,1,0:T(8,128)(2,1)}, u32[]{:S(2)}, u32[]{:S(2)}) collective-permute-start(bf16[2,2,384,512]{3,2,1,0:T(8,128)(2,1)} %get-tuple-element.78), channel_id=1, source_target_pairs={{0,4},{4,0},{8,12},{12,8},{16,20},{20,16},{24,28},{28,24},{1,5},{5... | collective-permute-start | bytes 4718600 | tf_op jit(solution)/shard_map/ppermute | solution.py:916
  190.6 16.3 %all-to-all-start.1 = ((bf16[8,384,128]{2,1,0:T(8,128)(2,1)}), bf16[8,384,128]{2,1,0:T(8,128)(2,1)S(1)}, u32[]{:S(2)}, u32[]{:S(2)}) async-start(bf16[8,384,128]{2,1,0:T(8,128)(2,1)} %bitcast.134), calls=%async_computation.1 | async-start | bytes 1572864 | tf_op jit(solution)/shard_map/all_to_all | solution.py:1161
  236.4 15.6 %collective-permute-start.23 = (bf16[4096,384]{1,0:T(8,128)(2,1)}, bf16[4096,384]{1,0:T(8,128)(2,1)S(1)}, u32[]{:S(2)}, u32[]{:S(2)}) collective-permute-start(bf16[4096,384]{1,0:T(8,128)(2,1)} %get-tuple-element.49.refs_0_.refs_1_), channel_id=1, source_target_pairs={{0,4},{4,0},{8,12},{12,8},{16,20},{20,16},{24,28},{28,24},{1,5},{5... | collective-permute-start | bytes 9437192 | tf_op jit(solution)/shard_map/ppermute | solution.py:916
  236.5 15.6 %collective-permute-start.25 = (bf16[384,4096]{1,0:T(8,128)(2,1)}, bf16[384,4096]{1,0:T(8,128)(2,1)}, u32[]{:S(2)}, u32[]{:S(2)}) collective-permute-start(bf16[384,4096]{1,0:T(8,128)(2,1)} %get-tuple-element.51.refs_10_), channel_id=1, source_target_pairs={{0,4},{4,0},{8,12},{12,8},{16,20},{20,16},{24,28},{28,24},{1,5},{5... | collective-permute-start | bytes 9437192 | tf_op jit(solution)/shard_map/ppermute | solution.py:916
  237.0 12.4 %collective-permute-start.24 = (bf16[1024,384]{1,0:T(8,128)(2,1)}, bf16[1024,384]{1,0:T(8,128)(2,1)}, u32[]{:S(2)}, u32[]{:S(2)}) collective-permute-start(bf16[1024,384]{1,0:T(8,128)(2,1)} %get-tuple-element.50.refs_6_.refs_7_), channel_id=1, source_target_pairs={{0,4},{4,0},{8,12},{12,8},{16,20},{20,16},{24,28},{28,24},{1,5},{5... | collective-permute-start | bytes 2359304 | tf_op jit(solution)/shard_map/ppermute | solution.py:916
  237.1 13.4 %collective-permute-start.26 = (bf16[1024,384]{1,0:T(8,128)(2,1)}, bf16[1024,384]{1,0:T(8,128)(2,1)}, u32[]{:S(2)}, u32[]{:S(2)}) collective-permute-start(bf16[1024,384]{1,0:T(8,128)(2,1)} %get-tuple-element.52.refs_12_.refs_13_), channel_id=1, source_target_pairs={{0,4},{4,0},{8,12},{12,8},{16,20},{20,16},{24,28},{28,24},{1,5},{5... | collective-permute-start | bytes 2359304 | tf_op jit(solution)/shard_map/ppermute | solution.py:916
  237.5 14.5 %collective-permute-start.27 = (bf16[384,1024]{1,0:T(8,128)(2,1)}, bf16[384,1024]{1,0:T(8,128)(2,1)}, u32[]{:S(2)}, u32[]{:S(2)}) collective-permute-start(bf16[384,1024]{1,0:T(8,128)(2,1)} %get-tuple-element.53.refs_16_), channel_id=1, source_target_pairs={{0,4},{4,0},{8,12},{12,8},{16,20},{20,16},{24,28},{28,24},{1,5},{5... | collective-permute-start | bytes 2359304 | tf_op jit(solution)/shard_map/ppermute | solution.py:916
  238.1 34.3 %all-to-all-start.2 = ((bf16[8,384,128]{2,1,0:T(8,128)(2,1)}), bf16[8,384,128]{2,1,0:T(8,128)(2,1)}, u32[]{:S(2)}, u32[]{:S(2)}) async-start(bf16[8,384,128]{2,1,0:T(8,128)(2,1)} %get-tuple-element.47), calls=%async_computation.2 | async-start | bytes 1572864 | tf_op jit(solution)/shard_map/all_to_all | solution.py:1173
  262.8 69.3 %collective-permute-start.28 = (bf16[2,4,288,512]{3,2,1,0:T(8,128)(2,1)}, bf16[2,4,288,512]{3,2,1,0:T(8,128)(2,1)}, u32[]{:S(2)}, u32[]{:S(2)}) collective-permute-start(bf16[2,4,288,512]{3,2,1,0:T(8,128)(2,1)} %outer.8.rest_0_), channel_id=1, source_target_pairs={{0,8},{4,12},{8,0},{12,4},{16,24},{20,28},{24,16},{28,20},{1,9},{5... | collective-permute-start | bytes 7077896 | tf_op jit(solution)/shard_map/ppermute | solution.py:916
  272.0 60.1 %collective-permute-start.29 = (bf16[2,4,288,512]{3,2,1,0:T(8,128)(2,1)}, bf16[2,4,288,512]{3,2,1,0:T(8,128)(2,1)S(1)}, u32[]{:S(2)}, u32[]{:S(2)}) collective-permute-start(bf16[2,4,288,512]{3,2,1,0:T(8,128)(2,1)} %outer.9.rest_1_), channel_id=1, source_target_pairs={{0,16},{4,20},{8,24},{12,28},{16,0},{20,4},{24,8},{28,12},{1,17},{... | collective-permute-start | bytes 7077896 | tf_op jit(solution)/shard_map/ppermute | solution.py:916
  345.4 71.4 %all-to-all-start.3 = ((bf16[8,3,512,128]{3,2,1,0:T(8,128)(2,1)}), bf16[8,3,512,128]{3,2,1,0:T(8,128)(2,1)S(1)}, u32[]{:S(2)}, u32[]{:S(2)}) async-start(bf16[8,3,512,128]{3,2,1,0:T(8,128)(2,1)} %outgoing.1.refs_19_), calls=%async_computation.3 | async-start | bytes 6291456 | tf_op jit(solution)/shard_map/all_to_all | solution.py:1194
  360.5 51.8 %collective-permute-start.30 = (bf16[4,288,512]{2,1,0:T(8,128)(2,1)}, bf16[4,288,512]{2,1,0:T(8,128)(2,1)}, u32[]{:S(2)}, u32[]{:S(2)}) collective-permute-start(bf16[4,288,512]{2,1,0:T(8,128)(2,1)} %get-tuple-element.58), channel_id=1, source_target_pairs={{0,16},{4,20},{8,24},{12,28},{16,0},{20,4},{24,8},{28,12},{1,17},{... | collective-permute-start | bytes 3538952 | tf_op jit(solution)/shard_map/ppermute | solution.py:916
  372.5 39.9 %collective-permute-start.31 = (bf16[4,288,512]{2,1,0:T(8,128)(2,1)}, bf16[4,288,512]{2,1,0:T(8,128)(2,1)}, u32[]{:S(2)}, u32[]{:S(2)}) collective-permute-start(bf16[4,288,512]{2,1,0:T(8,128)(2,1)} %get-tuple-element.60), channel_id=1, source_target_pairs={{0,8},{4,12},{8,0},{12,4},{16,24},{20,28},{24,16},{28,20},{1,9},{5... | collective-permute-start | bytes 3538952 | tf_op jit(solution)/shard_map/ppermute | solution.py:916
  418.4 68.0 %all-to-all-start.4 = ((bf16[4,2,288,512]{3,2,1,0:T(8,128)(2,1)}), bf16[4,2,288,512]{3,2,1,0:T(8,128)(2,1)}, u32[]{:S(2)}, u32[]{:S(2)}) async-start(bf16[4,2,288,512]{3,2,1,0:T(8,128)(2,1)} %merge.2.rest_0_), calls=%async_computation.4 | async-start | bytes 4718592 | tf_op jit(solution)/shard_map/all_to_all | solution.py:988
  441.4 14.2 %collective-permute-start.34 = (bf16[2,4,64,512]{3,2,1,0:T(8,128)(2,1)}, bf16[2,4,64,512]{3,2,1,0:T(8,128)(2,1)S(1)}, u32[]{:S(2)}, u32[]{:S(2)}) collective-permute-start(bf16[2,4,64,512]{3,2,1,0:T(8,128)(2,1)} %outer.12.rest_0_), channel_id=1, source_target_pairs={{0,8},{4,12},{8,0},{12,4},{16,24},{20,28},{24,16},{28,20},{1,9},{5... | collective-permute-start | bytes 1572872 | tf_op jit(solution)/shard_map/ppermute | solution.py:916
  446.3 13.9 %collective-permute-start.35 = (bf16[2,4,64,512]{3,2,1,0:T(8,128)(2,1)}, bf16[2,4,64,512]{3,2,1,0:T(8,128)(2,1)S(1)}, u32[]{:S(2)}, u32[]{:S(2)}) collective-permute-start(bf16[2,4,64,512]{3,2,1,0:T(8,128)(2,1)} %outer.13.rest_1_), channel_id=1, source_target_pairs={{0,16},{4,20},{8,24},{12,28},{16,0},{20,4},{24,8},{28,12},{1,17},{... | collective-permute-start | bytes 1572872 | tf_op jit(solution)/shard_map/ppermute | solution.py:916
  465.6 13.0 %collective-permute-start.38 = (bf16[4,64,512]{2,1,0:T(8,128)(2,1)S(1)}, bf16[4,64,512]{2,1,0:T(8,128)(2,1)S(1)}, u32[]{:S(2)}, u32[]{:S(2)}) collective-permute-start(bf16[4,64,512]{2,1,0:T(8,128)(2,1)S(1)} %copy-done.15), channel_id=1, source_target_pairs={{0,16},{4,20},{8,24},{12,28},{16,0},{20,4},{24,8},{28,12},{1,17},{... | collective-permute-start | bytes 786440 | tf_op jit(solution)/shard_map/ppermute | solution.py:916
  466.7 12.0 %collective-permute-start.39 = (bf16[4,64,512]{2,1,0:T(8,128)(2,1)}, bf16[4,64,512]{2,1,0:T(8,128)(2,1)S(1)}, u32[]{:S(2)}, u32[]{:S(2)}) collective-permute-start(bf16[4,64,512]{2,1,0:T(8,128)(2,1)} %get-tuple-element.66.refs_2_), channel_id=1, source_target_pairs={{0,8},{4,12},{8,0},{12,4},{16,24},{20,28},{24,16},{28,20},{1,9},{5... | collective-permute-start | bytes 786440 | tf_op jit(solution)/shard_map/ppermute | solution.py:916
  469.9 6.1 %collective-permute-start.37 = (f32[4,4096]{1,0:T(4,128)S(1)}, f32[4,4096]{1,0:T(4,128)S(1)}, u32[]{:S(2)}, u32[]{:S(2)}) collective-permute-start(f32[4,4096]{1,0:T(4,128)S(1)} %add.217), channel_id=1, source_target_pairs={{0,16},{4,20},{8,24},{12,28},{16,0},{20,4},{24,8},{28,12},{1,17},{... | collective-permute-start | bytes 196616 | tf_op jit(solution)/shard_map/ppermute | solution.py:916
  471.7 40.7 %collective-permute-start.43 = (bf16[32,3072]{1,0:T(8,128)(2,1)S(1)}, bf16[32,3072]{1,0:T(8,128)(2,1)S(1)}, u32[]{:S(2)}, u32[]{:S(2)}) collective-permute-start(bf16[32,3072]{1,0:T(8,128)(2,1)S(1)} %get-tuple-element.81), channel_id=1, source_target_pairs={{0,1},{1,2},{2,3},{3,0},{4,5},{5,6},{6,7},{7,4},{8,9},{9,10},{10,1... | collective-permute-start | bytes 589832 | tf_op jit(solution)/shard_map/ppermute | solution.py:921
  473.7 38.8 %collective-permute-start.44 = (bf16[32,3072]{1,0:T(8,128)(2,1)S(1)}, bf16[32,3072]{1,0:T(8,128)(2,1)S(1)}, u32[]{:S(2)}, u32[]{:S(2)}) collective-permute-start(bf16[32,3072]{1,0:T(8,128)(2,1)S(1)} %get-tuple-element.80), channel_id=1, source_target_pairs={{0,2},{1,3},{2,0},{3,1},{4,6},{5,7},{6,4},{7,5},{8,10},{9,11},{10,... | collective-permute-start | bytes 589832 | tf_op jit(solution)/shard_map/ppermute | solution.py:921
  476.0 36.4 %collective-permute-start.45 = (bf16[32,3072]{1,0:T(8,128)(2,1)S(1)}, bf16[32,3072]{1,0:T(8,128)(2,1)}, u32[]{:S(2)}, u32[]{:S(2)}) collective-permute-start(bf16[32,3072]{1,0:T(8,128)(2,1)S(1)} %get-tuple-element.79), channel_id=1, source_target_pairs={{0,3},{1,0},{2,1},{3,2},{4,7},{5,4},{6,5},{7,6},{8,11},{9,8},{10,9... | collective-permute-start | bytes 589832 | tf_op jit(solution)/shard_map/ppermute | solution.py:921
  488.5 9.4 %collective-permute-start.40 = (f32[4,4096]{1,0:T(4,128)}, f32[4,4096]{1,0:T(4,128)S(1)}, u32[]{:S(2)}, u32[]{:S(2)}) collective-permute-start(f32[4,4096]{1,0:T(4,128)} %tie.4), channel_id=1, source_target_pairs={{0,1},{1,2},{2,3},{3,0},{4,5},{5,6},{6,7},{7,4},{8,9},{9,10},{10,1... | collective-permute-start | bytes 196616 | tf_op jit(solution)/shard_map/ppermute | solution.py:921
  488.5 14.6 %collective-permute-start.41 = (f32[4,4096]{1,0:T(4,128)}, f32[4,4096]{1,0:T(4,128)S(1)}, u32[]{:S(2)}, u32[]{:S(2)}) collective-permute-start(f32[4,4096]{1,0:T(4,128)} %tie.4), channel_id=1, source_target_pairs={{0,2},{1,3},{2,0},{3,1},{4,6},{5,7},{6,4},{7,5},{8,10},{9,11},{10,... | collective-permute-start | bytes 196616 | tf_op jit(solution)/shard_map/ppermute | solution.py:921
  488.5 21.3 %all-to-all-start.5 = ((bf16[4,2,64,512]{3,2,1,0:T(8,128)(2,1)}), bf16[4,2,64,512]{3,2,1,0:T(8,128)(2,1)S(1)}, u32[]{:S(2)}, u32[]{:S(2)}) async-start(bf16[4,2,64,512]{3,2,1,0:T(8,128)(2,1)} %merge.3.refs_1_.rest_0_), calls=%async_computation.5 | async-start | bytes 1048576 | tf_op jit(solution)/shard_map/all_to_all | solution.py:988
  498.0 7.2 %collective-permute-start.42 = (f32[4,4096]{1,0:T(4,128)S(1)}, f32[4,4096]{1,0:T(4,128)S(1)}, u32[]{:S(2)}, u32[]{:S(2)}) collective-permute-start(f32[4,4096]{1,0:T(4,128)S(1)} %copy-done.14), channel_id=1, source_target_pairs={{0,3},{1,0},{2,1},{3,2},{4,7},{5,4},{6,5},{7,6},{8,11},{9,8},{10,9... | collective-permute-start | bytes 196616 | tf_op jit(solution)/shard_map/ppermute | solution.py:921
  (50 other events, 324.8 us)
Sparse Core Ops, SparseCore 0:
  22.8 38.7 all-gather.4
  65.0 138.2 all-gather.8
  205.8 45.9 all-gather.6

commit v5 on v4

--- a/solution.py
+++ b/solution.py
@@ -1030,7 +1030,7 @@
     have = []
     for bit in bits:
         came = swap(value, bit)
-        value = jnp.stack([value, came], axis=sum(b > bit for b in have))
+        value = jnp.stack([value, came], axis=sum(b > bit for b in have) if bit > 1 else 0)
         have.append(bit)
     return value.reshape((lax.axis_size("seq"),) + value.shape[len(have) :])
 
@@ -1078,6 +1078,7 @@
     high = [seq >> (i + 1) for i in range(seq.bit_length() - 2)]
     low = high[::-1]
     rel = (jnp.arange(seq, dtype=jnp.int32) ^ seq_at).astype(jnp.int32)
+    spot = (rel & 1) * (seq // 2) + (rel >> 1)
     half = width // 2
     skip_each, qkv_each, out_each, up_each, down_each = (
         skip_proj.shape[0],
@@ -1156,7 +1157,7 @@
         (group_cos, group_sin, own_qkv, branch_pair[1], joined_pair[1]),
     )
     normed_halves = [seq_pieces(normed_one[0], low + [1]), seq_pieces(normed_one[1], high + [1])]
-    held = project(rel, normed_halves, own_qkv, group_cos, group_sin, ())
+    held = project(spot, normed_halves, own_qkv, group_cos, group_sin, ())
     head_out, log_sums = attend(held, ends, heads, 1536, 1536)
     att = lax.all_to_all(
         head_out.reshape(seq, rows, LANES)[:, :, :per_device], "seq", 0, 0, tiled=True
@@ -1189,7 +1190,7 @@
     grad_held = attend_back(
         held, back, head_out, log_sums, group_cos, group_sin, ends, heads, waits + [full_qkv], 1024, 1024
     )
-    grad_held = outgoing(rel, grad_held, normed_halves, tuple(sums.came()))
+    grad_held = outgoing(spot, grad_held, normed_halves, tuple(sums.came()))
     mark = (grad_held,)
     grad_held = lax.all_to_all(grad_held[..., :per_device], "seq", 0, 0, tiled=True)
     if per_device < LANES:

time: 530 us -> 535 us (level)
  transfers between devices with their start and end apart: 55 -> 55, of which waited for: 23 -> 22; matrix products, arithmetic and copies ran while one was open for 10% -> 10% of each run, Pallas kernels for 42% -> 41%
where the time goes in v5:
time: 535 us; the launch traced here: 526 us
  Pallas kernels  232 us (43%)
  waiting for transfers between devices  133 us (25%)
  starting transfers between devices  80.6 us (15%)
  local copies, waits for them, and re-layouts  36.5 us (7%)
  other arithmetic  27 us (5%)
  between operations  15 us (3%)
    ppermute x28, waiting for transfers between devices, swap(): return lax.ppermute(value, 'seq', [(i, i ^ bit) for i in range(size)])  99.2 us
    pallas_call x1, Pallas kernels, attend_back(): pl.pallas_call(functools.partial(bwd_kernel, heads=heads, utts=utts, bq=b...  59.7 us
    pallas_call x8, Pallas kernels, outer(): pl.pallas_call(functools.partial(outer_kernel, sizes=sizes, counts=counts...  52.1 us
    ppermute x18, starting transfers between devices, ahead(): lax.ppermute(value, 'batch', [(i, (i + step) % size) for i in range(size)])  31.8 us
    pallas_call x1, Pallas kernels, attend(): pl.pallas_call(functools.partial(fwd_kernel, heads=heads, utts=utts, bq=b...  31.8 us
    pallas_call x1, Pallas kernels, middle(): pl.pallas_call(functools.partial(middle_kernel, utts=utts, blocks=blocks)...  28.9 us
    ppermute x28, starting transfers between devices, swap(): return lax.ppermute(value, 'seq', [(i, i ^ bit) for i in range(size)])  21.9 us
    unnamed x95, local copies, waits for them, and re-layouts  16.9 us
  transfers between devices with their start and end apart: 55, of which 22 were waited for; matrix products, arithmetic and copies ran while one was open for 10% of the time, Pallas kernels for 41%

profile of v5, /device:TPU:0, one launch (start us, length us, event | category | flops | bytes accessed | tf_op | source)
XLA Modules:
  0.0 526.3 jit_solution(12846705658114796132)
XLA Ops:
  7.3 3.1 collective-permute-start.9
  10.3 2.6 collective-permute-start.10
  17.0 4.8 collective-permute-done.10
  23.7 3.3 collective-permute-start
  45.6 2.6 collective-permute-start.14
  48.2 2.9 collective-permute-done.4
  59.0 4.2 all-to-all-start
  63.6 7.8 %fusion = (f32[3072,128]{1,0:T(8,128)}, f32[3072,128]{1,0:T(8,128)}) fusion(f32[128]{0:T(128)} %get-tuple-element.94, f32[128]{0:T(128)} %get-tuple-element.95, f32[3072]{0:T(1024)S(1)} %subtract_convert_fusion), kind=kLoop, calls=%fused_computation.5 | loop fusion | flops 786432 | bytes 3159040 | tf_op jit(solution)/shard_map/mul | solution.py:1004
  73.5 2.9 collective-permute-done.7
  78.7 3.4 collective-permute-done.8
  86.8 7.4 %front.1 = (f32[384,1024]{1,0:T(8,128)}, bf16[384,512]{1,0:T(8,128)(2,1)}, bf16[384,512]{1,0:T(8,128)(2,1)}) custom-call(bf16[384,1024]{1,0:T(8,128)(2,1)} %bitcast.126, bf16[384,1024]{1,0:T(8,128)(2,1)} %bitcast.127, f32[384,128]{1,0:T(8,128)} %pad_convert_fusion.info_ref, f32[3,4096]{1,0:T(4,128)} %bitcast.135, ...), custom_call_target="tpu_custom_call" | custom-call | flops 1610612736 | bytes 8388608 | tf_op jit(solution)/shard_map/front/pallas_call | solution.py:429
  94.5 2.3 collective-permute-start.17
  96.8 16.2 %collective-permute-done.20 = bf16[384,512]{1,0:T(8,128)(2,1)S(1)} collective-permute-done((bf16[384,512]{1,0:T(8,128)(2,1)}, bf16[384,512]{1,0:T(8,128)(2,1)S(1)}, u32[]{:S(2)}, u32[]{:S(2)}) %collective-permute-start.20) | collective-permute-done | bytes 393248 | tf_op jit(solution)/shard_map/ppermute | solution.py:916
  116.1 22.7 %collective-permute-done.21 = bf16[2,384,512]{2,1,0:T(8,128)(2,1)S(1)} collective-permute-done((bf16[2,384,512]{2,1,0:T(8,128)(2,1)S(1)}, bf16[2,384,512]{2,1,0:T(8,128)(2,1)S(1)}, u32[]{:S(2)}, u32[]{:S(2)}) %collective-permute-start.21) | collective-permute-done | bytes 786464 | tf_op jit(solution)/shard_map/ppermute | solution.py:916
  145.6 2.3 copy.74
  147.9 3.8 pad_maximum_fusion
  151.7 11.1 %project.1.qkv_ref = bf16[8,3,384,128]{3,2,1,0:T(8,128)(2,1)} custom-call(s32[8]{0:T(128)} %shift-right-arithmetic_add_fusion.rel_ref, bf16[8,384,512]{2,1,0:T(8,128)(2,1)} %bitcast.120, bf16[8,384,512]{2,1,0:T(8,128)(2,1)} %bitcast.118, bf16[1024,384]{1,0:T(8,128)(2,1)} %bitcast.123, f32[3072,128]{1,0:T(8,128)} %get-tuple-element.93.rest_0_.cos_ref, ...), custom_call_target="tpu_custom_call" | custom-call | flops 2415919104 | bytes 4194304 | tf_op jit(solution)/shard_map/project/pallas_call | solution.py:474
  162.8 31.8 %attend.1 = (bf16[3072,128]{1,0:T(8,128)(2,1)}, f32[3072,128]{1,0:T(8,128)}) custom-call(s32[3]{0:T(128)} %bitcast.144, bf16[8,3,384,128]{3,2,1,0:T(8,128)(2,1)} %project.1.qkv_ref), custom_call_target="tpu_custom_call" | custom-call | flops 48318382080 | bytes 4718592 | tf_op jit(solution)/shard_map/attend/pallas_call | solution.py:119
  194.6 3.7 all-to-all-start.1
  199.8 11.1 %all-to-all-done.1.att_ref = bf16[8,384,128]{2,1,0:T(8,128)(2,1)S(1)} async-done(((bf16[8,384,128]{2,1,0:T(8,128)(2,1)}), bf16[8,384,128]{2,1,0:T(8,128)(2,1)S(1)}, u32[]{:S(2)}, u32[]{:S(2)}) %all-to-all-start.1) | async-done | bytes 786464 | tf_op jit(solution)/shard_map/all_to_all | solution.py:1162
  211.8 28.9 %middle.1 = (bf16[384,1024]{1,0:T(8,128)(2,1)}, bf16[1024,384]{1,0:T(8,128)(2,1)}, bf16[1024,384]{1,0:T(8,128)(2,1)}, bf16[4096,384]{1,0:T(8,128)(2,1)}, bf16[38...) custom-call(bf16[8,384,128]{2,1,0:T(8,128)(2,1)} %copy-done.17, ...), custom_call_target="tpu_custom_call" | custom-call | flops 19327352832 | bytes 20971520 | tf_op jit(solution)/shard_map/middle/pallas_call | solution.py:574
  242.4 4.4 all-to-all-start.2
  247.4 6.5 %collective-permute-done.24.refs_8_.refs_9_ = bf16[1024,384]{1,0:T(8,128)(2,1)} collective-permute-done((bf16[1024,384]{1,0:T(8,128)(2,1)}, bf16[1024,384]{1,0:T(8,128)(2,1)}, u32[]{:S(2)}, u32[]{:S(2)}) %collective-permute-start.24) | collective-permute-done | bytes 786464 | tf_op jit(solution)/shard_map/ppermute | solution.py:916
  257.8 9.1 %outer.8.rest_0_ = bf16[2,4,288,512]{3,2,1,0:T(8,128)(2,1)} custom-call(s32[2]{0:T(128)} %fusion.33.pick_ref, bf16[4096,384]{1,0:T(8,128)(2,1)} %get-tuple-element.49.refs_0_.refs_1_, bf16[4096,384]{1,0:T(8,128)(2,1)} %get-tuple-element.49.refs_0_.refs_1_, bf16[4096,384]{1,0:T(8,128)(2,1)} %copy-done.1, bf16[4096,384]{1,0:T(8,128)(2,1)} %copy-done.1, ...), custom_call_target="tpu_custom_call" | custom-call | flops 3623878656 | bytes 6039797 | tf_op jit(solution)/shard_map/outer/pallas_call | solution.py:791
  267.4 9.1 %outer.9.rest_1_ = bf16[2,4,288,512]{3,2,1,0:T(8,128)(2,1)} custom-call(s32[2]{0:T(128)} %fusion.31.pick_ref, bf16[4096,384]{1,0:T(8,128)(2,1)} %get-tuple-element.49.refs_0_.refs_1_, bf16[4096,384]{1,0:T(8,128)(2,1)} %get-tuple-element.49.refs_0_.refs_1_, bf16[4096,384]{1,0:T(8,128)(2,1)} %copy-done.1, bf16[4096,384]{1,0:T(8,128)(2,1)} %copy-done.1, ...), custom_call_target="tpu_custom_call" | custom-call | flops 3623878656 | bytes 6039797 | tf_op jit(solution)/shard_map/outer/pallas_call | solution.py:791
  277.1 59.7 %attend_back.1.grad_ref = bf16[8,3,384,128]{3,2,1,0:T(8,128)(2,1)} custom-call(s32[3]{0:T(128)} %bitcast.145, bf16[8,3,384,128]{3,2,1,0:T(8,128)(2,1)} %project.1.qkv_ref, bf16[3072,128]{1,0:T(8,128)(2,1)} %bitcast.48.da_ref, bf16[3072,128]{1,0:T(8,128)(2,1)} %get-tuple-element.44.out_ref, f32[3072,128]{1,0:T(8,128)} %get-tuple-element.48.lse_ref, ...), custom_call_target="tpu_custom_call" | custom-call | flops 77309411328 | bytes 9437184 | tf_op jit(solution)/shard_map/attend_back/pallas_call | solution.py:242
  338.3 11.8 %outgoing.1.refs_19_ = bf16[8,3,512,128]{3,2,1,0:T(8,128)(2,1)} custom-call(s32[8]{0:T(128)} %shift-right-arithmetic_add_fusion.rel_ref, bf16[8,3,384,128]{3,2,1,0:T(8,128)(2,1)} %attend_back.1.grad_ref, bf16[8,384,512]{2,1,0:T(8,128)(2,1)} %bitcast.121, bf16[8,384,512]{2,1,0:T(8,128)(2,1)} %bitcast.119, ...), custom_call_target="tpu_custom_call" | custom-call | flops 2415919104 | bytes 4194304 | tf_op jit(solution)/shard_map/outgoing/pallas_call | solution.py:298
  350.1 4.0 all-to-all-start.3
  354.7 9.9 %outer.10 = (bf16[4,288,512]{2,1,0:T(8,128)(2,1)}, bf16[4,288,512]{2,1,0:T(8,128)(2,1)}) custom-call(s32[2]{0:T(128)} %get-tuple-element.97.pick_ref, bf16[4096,384]{1,0:T(8,128)(2,1)} %get-tuple-element.49.refs_0_.refs_1_, bf16[4096,384]{1,0:T(8,128)(2,1)} %get-tuple-element.49.refs_0_.refs_1_, bf16[4096,384]{1,0:T(8,128)(2,1)} %copy-done.1, ...), custom_call_target="tpu_custom_call" | custom-call | flops 3623878656 | bytes 6039797 | tf_op jit(solution)/shard_map/outer/pallas_call | solution.py:791
  364.6 2.1 collective-permute-start.30
  366.7 9.9 %outer.11 = (bf16[4,288,512]{2,1,0:T(8,128)(2,1)}, bf16[4,288,512]{2,1,0:T(8,128)(2,1)}) custom-call(s32[2]{0:T(128)} %get-tuple-element.96.pick_ref, bf16[4096,384]{1,0:T(8,128)(2,1)} %get-tuple-element.49.refs_0_.refs_1_, bf16[4096,384]{1,0:T(8,128)(2,1)} %get-tuple-element.49.refs_0_.refs_1_, bf16[4096,384]{1,0:T(8,128)(2,1)} %copy-done.1, ...), custom_call_target="tpu_custom_call" | custom-call | flops 3623878656 | bytes 6039797 | tf_op jit(solution)/shard_map/outer/pallas_call | solution.py:791
  378.1 38.3 %collective-permute-done.30.refs_1_ = bf16[4,288,512]{2,1,0:T(8,128)(2,1)} collective-permute-done((bf16[4,288,512]{2,1,0:T(8,128)(2,1)}, bf16[4,288,512]{2,1,0:T(8,128)(2,1)}, u32[]{:S(2)}, u32[]{:S(2)}) %collective-permute-start.30) | collective-permute-done | bytes 1179680 | tf_op jit(solution)/shard_map/ppermute | solution.py:916
  416.5 4.3 merge.2.rest_0_
  422.5 4.5 all-to-all-start.4
  427.0 10.0 %tail.1 = (bf16[384,1024]{1,0:T(8,128)(2,1)}, f32[4,4096]{1,0:T(4,128)}) custom-call(bf16[8,3,512,128]{3,2,1,0:T(8,128)(2,1)} %copy-done.4, f32[384,1024]{1,0:T(8,128)} %get-tuple-element.45.stream_ref, f32[384,128]{1,0:T(8,128)} %pad_convert_fusion.info_ref, f32[3,4096]{1,0:T(4,128)} %bitcast.137, f32[384,1024]{1,0:T(8,128)} %get-tuple-element.54.mid_ref, ...), custom_call_target="tpu_custom_call" | custom-call | flops 2415919104 | bytes 14680064 | tf_op jit(solution)/shard_map/tail/pallas_call | solution.py:669
  437.5 2.1 collective-permute-done.33
  442.0 3.5 outer.12.rest_0_
  446.9 3.5 outer.13.rest_1_
  451.0 5.7 %unjoin.1 = (bf16[384,1024]{1,0:T(8,128)(2,1)}, bf16[384,1024]{1,0:T(8,128)(2,1)}) custom-call(bf16[384,1024]{1,0:T(8,128)(2,1)} %get-tuple-element.61.refs_4_.grad_ref, bf16[32,64,1024]{2,1,0:T(8,128)(2,1)} %all-gather.5.cloned.1.call-done.weight_ref, bf16[2,4,64,512]{3,2,1,0:T(8,128)(2,1)} %outer.12.rest_0_, bf16[2,4,64,512]{3,2,1,0:T(8,128)(2,1)} %outer.13.rest_1_), custom_call_target="tpu_custom_call" | custom-call | flops 1610612736 | bytes 6291456 | tf_op jit(solution)/shard_map/unjoin/pallas_call | solution.py:335
  456.7 3.0 collective-permute-done.34.refs_6_
  460.5 3.5 outer.14
  465.0 3.6 outer.15
  477.7 2.4 collective-permute-start.44
  482.8 7.7 %all-to-all-done.4.refs_5_.came_ref = bf16[4,2,288,512]{3,2,1,0:T(8,128)(2,1)} async-done(((bf16[4,2,288,512]{3,2,1,0:T(8,128)(2,1)}), bf16[4,2,288,512]{3,2,1,0:T(8,128)(2,1)}, u32[]{:S(2)}, u32[]{:S(2)}) %all-to-all-start.4) | async-done | bytes 2359328 | tf_op jit(solution)/shard_map/all_to_all | solution.py:988
  490.5 2.1 merge.3.refs_1_.rest_0_
  492.6 5.6 %all-to-all-start.5 = ((bf16[4,2,64,512]{3,2,1,0:T(8,128)(2,1)}), bf16[4,2,64,512]{3,2,1,0:T(8,128)(2,1)S(1)}, u32[]{:S(2)}, u32[]{:S(2)}) async-start(bf16[4,2,64,512]{3,2,1,0:T(8,128)(2,1)} %merge.3.refs_1_.rest_0_), calls=%async_computation.5 | async-start | bytes 1048576 | tf_op jit(solution)/shard_map/all_to_all | solution.py:988
  499.2 2.8 finish.3
  502.0 3.9 collective-permute-start.42
  (261 shorter events, 99.4 us)
Async XLA Ops:
  7.2 78.4 %all-gather.5.cloned.1.call-start = ((), (), s32[]{:S(2)}) async-start(), calls=%async_computation.6 | async-start | bytes 4718592 | tf_op jit(solution)/shard_map/all_gather | solution.py:1092
  7.3 9.7 %collective-permute-start.9 = (bf16[64,1024]{1,0:T(8,128)(2,1)}, bf16[64,1024]{1,0:T(8,128)(2,1)S(1)}, u32[]{:S(2)}, u32[]{:S(2)}) collective-permute-start(bf16[64,1024]{1,0:T(8,128)(2,1)} %param.31), channel_id=1, source_target_pairs={{0,1},{1,2},{2,3},{3,0},{4,5},{5,6},{6,7},{7,4},{8,9},{9,10},{10,1... | collective-permute-start | bytes 393224 | tf_op jit(solution)/shard_map/ppermute | solution.py:921
  10.3 11.4 %collective-permute-start.10 = (bf16[64,1024]{1,0:T(8,128)(2,1)}, bf16[64,1024]{1,0:T(8,128)(2,1)S(1)}, u32[]{:S(2)}, u32[]{:S(2)}) collective-permute-start(bf16[64,1024]{1,0:T(8,128)(2,1)} %param.31), channel_id=1, source_target_pairs={{0,2},{1,3},{2,0},{3,1},{4,6},{5,7},{6,4},{7,5},{8,10},{9,11},{10,... | collective-permute-start | bytes 393224 | tf_op jit(solution)/shard_map/ppermute | solution.py:921
  12.9 8.9 %collective-permute-start.11 = (bf16[64,1024]{1,0:T(8,128)(2,1)}, bf16[64,1024]{1,0:T(8,128)(2,1)S(1)}, u32[]{:S(2)}, u32[]{:S(2)}) collective-permute-start(bf16[64,1024]{1,0:T(8,128)(2,1)} %param.31), channel_id=1, source_target_pairs={{0,3},{1,0},{2,1},{3,2},{4,7},{5,4},{6,5},{7,6},{8,11},{9,8},{10,9... | collective-permute-start | bytes 393224 | tf_op jit(solution)/shard_map/ppermute | solution.py:921
  22.7 188.2 %all-gather.9.cloned.1.call-start = ((), (), s32[]{:S(2)}) async-start(), calls=%async_computation.8 | async-start | bytes 19464192 | tf_op jit(solution)/shard_map/all_gather | solution.py:1103
  23.7 15.4 %collective-permute-start = (s32[3]{0:T(128)S(1)}, s32[3]{0:T(128)S(1)}, u32[]{:S(2)}, u32[]{:S(2)}) collective-permute-start(s32[3]{0:T(128)S(1)} %bitcast.149), channel_id=1, source_target_pairs={{0,1},{1,2},{2,3},{3,0},{4,5},{5,6},{6,7},{7,4},{8,9},{9,10},{10,1... | collective-permute-start | bytes 44 | tf_op jit(solution)/shard_map/ppermute | solution.py:921
  27.0 12.1 %collective-permute-start.1 = (s32[3]{0:T(128)S(1)}, s32[3]{0:T(128)S(1)}, u32[]{:S(2)}, u32[]{:S(2)}) collective-permute-start(s32[3]{0:T(128)S(1)} %bitcast.150), channel_id=1, source_target_pairs={{0,2},{1,3},{2,0},{3,1},{4,6},{5,7},{6,4},{7,5},{8,10},{9,11},{10,... | collective-permute-start | bytes 44 | tf_op jit(solution)/shard_map/ppermute | solution.py:921
  28.7 10.5 %collective-permute-start.2 = (s32[3]{0:T(128)S(1)}, s32[3]{0:T(128)S(1)}, u32[]{:S(2)}, u32[]{:S(2)}) collective-permute-start(s32[3]{0:T(128)S(1)} %bitcast.151), channel_id=1, source_target_pairs={{0,3},{1,0},{2,1},{3,2},{4,7},{5,4},{6,5},{7,6},{8,11},{9,8},{10,9... | collective-permute-start | bytes 44 | tf_op jit(solution)/shard_map/ppermute | solution.py:921
  29.4 23.2 %collective-permute-start.12 = (bf16[32,3072]{1,0:T(8,128)(2,1)}, bf16[32,3072]{1,0:T(8,128)(2,1)}, u32[]{:S(2)}, u32[]{:S(2)}) collective-permute-start(bf16[32,3072]{1,0:T(8,128)(2,1)} %param.34), channel_id=1, source_target_pairs={{0,1},{1,2},{2,3},{3,0},{4,5},{5,6},{6,7},{7,4},{8,9},{9,10},{10,1... | collective-permute-start | bytes 589832 | tf_op jit(solution)/shard_map/ppermute | solution.py:921
  30.7 23.6 %collective-permute-start.13 = (bf16[32,3072]{1,0:T(8,128)(2,1)}, bf16[32,3072]{1,0:T(8,128)(2,1)}, u32[]{:S(2)}, u32[]{:S(2)}) collective-permute-start(bf16[32,3072]{1,0:T(8,128)(2,1)} %param.34), channel_id=1, source_target_pairs={{0,2},{1,3},{2,0},{3,1},{4,6},{5,7},{6,4},{7,5},{8,10},{9,11},{10,... | collective-permute-start | bytes 589832 | tf_op jit(solution)/shard_map/ppermute | solution.py:921
  41.4 9.7 %collective-permute-start.4 = (f32[4,4096]{1,0:T(4,128)S(1)}, f32[4,4096]{1,0:T(4,128)S(1)}, u32[]{:S(2)}, u32[]{:S(2)}) collective-permute-start(f32[4,4096]{1,0:T(4,128)S(1)} %get-tuple-element.88), channel_id=1, source_target_pairs={{0,2},{1,3},{2,0},{3,1},{4,6},{5,7},{6,4},{7,5},{8,10},{9,11},{10,... | collective-permute-start | bytes 196616 | tf_op jit(solution)/shard_map/ppermute | solution.py:921
  43.4 7.8 %collective-permute-start.3 = (f32[4,4096]{1,0:T(4,128)S(1)}, f32[4,4096]{1,0:T(4,128)S(1)}, u32[]{:S(2)}, u32[]{:S(2)}) collective-permute-start(f32[4,4096]{1,0:T(4,128)S(1)} %get-tuple-element.87), channel_id=1, source_target_pairs={{0,1},{1,2},{2,3},{3,0},{4,5},{5,6},{6,7},{7,4},{8,9},{9,10},{10,1... | collective-permute-start | bytes 196616 | tf_op jit(solution)/shard_map/ppermute | solution.py:921
  45.6 10.4 %collective-permute-start.14 = (bf16[32,3072]{1,0:T(8,128)(2,1)}, bf16[32,3072]{1,0:T(8,128)(2,1)S(1)}, u32[]{:S(2)}, u32[]{:S(2)}) collective-permute-start(bf16[32,3072]{1,0:T(8,128)(2,1)} %param.34), channel_id=1, source_target_pairs={{0,3},{1,0},{2,1},{3,2},{4,7},{5,4},{6,5},{7,6},{8,11},{9,8},{10,9... | collective-permute-start | bytes 589832 | tf_op jit(solution)/shard_map/ppermute | solution.py:921
  51.1 34.5 %collective-permute-start.15 = (bf16[384,1024]{1,0:T(8,128)(2,1)}, bf16[384,1024]{1,0:T(8,128)(2,1)}, u32[]{:S(2)}, u32[]{:S(2)}) collective-permute-start(bf16[384,1024]{1,0:T(8,128)(2,1)} %fusion.1.branch_ref.refs_4_), channel_id=1, source_target_pairs={{0,4},{4,0},{8,12},{12,8},{16,20},{20,16},{24,28},{28,24},{1,5},{5... | collective-permute-start | bytes 2359304 | tf_op jit(solution)/shard_map/ppermute | solution.py:916
  51.1 34.5 %collective-permute-start.16 = (bf16[2048,384]{1,0:T(8,128)(2,1)S(1)}, bf16[2048,384]{1,0:T(8,128)(2,1)S(1)}, u32[]{:S(2)}, u32[]{:S(2)}) collective-permute-start(bf16[2048,384]{1,0:T(8,128)(2,1)S(1)} %pad_maximum_fusion.2.refs_0_.refs_1_), channel_id=1, source_target_pairs={{0,4},{4,0},{8,12},{12,8},{16,20},{20,16},{24,28},{28,24},{1,5},{5... | collective-permute-start | bytes 4718600 | tf_op jit(solution)/shard_map/ppermute | solution.py:916
  52.6 18.8 %collective-permute-start.6 = (f32[4,4096]{1,0:T(4,128)S(1)}, f32[4,4096]{1,0:T(4,128)S(1)}, u32[]{:S(2)}, u32[]{:S(2)}) collective-permute-start(f32[4,4096]{1,0:T(4,128)S(1)} %fusion.11), channel_id=1, source_target_pairs={{0,4},{4,0},{8,12},{12,8},{16,20},{20,16},{24,28},{28,24},{1,5},{5... | collective-permute-start | bytes 196616 | tf_op jit(solution)/shard_map/ppermute | solution.py:916
  59.0 23.8 %all-to-all-start = ((bf16[8,3,4,32,128]{4,3,2,1,0:T(8,128)(2,1)}), bf16[8,3,4,32,128]{4,3,2,1,0:T(8,128)(2,1)}, u32[]{:S(2)}, u32[]{:S(2)}) async-start(bf16[8,3,4,32,128]{4,3,2,1,0:T(8,128)(2,1)} %copy.70), calls=%async_computation | async-start | bytes 1572864 | tf_op jit(solution)/shard_map/all_to_all | solution.py:1095
  63.2 213.9 %all-gather.7.cloned.1.call-start = ((), (), s32[]{:S(2)}) async-start(), calls=%async_computation.7 | async-start | bytes 7077888 | tf_op jit(solution)/shard_map/all_gather | solution.py:1104
  94.2 18.8 %collective-permute-start.20 = (bf16[384,512]{1,0:T(8,128)(2,1)}, bf16[384,512]{1,0:T(8,128)(2,1)S(1)}, u32[]{:S(2)}, u32[]{:S(2)}) collective-permute-start(bf16[384,512]{1,0:T(8,128)(2,1)} %get-tuple-element.43), channel_id=1, source_target_pairs={{0,16},{4,20},{8,24},{12,28},{16,0},{20,4},{24,8},{28,12},{1,17},{... | collective-permute-start | bytes 1179656 | tf_op jit(solution)/shard_map/ppermute | solution.py:916
  94.5 21.1 %collective-permute-start.17 = (bf16[384,512]{1,0:T(8,128)(2,1)}, bf16[384,512]{1,0:T(8,128)(2,1)S(1)}, u32[]{:S(2)}, u32[]{:S(2)}) collective-permute-start(bf16[384,512]{1,0:T(8,128)(2,1)} %get-tuple-element.42), channel_id=1, source_target_pairs={{0,8},{4,12},{8,0},{12,4},{16,24},{20,28},{24,16},{28,20},{1,9},{5... | collective-permute-start | bytes 1179656 | tf_op jit(solution)/shard_map/ppermute | solution.py:916
  114.1 24.7 %collective-permute-start.21 = (bf16[2,384,512]{2,1,0:T(8,128)(2,1)S(1)}, bf16[2,384,512]{2,1,0:T(8,128)(2,1)S(1)}, u32[]{:S(2)}, u32[]{:S(2)}) collective-permute-start(bf16[2,384,512]{2,1,0:T(8,128)(2,1)S(1)} %get-tuple-element.84), channel_id=1, source_target_pairs={{0,8},{4,12},{8,0},{12,4},{16,24},{20,28},{24,16},{28,20},{1,9},{5... | collective-permute-start | bytes 2359304 | tf_op jit(solution)/shard_map/ppermute | solution.py:916
  115.7 24.5 %collective-permute-start.18 = (bf16[2,384,512]{2,1,0:T(8,128)(2,1)S(1)}, bf16[2,384,512]{2,1,0:T(8,128)(2,1)S(1)}, u32[]{:S(2)}, u32[]{:S(2)}) collective-permute-start(bf16[2,384,512]{2,1,0:T(8,128)(2,1)S(1)} %get-tuple-element.86), channel_id=1, source_target_pairs={{0,16},{4,20},{8,24},{12,28},{16,0},{20,4},{24,8},{28,12},{1,17},{... | collective-permute-start | bytes 2359304 | tf_op jit(solution)/shard_map/ppermute | solution.py:916
  141.5 6.4 %collective-permute-start.19 = (bf16[2,2,384,512]{3,2,1,0:T(8,128)(2,1)}, bf16[2,2,384,512]{3,2,1,0:T(8,128)(2,1)}, u32[]{:S(2)}, u32[]{:S(2)}) collective-permute-start(bf16[2,2,384,512]{3,2,1,0:T(8,128)(2,1)} %get-tuple-element.78), channel_id=1, source_target_pairs={{0,4},{4,0},{8,12},{12,8},{16,20},{20,16},{24,28},{28,24},{1,5},{5... | collective-permute-start | bytes 4718600 | tf_op jit(solution)/shard_map/ppermute | solution.py:916
  194.6 16.3 %all-to-all-start.1 = ((bf16[8,384,128]{2,1,0:T(8,128)(2,1)}), bf16[8,384,128]{2,1,0:T(8,128)(2,1)S(1)}, u32[]{:S(2)}, u32[]{:S(2)}) async-start(bf16[8,384,128]{2,1,0:T(8,128)(2,1)} %bitcast.134), calls=%async_computation.1 | async-start | bytes 1572864 | tf_op jit(solution)/shard_map/all_to_all | solution.py:1162
  240.7 15.4 %collective-permute-start.23 = (bf16[4096,384]{1,0:T(8,128)(2,1)}, bf16[4096,384]{1,0:T(8,128)(2,1)S(1)}, u32[]{:S(2)}, u32[]{:S(2)}) collective-permute-start(bf16[4096,384]{1,0:T(8,128)(2,1)} %get-tuple-element.49.refs_0_.refs_1_), channel_id=1, source_target_pairs={{0,4},{4,0},{8,12},{12,8},{16,20},{20,16},{24,28},{28,24},{1,5},{5... | collective-permute-start | bytes 9437192 | tf_op jit(solution)/shard_map/ppermute | solution.py:916
  240.8 15.3 %collective-permute-start.25 = (bf16[384,4096]{1,0:T(8,128)(2,1)}, bf16[384,4096]{1,0:T(8,128)(2,1)}, u32[]{:S(2)}, u32[]{:S(2)}) collective-permute-start(bf16[384,4096]{1,0:T(8,128)(2,1)} %get-tuple-element.51.refs_10_), channel_id=1, source_target_pairs={{0,4},{4,0},{8,12},{12,8},{16,20},{20,16},{24,28},{28,24},{1,5},{5... | collective-permute-start | bytes 9437192 | tf_op jit(solution)/shard_map/ppermute | solution.py:916
  241.3 12.6 %collective-permute-start.24 = (bf16[1024,384]{1,0:T(8,128)(2,1)}, bf16[1024,384]{1,0:T(8,128)(2,1)}, u32[]{:S(2)}, u32[]{:S(2)}) collective-permute-start(bf16[1024,384]{1,0:T(8,128)(2,1)} %get-tuple-element.50.refs_6_.refs_7_), channel_id=1, source_target_pairs={{0,4},{4,0},{8,12},{12,8},{16,20},{20,16},{24,28},{28,24},{1,5},{5... | collective-permute-start | bytes 2359304 | tf_op jit(solution)/shard_map/ppermute | solution.py:916
  241.4 13.6 %collective-permute-start.26 = (bf16[1024,384]{1,0:T(8,128)(2,1)}, bf16[1024,384]{1,0:T(8,128)(2,1)}, u32[]{:S(2)}, u32[]{:S(2)}) collective-permute-start(bf16[1024,384]{1,0:T(8,128)(2,1)} %get-tuple-element.52.refs_12_.refs_13_), channel_id=1, source_target_pairs={{0,4},{4,0},{8,12},{12,8},{16,20},{20,16},{24,28},{28,24},{1,5},{5... | collective-permute-start | bytes 2359304 | tf_op jit(solution)/shard_map/ppermute | solution.py:916
  241.8 14.3 %collective-permute-start.27 = (bf16[384,1024]{1,0:T(8,128)(2,1)}, bf16[384,1024]{1,0:T(8,128)(2,1)}, u32[]{:S(2)}, u32[]{:S(2)}) collective-permute-start(bf16[384,1024]{1,0:T(8,128)(2,1)} %get-tuple-element.53.refs_16_), channel_id=1, source_target_pairs={{0,4},{4,0},{8,12},{12,8},{16,20},{20,16},{24,28},{28,24},{1,5},{5... | collective-permute-start | bytes 2359304 | tf_op jit(solution)/shard_map/ppermute | solution.py:916
  242.4 34.7 %all-to-all-start.2 = ((bf16[8,384,128]{2,1,0:T(8,128)(2,1)}), bf16[8,384,128]{2,1,0:T(8,128)(2,1)}, u32[]{:S(2)}, u32[]{:S(2)}) async-start(bf16[8,384,128]{2,1,0:T(8,128)(2,1)} %get-tuple-element.47), calls=%async_computation.2 | async-start | bytes 1572864 | tf_op jit(solution)/shard_map/all_to_all | solution.py:1174
  266.8 69.9 %collective-permute-start.28 = (bf16[2,4,288,512]{3,2,1,0:T(8,128)(2,1)}, bf16[2,4,288,512]{3,2,1,0:T(8,128)(2,1)}, u32[]{:S(2)}, u32[]{:S(2)}) collective-permute-start(bf16[2,4,288,512]{3,2,1,0:T(8,128)(2,1)} %outer.8.rest_0_), channel_id=1, source_target_pairs={{0,8},{4,12},{8,0},{12,4},{16,24},{20,28},{24,16},{28,20},{1,9},{5... | collective-permute-start | bytes 7077896 | tf_op jit(solution)/shard_map/ppermute | solution.py:916
  276.6 60.2 %collective-permute-start.29 = (bf16[2,4,288,512]{3,2,1,0:T(8,128)(2,1)}, bf16[2,4,288,512]{3,2,1,0:T(8,128)(2,1)S(1)}, u32[]{:S(2)}, u32[]{:S(2)}) collective-permute-start(bf16[2,4,288,512]{3,2,1,0:T(8,128)(2,1)} %outer.9.rest_1_), channel_id=1, source_target_pairs={{0,16},{4,20},{8,24},{12,28},{16,0},{20,4},{24,8},{28,12},{1,17},{... | collective-permute-start | bytes 7077896 | tf_op jit(solution)/shard_map/ppermute | solution.py:916
  350.1 70.7 %all-to-all-start.3 = ((bf16[8,3,512,128]{3,2,1,0:T(8,128)(2,1)}), bf16[8,3,512,128]{3,2,1,0:T(8,128)(2,1)S(1)}, u32[]{:S(2)}, u32[]{:S(2)}) async-start(bf16[8,3,512,128]{3,2,1,0:T(8,128)(2,1)} %outgoing.1.refs_19_), calls=%async_computation.3 | async-start | bytes 6291456 | tf_op jit(solution)/shard_map/all_to_all | solution.py:1195
  364.6 51.8 %collective-permute-start.30 = (bf16[4,288,512]{2,1,0:T(8,128)(2,1)}, bf16[4,288,512]{2,1,0:T(8,128)(2,1)}, u32[]{:S(2)}, u32[]{:S(2)}) collective-permute-start(bf16[4,288,512]{2,1,0:T(8,128)(2,1)} %get-tuple-element.58), channel_id=1, source_target_pairs={{0,16},{4,20},{8,24},{12,28},{16,0},{20,4},{24,8},{28,12},{1,17},{... | collective-permute-start | bytes 3538952 | tf_op jit(solution)/shard_map/ppermute | solution.py:916
  376.6 39.9 %collective-permute-start.31 = (bf16[4,288,512]{2,1,0:T(8,128)(2,1)}, bf16[4,288,512]{2,1,0:T(8,128)(2,1)}, u32[]{:S(2)}, u32[]{:S(2)}) collective-permute-start(bf16[4,288,512]{2,1,0:T(8,128)(2,1)} %get-tuple-element.60), channel_id=1, source_target_pairs={{0,8},{4,12},{8,0},{12,4},{16,24},{20,28},{24,16},{28,20},{1,9},{5... | collective-permute-start | bytes 3538952 | tf_op jit(solution)/shard_map/ppermute | solution.py:916
  422.5 68.0 %all-to-all-start.4 = ((bf16[4,2,288,512]{3,2,1,0:T(8,128)(2,1)}), bf16[4,2,288,512]{3,2,1,0:T(8,128)(2,1)}, u32[]{:S(2)}, u32[]{:S(2)}) async-start(bf16[4,2,288,512]{3,2,1,0:T(8,128)(2,1)} %merge.2.rest_0_), calls=%async_computation.4 | async-start | bytes 4718592 | tf_op jit(solution)/shard_map/all_to_all | solution.py:988
  445.5 14.2 %collective-permute-start.34 = (bf16[2,4,64,512]{3,2,1,0:T(8,128)(2,1)}, bf16[2,4,64,512]{3,2,1,0:T(8,128)(2,1)S(1)}, u32[]{:S(2)}, u32[]{:S(2)}) collective-permute-start(bf16[2,4,64,512]{3,2,1,0:T(8,128)(2,1)} %outer.12.rest_0_), channel_id=1, source_target_pairs={{0,8},{4,12},{8,0},{12,4},{16,24},{20,28},{24,16},{28,20},{1,9},{5... | collective-permute-start | bytes 1572872 | tf_op jit(solution)/shard_map/ppermute | solution.py:916
  450.4 13.9 %collective-permute-start.35 = (bf16[2,4,64,512]{3,2,1,0:T(8,128)(2,1)}, bf16[2,4,64,512]{3,2,1,0:T(8,128)(2,1)S(1)}, u32[]{:S(2)}, u32[]{:S(2)}) collective-permute-start(bf16[2,4,64,512]{3,2,1,0:T(8,128)(2,1)} %outer.13.rest_1_), channel_id=1, source_target_pairs={{0,16},{4,20},{8,24},{12,28},{16,0},{20,4},{24,8},{28,12},{1,17},{... | collective-permute-start | bytes 1572872 | tf_op jit(solution)/shard_map/ppermute | solution.py:916
  469.7 13.0 %collective-permute-start.38 = (bf16[4,64,512]{2,1,0:T(8,128)(2,1)S(1)}, bf16[4,64,512]{2,1,0:T(8,128)(2,1)S(1)}, u32[]{:S(2)}, u32[]{:S(2)}) collective-permute-start(bf16[4,64,512]{2,1,0:T(8,128)(2,1)S(1)} %copy-done.15), channel_id=1, source_target_pairs={{0,16},{4,20},{8,24},{12,28},{16,0},{20,4},{24,8},{28,12},{1,17},{... | collective-permute-start | bytes 786440 | tf_op jit(solution)/shard_map/ppermute | solution.py:916
  470.7 12.0 %collective-permute-start.39 = (bf16[4,64,512]{2,1,0:T(8,128)(2,1)}, bf16[4,64,512]{2,1,0:T(8,128)(2,1)S(1)}, u32[]{:S(2)}, u32[]{:S(2)}) collective-permute-start(bf16[4,64,512]{2,1,0:T(8,128)(2,1)} %get-tuple-element.66.refs_2_), channel_id=1, source_target_pairs={{0,8},{4,12},{8,0},{12,4},{16,24},{20,28},{24,16},{28,20},{1,9},{5... | collective-permute-start | bytes 786440 | tf_op jit(solution)/shard_map/ppermute | solution.py:916
  474.0 6.1 %collective-permute-start.37 = (f32[4,4096]{1,0:T(4,128)S(1)}, f32[4,4096]{1,0:T(4,128)S(1)}, u32[]{:S(2)}, u32[]{:S(2)}) collective-permute-start(f32[4,4096]{1,0:T(4,128)S(1)} %add.221), channel_id=1, source_target_pairs={{0,16},{4,20},{8,24},{12,28},{16,0},{20,4},{24,8},{28,12},{1,17},{... | collective-permute-start | bytes 196616 | tf_op jit(solution)/shard_map/ppermute | solution.py:916
  475.8 40.7 %collective-permute-start.43 = (bf16[32,3072]{1,0:T(8,128)(2,1)S(1)}, bf16[32,3072]{1,0:T(8,128)(2,1)S(1)}, u32[]{:S(2)}, u32[]{:S(2)}) collective-permute-start(bf16[32,3072]{1,0:T(8,128)(2,1)S(1)} %get-tuple-element.81), channel_id=1, source_target_pairs={{0,1},{1,2},{2,3},{3,0},{4,5},{5,6},{6,7},{7,4},{8,9},{9,10},{10,1... | collective-permute-start | bytes 589832 | tf_op jit(solution)/shard_map/ppermute | solution.py:921
  477.7 38.8 %collective-permute-start.44 = (bf16[32,3072]{1,0:T(8,128)(2,1)S(1)}, bf16[32,3072]{1,0:T(8,128)(2,1)S(1)}, u32[]{:S(2)}, u32[]{:S(2)}) collective-permute-start(bf16[32,3072]{1,0:T(8,128)(2,1)S(1)} %get-tuple-element.80), channel_id=1, source_target_pairs={{0,2},{1,3},{2,0},{3,1},{4,6},{5,7},{6,4},{7,5},{8,10},{9,11},{10,... | collective-permute-start | bytes 589832 | tf_op jit(solution)/shard_map/ppermute | solution.py:921
  480.1 36.4 %collective-permute-start.45 = (bf16[32,3072]{1,0:T(8,128)(2,1)S(1)}, bf16[32,3072]{1,0:T(8,128)(2,1)}, u32[]{:S(2)}, u32[]{:S(2)}) collective-permute-start(bf16[32,3072]{1,0:T(8,128)(2,1)S(1)} %get-tuple-element.79), channel_id=1, source_target_pairs={{0,3},{1,0},{2,1},{3,2},{4,7},{5,4},{6,5},{7,6},{8,11},{9,8},{10,9... | collective-permute-start | bytes 589832 | tf_op jit(solution)/shard_map/ppermute | solution.py:921
  492.6 9.4 %collective-permute-start.40 = (f32[4,4096]{1,0:T(4,128)}, f32[4,4096]{1,0:T(4,128)S(1)}, u32[]{:S(2)}, u32[]{:S(2)}) collective-permute-start(f32[4,4096]{1,0:T(4,128)} %tie.4), channel_id=1, source_target_pairs={{0,1},{1,2},{2,3},{3,0},{4,5},{5,6},{6,7},{7,4},{8,9},{9,10},{10,1... | collective-permute-start | bytes 196616 | tf_op jit(solution)/shard_map/ppermute | solution.py:921
  492.6 14.6 %collective-permute-start.41 = (f32[4,4096]{1,0:T(4,128)}, f32[4,4096]{1,0:T(4,128)S(1)}, u32[]{:S(2)}, u32[]{:S(2)}) collective-permute-start(f32[4,4096]{1,0:T(4,128)} %tie.4), channel_id=1, source_target_pairs={{0,2},{1,3},{2,0},{3,1},{4,6},{5,7},{6,4},{7,5},{8,10},{9,11},{10,... | collective-permute-start | bytes 196616 | tf_op jit(solution)/shard_map/ppermute | solution.py:921
  492.6 21.3 %all-to-all-start.5 = ((bf16[4,2,64,512]{3,2,1,0:T(8,128)(2,1)}), bf16[4,2,64,512]{3,2,1,0:T(8,128)(2,1)S(1)}, u32[]{:S(2)}, u32[]{:S(2)}) async-start(bf16[4,2,64,512]{3,2,1,0:T(8,128)(2,1)} %merge.3.refs_1_.rest_0_), calls=%async_computation.5 | async-start | bytes 1048576 | tf_op jit(solution)/shard_map/all_to_all | solution.py:988
  502.0 7.2 %collective-permute-start.42 = (f32[4,4096]{1,0:T(4,128)S(1)}, f32[4,4096]{1,0:T(4,128)S(1)}, u32[]{:S(2)}, u32[]{:S(2)}) collective-permute-start(f32[4,4096]{1,0:T(4,128)S(1)} %copy-done.14), channel_id=1, source_target_pairs={{0,3},{1,0},{2,1},{3,2},{4,7},{5,4},{6,5},{7,6},{8,11},{9,8},{10,9... | collective-permute-start | bytes 196616 | tf_op jit(solution)/shard_map/ppermute | solution.py:921
  (50 other events, 325.5 us)
Sparse Core Ops, SparseCore 0:
  22.8 38.7 all-gather.4
  65.0 140.0 all-gather.8
  207.5 46.0 all-gather.6
